TPU v7x, 256 devices: a whole 4x4x8 slice. The times are simulated.
256 devices in a mesh: atoms: 64 (over x, z, core), kern: 4 (over y).
Axes of the slice: x: 4, y: 4, z: 8, core: 2. Of those that a mesh axis runs over, the one named last changes fastest.
Arguments:
- psi: bfloat16 [4096, 4, 128, 256], P('atoms', None, 'kern'), may hold values from -0.03125 to 0.03125
- potential: float32 [64, 128, 256], P('atoms', 'kern'), may hold values from -2 to 1
- kernel: float32 [64, 3, 256, 256], P('atoms', None, 'kern'), may hold values from -0.75 to 0.75
- live_count: int32 [64], replicated, may hold values from 16 to 64, as said below
- rotation: int32 [64], replicated, may hold values from 0 to 63
- bond: int32 [64], replicated, may hold values 0 or 1
Outputs:
- ham: float32 [64, 256, 256], P('atoms', 'kern')
- kernel_new: float32 [64, 3, 256, 256], P('atoms', None, 'kern')
Inputs may be any that keep to these rules, and one draw needn't show every extreme that they name: Region r has live_count[r] live atom slots; some region is full in every draw.
All inputs are finite; a program needn't handle non-finite values.
Results may differ from a plain program's by a relative error of at most 0.0003.
Values may be sent and summed in bfloat16 or wider, within the bound.
No kernel may reach another device: no remote copies, remote signals or barrier semaphores. Data moves between devices by JAX's collectives and lax.ppermute only.
A program may use at most 128 MiB of HBM per device.

v0:
```python
import jax
import jax.numpy as jnp
from jax import lax
from jax.sharding import PartitionSpec as P

ATOMS_REG = 64
SF_ATOM = 4
PX = 16


REACHES = ((1, 4.0 / 3.0), (2, -1.0 / 12.0))
PRECISE = lax.Precision.HIGHEST


def with_halo(block, sides, width, periodic):
    for axis, dim in sides:
        count = lax.axis_size(axis)
        forward = [(i, i + 1) for i in range(count - 1)]
        if periodic:
            forward.append((count - 1, 0))
        backward = [(target, source) for source, target in forward]
        low = lax.ppermute(
            lax.slice_in_dim(block, block.shape[dim] - width, None, axis=dim), axis, forward
        )
        high = lax.ppermute(lax.slice_in_dim(block, 0, width, axis=dim), axis, backward)
        block = jnp.concatenate([low, block, high], axis=dim)
    return block


def live_table(live_count, rotation):
    member = jnp.arange(ATOMS_REG, dtype=jnp.int32)
    shifted = (member[None, :] - rotation[:, None]) % ATOMS_REG
    alive = (shifted < live_count[:, None]).astype(jnp.float32)
    return jnp.repeat(alive, SF_ATOM, axis=1)


def plane_terms(inner_field, row_cells):
    plane_cells = inner_field.shape[-1]
    last_axis = inner_field.ndim - 1
    margin = 2 * row_cells
    padded = jnp.pad(inner_field, [(0, 0)] * last_axis + [(margin, margin)])
    column = jnp.arange(plane_cells, dtype=jnp.int32) % row_cells
    running = jnp.zeros_like(inner_field)
    for reach_cells, weight in REACHES:
        for direction in (1, -1):
            offset = direction * reach_cells
            along_x = lax.slice_in_dim(
                padded, margin + offset, margin + offset + plane_cells, axis=last_axis
            )
            inside = ((column + offset >= 0) & (column + offset < row_cells)).astype(
                inner_field.dtype
            )
            along_y = lax.slice_in_dim(
                padded,
                margin + offset * row_cells,
                margin + offset * row_cells + plane_cells,
                axis=last_axis,
            )
            running = running + weight * (along_x * inside + along_y)
    return running


def depth_terms(extended):
    depth_cells = extended.shape[1] - 4
    running = jnp.zeros_like(lax.slice_in_dim(extended, 2, 2 + depth_cells, axis=1))
    for reach_cells, weight in REACHES:
        upper = lax.slice_in_dim(extended, 2 + reach_cells, 2 + reach_cells + depth_cells, axis=1)
        lower = lax.slice_in_dim(extended, 2 - reach_cells, 2 - reach_cells + depth_cells, axis=1)
        running = running + weight * (upper + lower)
    return running


def local_ham(extended, potential):
    depth_cells = extended.shape[1] - 4
    inner_field = lax.slice_in_dim(extended, 2, 2 + depth_cells, axis=1)
    laplace = plane_terms(inner_field, PX) + depth_terms(extended) - 7.5 * inner_field
    groups = potential.shape[0]
    field_shape = inner_field.shape
    grouped = inner_field.reshape((groups, -1) + field_shape[1:])
    kinetic = (-0.5 * laplace).reshape(grouped.shape)
    applied = kinetic + potential[:, None] * grouped
    return applied.reshape(field_shape).astype(jnp.bfloat16)


def apply_ham(row_boxes, potential):
    extended = with_halo(row_boxes, (("kern", 1),), 2, False)
    return local_ham(extended.astype(jnp.float32), potential)


def contract_cells(left, right):
    return lax.dot_general(
        left, right, (((1,), (1,)), ((), ())), preferred_element_type=jnp.float32
    )


def multiply(left, right):
    return jnp.dot(left, right, precision=PRECISE, preferred_element_type=jnp.float32)


def neighbours(block_rows):
    return with_halo(block_rows, (("atoms", 0),), 1, True)


def full_rows(block_rows):
    return lax.all_gather(block_rows, "kern", axis=2, tiled=True)


def truncated(product_one, rows_three, pattern):
    result = []
    for offset in range(3):
        running = jnp.zeros_like(product_one[0])
        for inner_offset in range(3):
            target = offset - inner_offset + 1
            if 0 <= target <= 2:
                running = running + multiply(
                    product_one[inner_offset], rows_three[inner_offset, target]
                )
        result.append(running * pattern[offset])
    return result


def shards(psi, potential, kernel, live_count, rotation, bond):
    atom_count = lax.axis_size("atoms")
    region = lax.axis_index("atoms")
    kern_pos = lax.axis_index("kern")
    slot_count = psi.shape[0] // atom_count
    depth_cells = psi.shape[2]
    plane_cells = psi.shape[3]
    sf_rows = SF_ATOM * ATOMS_REG
    own_rows = kernel.shape[2]
    live_sf = live_table(live_count, rotation)
    my_live = lax.dynamic_index_in_dim(live_sf, region, 0, keepdims=False)
    row_mask = my_live.astype(jnp.bfloat16)[:, None, None]
    psi_rows = psi.reshape(sf_rows, depth_cells, plane_cells)
    send_boxes = psi_rows.reshape(atom_count, slot_count * SF_ATOM, depth_cells, plane_cells)
    got_boxes = lax.all_to_all(send_boxes, "atoms", split_axis=0, concat_axis=0, tiled=True)
    region_boxes = got_boxes.reshape(sf_rows, depth_cells, plane_cells) * row_mask
    h_boxes = apply_ham(region_boxes, potential)
    flat_boxes = region_boxes.reshape(sf_rows, depth_cells * plane_cells)
    flat_images = h_boxes.reshape(sf_rows, depth_cells * plane_cells)
    row_sums = lax.psum_scatter(
        jnp.concatenate(
            [contract_cells(flat_boxes, flat_boxes), contract_cells(flat_boxes, flat_images)],
            axis=1,
        ),
        "kern",
        scatter_dimension=0,
        tiled=True,
    )
    ham_mine = row_sums[:, sf_rows:]
    intersection_full = lax.all_gather(row_sums[:, :sf_rows], "kern", axis=0, tiled=True)
    lower_bond = lax.dynamic_index_in_dim(bond, (region - 1) % atom_count, 0, keepdims=False)
    upper_bond = lax.dynamic_index_in_dim(bond, region, 0, keepdims=False)
    pattern = jnp.stack([lower_bond, jnp.ones_like(upper_bond), upper_bond]).astype(jnp.float32)
    row_live = lax.dynamic_slice_in_dim(my_live, kern_pos * own_rows, own_rows, 0)
    kernel_eff = jnp.stack(
        [
            kernel[0, offset]
            * row_live[:, None]
            * lax.dynamic_index_in_dim(
                live_sf, (region + offset - 1) % atom_count, 0, keepdims=False
            )[None, :]
            * pattern[offset]
            for offset in range(3)
        ]
    )
    intersection_three = neighbours(intersection_full[None])
    product_one = [multiply(kernel_eff[offset], intersection_three[offset]) for offset in range(3)]
    kernel_three = neighbours(full_rows(kernel_eff[None]))
    second = truncated(product_one, kernel_three, pattern)
    second_three = neighbours(full_rows(jnp.stack(second)[None]))
    triple = truncated(product_one, second_three, pattern)
    kernel_new = 3.0 * jnp.stack(second) - 2.0 * jnp.stack(triple)
    return (ham_mine[None], kernel_new[None])


def solution(mesh):
    in_specs = (
        P("atoms", None, "kern", None),
        P("atoms", "kern", None),
        P("atoms", None, "kern", None),
        P(),
        P(),
        P(),
    )
    out_specs = (P("atoms", "kern", None), P("atoms", None, "kern", None))
    return jax.shard_map(shards, mesh=mesh, in_specs=in_specs, out_specs=out_specs, check_vma=False)
```

profile of v0, /device:TPU:1, one launch (start us, length us, event | category | flops | bytes accessed | tf_op | source)
XLA Modules:
  0.0 282.6 jit_solution(5537244442975552471)
XLA Ops:
  7.2 13.3 %all-to-all-start = ((bf16[64,4,32,256]{3,2,1,0:T(8,128)(2,1)}), bf16[64,4,32,256]{3,2,1,0:T(8,128)(2,1)}, u32[]{:S(2)}, u32[]{:S(2)}) async-start(bf16[64,4,32,256]{3,2,1,0:T(8,128)(2,1)} %param.6), calls=%async_computation | async-start | bytes 8388608 | tf_op jit(solution)/shard_map/all_to_all | solution.py:136
  21.0 95.4 %all-to-all-done = bf16[64,4,32,256]{3,2,1,0:T(8,128)(2,1)} async-done(((bf16[64,4,32,256]{3,2,1,0:T(8,128)(2,1)}), bf16[64,4,32,256]{3,2,1,0:T(8,128)(2,1)}, u32[]{:S(2)}, u32[]{:S(2)}) %all-to-all-start) | async-done | bytes 4194336 | tf_op jit(solution)/shard_map/all_to_all | solution.py:136
  116.4 6.8 %copy_multiply_fusion = bf16[256,32,256]{2,0,1:T(8,128)(2,1)S(1)} fusion(bf16[256,32,256]{2,1,0:T(8,128)(2,1)} %bitcast.3, bf16[256]{0:T(256)(128)(2,1)S(1)} %fusion.59), kind=kLoop, calls=%fused_computation.33 | loop fusion | flops 2097152 | bytes 8389120 | tf_op jit(solution)/shard_map/mul | solution.py:137
  123.2 1.3 collective-permute-start.1
  124.5 4.2 %collective-permute-start = (bf16[256,2,256]{2,0,1:T(8,128)(2,1)S(1)}, bf16[256,2,256]{2,0,1:T(8,128)(2,1)S(1)}, u32[]{:S(2)}, u32[]{:S(2)}) collective-permute-start(bf16[256,2,256]{2,0,1:T(8,128)(2,1)S(1)} %get-tuple-element.13), channel_id=1, source_target_pairs={{0,1},{1,2},{2,3},{4,5},{5,6},{6,7},{8,9},{9,10},{10,11},{12,13},{... | collective-permute-start | bytes 786440 | tf_op jit(solution)/shard_map/ppermute | solution.py:22
  128.7 2.5 broadcast_multiply_fusion
  131.3 6.6 %fusion.32 = f32[256,256]{0,1:T(8,128)S(1)} fusion(bf16[256,32,256]{2,1,0:T(8,128)(2,1)S(1)} %bitcast.124), kind=kOutput, calls=%fused_computation.40 | convolution fusion | flops 1073741824 | bytes 4456448 | tf_op jit(solution)/shard_map/dot_general | solution.py:91
  138.6 4.6 %slice.156 = f32[256,32,256]{2,0,1:T(8,128)} slice(f32[256,36,256]{2,0,1:T(8,128)S(1)} %maximum_convert_fusion), slice={[0:256], [2:34], [0:256]} | slice | bytes 16777216 | tf_op jit(solution)/shard_map/slice | solution.py:75
  143.2 1.5 copy-done
  144.7 42.3 %fusion.123 = bf16[256,32,256]{2,0,1:T(8,128)(2,1)} fusion(f32[256,32,256]{2,0,1:T(8,128)} %slice.156, f32[256,36,256]{2,0,1:T(8,128)} %copy-done, f32[32,256]{1,0:T(8,128)S(1)} %bitcast.148, f32[256]{0:T(256)S(1)} %get-tuple-element.25, f32[256]{0:T(256)S(1)} %get-tuple-element.26, f32[256]{0:T(256)S(1)} %get-tuple-element.27, ...), kind=kLoop, calls=%fused_computation.18.clone.clone.clone.clone.1 | loop fusion | flops 54525952 | bytes 46174208 | tf_op jit(solution)/shard_map/dot_general | solution.py:91
  186.9 7.1 %fusion.27 = f32[256,256]{0,1:T(8,128)S(1)} fusion(bf16[256,32,256]{2,1,0:T(8,128)(2,1)S(1)} %bitcast.125, bf16[256,32,256]{2,0,1:T(8,128)(2,1)} %fusion.123), kind=kOutput, calls=%fused_computation.39 | convolution fusion | flops 1073741824 | bytes 8650752 | tf_op jit(solution)/shard_map/dot_general | solution.py:91
  194.1 1.0 copy.29
  196.3 1.4 add_convert_fusion
  198.3 2.0 fusion.70
  200.3 13.5 %all-gather = f32[3,256,256]{2,1,0:T(8,128)S(1)} all-gather(f32[3,64,256]{2,1,0:T(8,128)S(1)} %pad_maximum_fusion.1), channel_id=2, replica_groups=mesh['atoms'=64,'kern'=4] {'kern'}, dimensions={1}, use_global_device_ids=true | all-gather | bytes 983040 | tf_op jit(solution)/shard_map/all_gather | solution.py:105
  213.8 4.7 %collective-permute-start.5 = (f32[1,3,256,256]{3,2,1,0:T(8,128)S(1)}, f32[1,3,256,256]{3,2,1,0:T(8,128)}, u32[]{:S(2)}, u32[]{:S(2)}) collective-permute-start(f32[1,3,256,256]{3,2,1,0:T(8,128)S(1)} %bitcast.126), channel_id=1, source_target_pairs={{4,0},{8,4},{12,8},{16,12},{20,16},{24,20},{28,24},{32,28},{36,32}... | collective-permute-start | bytes 2359304 | tf_op jit(solution)/shard_map/ppermute | solution.py:25
  219.4 10.0 %all_gather.9 = f32[256,256]{1,0:T(8,128)S(1)} all-gather(f32[64,256]{1,0:T(8,128)S(1)} %get-tuple-element.18), channel_id=1, replica_groups=mesh['atoms'=64,'kern'=4] {'kern'}, dimensions={0}, use_global_device_ids=true | all-gather | bytes 327680 | tf_op jit(solution)/shard_map/all_gather | solution.py:151
  229.4 0.9 fusion.63
  230.6 3.2 %collective-permute-start.4 = (f32[1,256,256]{2,1,0:T(8,128)S(1)}, f32[1,256,256]{2,1,0:T(8,128)S(1)}, u32[]{:S(2)}, u32[]{:S(2)}) collective-permute-start(f32[1,256,256]{2,1,0:T(8,128)S(1)} %bitcast.139), channel_id=1, source_target_pairs={{4,0},{8,4},{12,8},{16,12},{20,16},{24,20},{28,24},{32,28},{36,32}... | collective-permute-start | bytes 786440 | tf_op jit(solution)/shard_map/ppermute | solution.py:25
  234.6 3.2 %collective-permute-done.4 = f32[1,256,256]{2,1,0:T(8,128)S(1)} collective-permute-done((f32[1,256,256]{2,1,0:T(8,128)S(1)}, f32[1,256,256]{2,1,0:T(8,128)S(1)}, u32[]{:S(2)}, u32[]{:S(2)}) %collective-permute-start.4) | collective-permute-done | bytes 262176 | tf_op jit(solution)/shard_map/ppermute | solution.py:25
  237.7 0.9 fusion.54
  238.7 1.2 fusion.51
  239.9 1.0 fusion.56
  240.9 1.8 fusion.42
  242.7 0.9 fusion.45
  244.5 10.9 %all-gather.1 = f32[3,256,256]{2,1,0:T(8,128)S(1)} all-gather(f32[3,64,256]{2,1,0:T(8,128)S(1)} %pad_maximum_fusion.2), channel_id=3, replica_groups=mesh['atoms'=64,'kern'=4] {'kern'}, dimensions={1}, use_global_device_ids=true | all-gather | bytes 983040 | tf_op jit(solution)/shard_map/all_gather | solution.py:105
  255.4 8.1 %collective-permute-start.7 = (f32[1,3,256,256]{3,2,1,0:T(8,128)S(1)}, f32[1,3,256,256]{3,2,1,0:T(8,128)S(1)}, u32[]{:S(2)}, u32[]{:S(2)}) collective-permute-start(f32[1,3,256,256]{3,2,1,0:T(8,128)S(1)} %bitcast.131), channel_id=1, source_target_pairs={{4,0},{8,4},{12,8},{16,12},{20,16},{24,20},{28,24},{32,28},{36,32}... | collective-permute-start | bytes 2359304 | tf_op jit(solution)/shard_map/ppermute | solution.py:25
  265.1 3.6 %collective-permute-done.7 = f32[1,3,256,256]{3,2,1,0:T(8,128)S(1)} collective-permute-done((f32[1,3,256,256]{3,2,1,0:T(8,128)S(1)}, f32[1,3,256,256]{3,2,1,0:T(8,128)S(1)}, u32[]{:S(2)}, u32[]{:S(2)}) %collective-permute-start.7) | collective-permute-done | bytes 786464 | tf_op jit(solution)/shard_map/ppermute | solution.py:25
  268.7 0.9 fusion.36
  269.9 3.4 %collective-permute-done.6 = f32[1,3,256,256]{3,2,1,0:T(8,128)S(1)} collective-permute-done((f32[1,3,256,256]{3,2,1,0:T(8,128)S(1)}, f32[1,3,256,256]{3,2,1,0:T(8,128)S(1)}, u32[]{:S(2)}, u32[]{:S(2)}) %collective-permute-start.6) | collective-permute-done | bytes 786464 | tf_op jit(solution)/shard_map/ppermute | solution.py:22
  273.3 0.9 fusion.41
  274.2 0.9 fusion.39
  (49 shorter events, 8.4 us)
Async XLA Ops:
  7.2 13.4 %copy-start.4 = (s32[64]{0:T(128)S(1)}, s32[64]{0:T(128)}, u32[]{:S(2)}) copy-start(s32[64]{0:T(128)} %param.9) | copy-start | bytes 772
  7.2 13.4 %copy-start.5 = (s32[64]{0:T(128)S(1)}, s32[64]{0:T(128)}, u32[]{:S(2)}) copy-start(s32[64]{0:T(128)} %param.10) | copy-start | bytes 772
  7.2 109.2 %all-to-all-start = ((bf16[64,4,32,256]{3,2,1,0:T(8,128)(2,1)}), bf16[64,4,32,256]{3,2,1,0:T(8,128)(2,1)}, u32[]{:S(2)}, u32[]{:S(2)}) async-start(bf16[64,4,32,256]{3,2,1,0:T(8,128)(2,1)} %param.6), calls=%async_computation | async-start | bytes 8388608 | tf_op jit(solution)/shard_map/all_to_all | solution.py:136
  20.5 198.0 %reduce-scatter.4.cloned.1.call-start = ((), (), s32[]{:S(2)}) async-start(), calls=%async_computation.2 | async-start | bytes 655360
  123.2 14.6 %collective-permute-start.1 = (bf16[256,2,256]{2,0,1:T(8,128)(2,1)S(1)}, bf16[256,2,256]{2,0,1:T(8,128)(2,1)S(1)}, u32[]{:S(2)}, u32[]{:S(2)}) collective-permute-start(bf16[256,2,256]{2,0,1:T(8,128)(2,1)S(1)} %get-tuple-element.14), channel_id=1, source_target_pairs={{1,0},{2,1},{3,2},{5,4},{6,5},{7,6},{9,8},{10,9},{11,10},{13,12},{... | collective-permute-start | bytes 786440 | tf_op jit(solution)/shard_map/ppermute | solution.py:25
  124.5 13.3 %collective-permute-start = (bf16[256,2,256]{2,0,1:T(8,128)(2,1)S(1)}, bf16[256,2,256]{2,0,1:T(8,128)(2,1)S(1)}, u32[]{:S(2)}, u32[]{:S(2)}) collective-permute-start(bf16[256,2,256]{2,0,1:T(8,128)(2,1)S(1)} %get-tuple-element.13), channel_id=1, source_target_pairs={{0,1},{1,2},{2,3},{4,5},{5,6},{6,7},{8,9},{9,10},{10,11},{12,13},{... | collective-permute-start | bytes 786440 | tf_op jit(solution)/shard_map/ppermute | solution.py:22
  138.6 6.1 %copy-start = (f32[256,36,256]{2,0,1:T(8,128)}, f32[256,36,256]{2,0,1:T(8,128)S(1)}, u32[]{:S(2)}) copy-start(f32[256,36,256]{2,0,1:T(8,128)S(1)} %maximum_convert_fusion) | copy-start | bytes 28311556
  138.6 6.1 %copy-start.2 = (f32[1,32,256]{2,1,0:T(8,128)S(1)}, f32[1,32,256]{2,1,0:T(8,128)}, u32[]{:S(2)}) copy-start(f32[1,32,256]{2,1,0:T(8,128)} %param.7) | copy-start | bytes 98308
  186.9 8.2 %copy-start.3 = (s32[64]{0:T(128)S(1)}, s32[64]{0:T(128)}, u32[]{:S(2)}) copy-start(s32[64]{0:T(128)} %param.11) | copy-start | bytes 772
  186.9 11.4 %copy-start.1 = (f32[1,3,64,256]{3,2,1,0:T(8,128)S(1)}, f32[1,3,64,256]{3,2,1,0:T(8,128)}, u32[]{:S(2)}) copy-start(f32[1,3,64,256]{3,2,1,0:T(8,128)} %param.8) | copy-start | bytes 589828
  213.8 24.9 %collective-permute-start.5 = (f32[1,3,256,256]{3,2,1,0:T(8,128)S(1)}, f32[1,3,256,256]{3,2,1,0:T(8,128)}, u32[]{:S(2)}, u32[]{:S(2)}) collective-permute-start(f32[1,3,256,256]{3,2,1,0:T(8,128)S(1)} %bitcast.126), channel_id=1, source_target_pairs={{4,0},{8,4},{12,8},{16,12},{20,16},{24,20},{28,24},{32,28},{36,32}... | collective-permute-start | bytes 2359304 | tf_op jit(solution)/shard_map/ppermute | solution.py:25
  218.5 24.2 %collective-permute-start.3 = (f32[1,3,256,256]{3,2,1,0:T(8,128)S(1)}, f32[1,3,256,256]{3,2,1,0:T(8,128)S(1)}, u32[]{:S(2)}, u32[]{:S(2)}) collective-permute-start(f32[1,3,256,256]{3,2,1,0:T(8,128)S(1)} %bitcast.127), channel_id=1, source_target_pairs={{0,4},{4,8},{8,12},{12,16},{16,20},{20,24},{24,28},{28,32},{32,36}... | collective-permute-start | bytes 2359304 | tf_op jit(solution)/shard_map/ppermute | solution.py:22
  230.6 7.2 %collective-permute-start.4 = (f32[1,256,256]{2,1,0:T(8,128)S(1)}, f32[1,256,256]{2,1,0:T(8,128)S(1)}, u32[]{:S(2)}, u32[]{:S(2)}) collective-permute-start(f32[1,256,256]{2,1,0:T(8,128)S(1)} %bitcast.139), channel_id=1, source_target_pairs={{4,0},{8,4},{12,8},{16,12},{20,16},{24,20},{28,24},{32,28},{36,32}... | collective-permute-start | bytes 786440 | tf_op jit(solution)/shard_map/ppermute | solution.py:25
  234.0 5.9 %collective-permute-start.2 = (f32[1,256,256]{2,1,0:T(8,128)S(1)}, f32[1,256,256]{2,1,0:T(8,128)S(1)}, u32[]{:S(2)}, u32[]{:S(2)}) collective-permute-start(f32[1,256,256]{2,1,0:T(8,128)S(1)} %bitcast.140), channel_id=1, source_target_pairs={{0,4},{4,8},{8,12},{12,16},{16,20},{20,24},{24,28},{28,32},{32,36}... | collective-permute-start | bytes 786440 | tf_op jit(solution)/shard_map/ppermute | solution.py:22
  255.4 13.3 %collective-permute-start.7 = (f32[1,3,256,256]{3,2,1,0:T(8,128)S(1)}, f32[1,3,256,256]{3,2,1,0:T(8,128)S(1)}, u32[]{:S(2)}, u32[]{:S(2)}) collective-permute-start(f32[1,3,256,256]{3,2,1,0:T(8,128)S(1)} %bitcast.131), channel_id=1, source_target_pairs={{4,0},{8,4},{12,8},{16,12},{20,16},{24,20},{28,24},{32,28},{36,32}... | collective-permute-start | bytes 2359304 | tf_op jit(solution)/shard_map/ppermute | solution.py:25
  264.4 8.9 %collective-permute-start.6 = (f32[1,3,256,256]{3,2,1,0:T(8,128)S(1)}, f32[1,3,256,256]{3,2,1,0:T(8,128)S(1)}, u32[]{:S(2)}, u32[]{:S(2)}) collective-permute-start(f32[1,3,256,256]{3,2,1,0:T(8,128)S(1)} %bitcast.132), channel_id=1, source_target_pairs={{0,4},{4,8},{8,12},{12,16},{16,20},{20,24},{24,28},{28,32},{32,36}... | collective-permute-start | bytes 2359304 | tf_op jit(solution)/shard_map/ppermute | solution.py:22
Sparse Core Ops, SparseCore 0:
  195.2 21.4 reduce-scatter.3
where the time goes:
time: 286 us; the launch traced here: 283 us
  waiting for transfers between devices  106 us (37%)
  other arithmetic  56.5 us (20%)
  starting transfers between devices  35.2 us (12%)
  blocking collectives  34.3 us (12%)
  matrix products  25.7 us (9%)
  between operations  14.5 us (5%)
  local copies, waits for them, and re-layouts  10.9 us (4%)
    all_to_all x1, waiting for transfers between devices, shards(): lax.all_to_all(send_boxes, 'atoms', split_axis=0, concat_axis=0, tiled=True)  95.4 us
    dot_general x1, other arithmetic, contract_cells(): lax.dot_general(left, right, (((1,), (1,)), ((), ())), preferred_element_...  42.3 us
    all_gather x2, blocking collectives, full_rows(): return lax.all_gather(block_rows, 'kern', axis=2, tiled=True)  24.4 us
    ppermute x4, starting transfers between devices, with_halo(): lax.ppermute(lax.slice_in_dim(block, 0, width, axis=dim), axis, backward)  17.3 us
    dot_general x2, matrix products, contract_cells(): lax.dot_general(left, right, (((1,), (1,)), ((), ())), preferred_element_...  13.7 us
    all_to_all x1, starting transfers between devices, shards(): lax.all_to_all(send_boxes, 'atoms', split_axis=0, concat_axis=0, tiled=True)  13.3 us
    dot_general x17, matrix products, multiply(): jnp.dot(left, right, precision=PRECISE, preferred_element_type=jnp.float32)  12 us
    all_gather x1, blocking collectives, shards(): lax.all_gather(row_sums[:, :sf_rows], 'kern', axis=0, tiled=True)  9.96 us
  transfers between devices with their start and end apart: 10, of which 4 were waited for; matrix products, arithmetic and copies ran while one was open for 9% of the time, Pallas kernels for 0%

commit v1 on v0

v1 whole, which is shorter than its diff:
```python
import functools

import jax
import jax.numpy as jnp
import numpy as np
from jax import lax
from jax.experimental import pallas as pl
from jax.experimental.pallas import tpu as pltpu
from jax.sharding import PartitionSpec as P

ATOMS_REG = 64
SF_ATOM = 4
PX = 16
SFR = ATOMS_REG * SF_ATOM
GROUP = 16
EDGE = 2

REACHES_12 = ((1, 16), (2, -1))
CENTRE_12 = -90

NT = (((1,), (1,)), ((), ()))
VMEM_LIMIT = 48 * 1024 * 1024


def tile_order():
    order = np.zeros((GROUP * GROUP, GROUP * GROUP), np.float32)
    for row in range(GROUP):
        for plane in range(GROUP):
            order[plane * GROUP + row, row * GROUP + plane] = 1.0
    return order


def plane_weights(cells):
    weights = np.zeros((cells, cells), np.float32)
    for cell in range(cells):
        weights[cell, cell] = CENTRE_12
        for reach, weight in REACHES_12:
            for step in (reach, -reach):
                if 0 <= cell % PX + step < PX:
                    weights[cell + step, cell] += weight
                if 0 <= cell + step * PX < cells:
                    weights[cell + step * PX, cell] += weight
    return weights


def gram_kernel(order_ref, box_ref, planes_ref, inter_ref, low_ref, high_ref):
    rows, depth, cells = box_ref.shape
    order = order_ref[...]
    for group in range(rows // GROUP):
        own = slice(group * GROUP, (group + 1) * GROUP)
        tile = box_ref[own].reshape(GROUP * depth, cells)
        moved = jnp.dot(order, tile, preferred_element_type=jnp.float32).astype(jnp.bfloat16)
        for plane in range(depth):
            planes_ref[own, plane * cells : (plane + 1) * cells] = moved[plane * GROUP : (plane + 1) * GROUP]
    share = lax.dot_general(planes_ref[...], planes_ref[...], NT, preferred_element_type=jnp.float32)
    first = pl.program_id(0) == 0

    @pl.when(first)
    def _():
        inter_ref[...] = share
        low_ref[...] = planes_ref[:, : EDGE * cells]

    @pl.when(jnp.logical_not(first))
    def _():
        inter_ref[...] += share
        high_ref[...] = planes_ref[:, (depth - EDGE) * cells :]


def gram(boxes):
    rows, depth, cells = boxes.shape
    halves = depth // GROUP
    whole = lambda step: (0, 0)
    return pl.pallas_call(
        gram_kernel,
        grid=(halves,),
        in_specs=[
            pl.BlockSpec((GROUP * GROUP, GROUP * GROUP), whole),
            pl.BlockSpec((rows, GROUP, cells), lambda step: (0, step, 0)),
        ],
        out_specs=[
            pl.BlockSpec((rows, GROUP * cells), lambda step: (0, step)),
            pl.BlockSpec((rows, rows), whole),
            pl.BlockSpec((rows, EDGE * cells), whole),
            pl.BlockSpec((rows, EDGE * cells), whole),
        ],
        out_shape=[
            jax.ShapeDtypeStruct((rows, depth * cells), jnp.bfloat16),
            jax.ShapeDtypeStruct((rows, rows), jnp.float32),
            jax.ShapeDtypeStruct((rows, EDGE * cells), jnp.bfloat16),
            jax.ShapeDtypeStruct((rows, EDGE * cells), jnp.bfloat16),
        ],
        compiler_params=pltpu.CompilerParams(vmem_limit_bytes=VMEM_LIMIT),
        cost_estimate=pl.CostEstimate(flops=4 * rows * rows * depth * cells, bytes_accessed=4 * rows * depth * cells, transcendentals=0),
        name="gram",
    )(jnp.asarray(tile_order(), jnp.bfloat16), boxes)


def ham_kernel(weights_ref, planes_ref, below_ref, above_ref, potential_ref, ham_ref, image_ref):
    depth, cells = potential_ref.shape
    weights = weights_ref[...]

    def plane_at(plane):
        if plane < 0:
            return below_ref[:, (plane + EDGE) * cells : (plane + EDGE + 1) * cells]
        if plane >= depth:
            return above_ref[:, (plane - depth) * cells : (plane - depth + 1) * cells]
        return planes_ref[:, plane * cells : (plane + 1) * cells]

    for plane in range(depth):
        field = plane_at(plane)
        lap = jnp.dot(field, weights, preferred_element_type=jnp.float32)
        for reach, weight in REACHES_12:
            both = plane_at(plane + reach).astype(jnp.float32) + plane_at(plane - reach).astype(jnp.float32)
            lap = lap + weight * both
        image = lap * (-1.0 / 24.0) + potential_ref[plane : plane + 1, :] * field.astype(jnp.float32)
        image_ref[:, plane * cells : (plane + 1) * cells] = image.astype(jnp.bfloat16)
    ham_ref[...] = lax.dot_general(planes_ref[...], image_ref[...], NT, preferred_element_type=jnp.float32)


def hamiltonian(planes, below, above, potential):
    rows = planes.shape[0]
    depth, cells = potential.shape
    return pl.pallas_call(
        ham_kernel,
        out_shape=jax.ShapeDtypeStruct((rows, rows), jnp.float32),
        in_specs=[pl.BlockSpec(memory_space=pltpu.VMEM)] * 5,
        out_specs=pl.BlockSpec(memory_space=pltpu.VMEM),
        scratch_shapes=[pltpu.VMEM(planes.shape, jnp.bfloat16)],
        compiler_params=pltpu.CompilerParams(vmem_limit_bytes=VMEM_LIMIT),
        cost_estimate=pl.CostEstimate(flops=4 * rows * rows * depth * cells, bytes_accessed=2 * rows * depth * cells, transcendentals=0),
        name="ham",
    )(jnp.asarray(plane_weights(cells), jnp.bfloat16), planes, below, above, potential)


def halves_of(value):
    high = value.astype(jnp.bfloat16)
    return high, (value - high.astype(jnp.float32)).astype(jnp.bfloat16)


def split_kernel(value_ref, high_ref, low_ref):
    high_ref[...], low_ref[...] = halves_of(value_ref[...])


def split(blocks):
    return pl.pallas_call(
        split_kernel,
        grid=(blocks.shape[0],),
        in_specs=[pl.BlockSpec((1,) + blocks.shape[1:], lambda step: (step, 0, 0))],
        out_specs=[pl.BlockSpec((1,) + blocks.shape[1:], lambda step: (step, 0, 0))] * 2,
        out_shape=[jax.ShapeDtypeStruct(blocks.shape, jnp.bfloat16)] * 2,
        name="split",
    )(blocks)


def times(left, high, low):
    count = left.shape[0]
    left_high, left_low = halves_of(left)
    both = jnp.dot(jnp.concatenate([left_high, left_low], axis=0), high, preferred_element_type=jnp.float32)
    return both[:count] + both[count:] + jnp.dot(left_high, low, preferred_element_type=jnp.float32)


BLOCK_AT = {
    (-1, -1): 0, (-1, 0): 1, (-1, 1): 2,
    (0, -1): 3, (0, 0): 4, (0, 1): 5,
    (1, -1): 6, (1, 0): 7, (1, 1): 8,
    (-2, 1): 9, (2, -1): 10,
}
NEAR = (-1, 0, 1)


def purify_kernel(bond_ref, slab_ref, high_ref, low_ref, s_m2, s_m1, s_0, s_p1, s_p2, row_ref, column_ref, out_ref):
    bonds = {place - 2: bond_ref[place] for place in range(4)}

    def pattern(region, offset):
        return 1.0 if offset == 0 else bonds[region + min(offset, 0)]

    overlap = {place: halves_of(ref[...]) for place, ref in zip(range(-2, 3), (s_m2, s_m1, s_0, s_p1, s_p2))}

    def by_block(left, region, offset):
        place = BLOCK_AT[region, offset]
        return times(left, high_ref[place], low_ref[place])

    rows = slab_ref.shape[1]
    first = {e: times(slab_ref[e + 1] * pattern(0, e), *overlap[e]) for e in NEAR}
    chain = {(e, f): by_block(first[e], e, f) * pattern(e, f) for e in NEAR for f in NEAR}
    longer = {}
    for h in range(-2, 3):
        members = [(e, h - e) for e in NEAR if h - e in NEAR]
        product = times(jnp.concatenate([chain[m] for m in members], axis=0), *overlap[h])
        for place, member in enumerate(members):
            longer[member] = product[place * rows : (place + 1) * rows]
    for d in NEAR:
        second = sum(chain[e, d - e] for e in NEAR if d - e in NEAR)
        triple = jnp.zeros_like(second)
        for h in range(-2, 3):
            if d - h not in NEAR:
                continue
            left = sum(longer[e, h - e] * pattern(e, d - e) for e in NEAR if h - e in NEAR and d - e in NEAR)
            triple = triple + by_block(left * pattern(h, d - h), h, d - h)
        kept = row_ref[...] * column_ref[d + 1 : d + 2, :] * pattern(0, d)
        out_ref[d + 1] = (3.0 * second - 2.0 * triple) * kept


def purify(bonds, slab, high, low, overlaps, row_live, column_live):
    vmem = pl.BlockSpec(memory_space=pltpu.VMEM)
    return pl.pallas_call(
        purify_kernel,
        out_shape=jax.ShapeDtypeStruct(slab.shape, jnp.float32),
        in_specs=[pl.BlockSpec(memory_space=pltpu.SMEM)] + [vmem] * 10,
        out_specs=vmem,
        compiler_params=pltpu.CompilerParams(vmem_limit_bytes=VMEM_LIMIT),
        name="purify",
    )(bonds, slab, high, low, *overlaps, row_live, column_live)


def live_table(live_count, rotation):
    member = jnp.arange(ATOMS_REG, dtype=jnp.int32)
    shifted = (member[None, :] - rotation[:, None]) % ATOMS_REG
    alive = (shifted < live_count[:, None]).astype(jnp.float32)
    return jnp.repeat(alive, SF_ATOM, axis=1)


def moved(block, axis, by):
    count = lax.axis_size(axis)
    return lax.ppermute(block, axis, [(place, (place + by) % count) for place in range(count)])


def shards(psi, potential, kernel, live_count, rotation, bond):
    atom_count = lax.axis_size("atoms")
    kern_count = lax.axis_size("kern")
    region = lax.axis_index("atoms")
    kern_pos = lax.axis_index("kern")
    depth, cells = psi.shape[2:]
    own_rows = kernel.shape[2]

    got = lax.all_to_all(psi, "atoms", split_axis=0, concat_axis=0, tiled=True)

    slab = kernel[0]
    before = moved(slab, "atoms", 1)
    after = moved(slab, "atoms", -1)
    before_two = moved(slab[2:], "atoms", 2)
    after_two = moved(slab[:1], "atoms", -2)
    stack = jnp.concatenate([before, slab, after, before_two, after_two], axis=0)
    others = [moved(stack, "kern", by) for by in range(1, kern_count)]
    blocks = jnp.zeros((stack.shape[0], kern_count) + stack.shape[1:], stack.dtype)
    for by, part in enumerate([stack] + others):
        blocks = lax.dynamic_update_slice_in_dim(blocks, part[:, None], (kern_pos - by) % kern_count, 1)
    high, low = split(blocks.reshape(stack.shape[0], SFR, SFR))

    live_sf = live_table(live_count, rotation)
    near_live = jnp.stack([lax.dynamic_index_in_dim(live_sf, (region + e) % atom_count, 0, keepdims=False) for e in NEAR])
    my_live = near_live[1]
    row_live = lax.dynamic_slice_in_dim(my_live, kern_pos * own_rows, own_rows, 0)
    bonds = jnp.stack([lax.dynamic_index_in_dim(bond, (region + e) % atom_count, 0, keepdims=False) for e in range(-2, 2)]).astype(jnp.float32)

    planes, inter, low_edge, high_edge = gram(got.reshape(SFR, depth, cells))
    inter = inter + sum(moved(inter, "kern", by) for by in range(1, kern_count))
    inter = inter * my_live[:, None] * my_live[None, :]
    overlaps = [moved(inter, "atoms", -e) if e else inter for e in range(-2, 3)]

    up = [(place, place + 1) for place in range(kern_count - 1)]
    below = lax.ppermute(high_edge, "kern", up)
    above = lax.ppermute(low_edge, "kern", [(target, source) for source, target in up])
    ham = hamiltonian(planes, below, above, potential[0])

    def rows_of(place):
        return lax.dynamic_slice_in_dim(ham, (place % kern_count) * own_rows, own_rows, 0)

    ham_mine = rows_of(kern_pos) + sum(moved(rows_of(kern_pos + by), "kern", by) for by in range(1, kern_count))
    ham_mine = ham_mine * row_live[:, None] * my_live[None, :]

    kernel_new = purify(bonds, slab, high, low, overlaps, row_live[:, None], near_live)
    return (ham_mine[None], kernel_new[None])


def solution(mesh):
    in_specs = (
        P("atoms", None, "kern", None),
        P("atoms", "kern", None),
        P("atoms", None, "kern", None),
        P(),
        P(),
        P(),
    )
    out_specs = (P("atoms", "kern", None), P("atoms", None, "kern", None))
    return jax.shard_map(shards, mesh=mesh, in_specs=in_specs, out_specs=out_specs, check_vma=False)
```

time: 286 us -> 193 us (0.67); the launches traced: 283 us -> 193 us
  other arithmetic: 56.5 us -> 3.41 us
  blocking collectives: 34.3 us -> 0 us
  matrix products: 25.7 us -> 0 us
  Pallas kernels: 0 us -> 21.2 us
  between operations: 14.5 us -> 0.99 us
  starting transfers between devices: 35.2 us -> 43.7 us
  local copies, waits for them, and re-layouts: 10.9 us -> 14.6 us
  waiting for transfers between devices: 106 us -> 109 us
    ppermute x8 -> x19, waiting for transfers between devices: 10.2 us -> 109 us  [the longest x17 108 us: moved(): lax.ppermute(block, axis, [(place, (place + by) % count) for place in ran...]
    all_to_all x1, waiting for transfers between devices: 95.4 us -> 0.01 us  [shards(): got = lax.all_to_all(psi, 'atoms', split_axis=0, concat_axis=0, tiled=True)]
    dot_general x1 -> x0, other arithmetic: 42.3 us -> none  [contract_cells(): lax.dot_general(left, right, (((1,), (1,)), ((), ())), preferred_element_...]
    all_gather x3 -> x0, blocking collectives: 34.3 us -> none  [the longest x2 24.4 us: full_rows(): return lax.all_gather(block_rows, 'kern', axis=2, tiled=True)]
    dot_general x19 -> x0, matrix products: 25.7 us -> none  [the longest x2 13.7 us: contract_cells(): lax.dot_general(left, right, (((1,), (1,)), ((), ())), preferred_element_...]
    pallas_call x0 -> x4, Pallas kernels: none -> 21.2 us  [the longest x1 7.42 us: split(): pl.pallas_call(split_kernel, grid=(blocks.shape[0],), in_specs=[pl.BlockS...]
    mul x3 -> x1, other arithmetic: 11.3 us -> 0.11 us  [shards(): inter = inter * my_live[:, None] * my_live[None, :]]
    dynamic_update_slice x0 -> x5, local copies, waits for them, and re-layouts: none -> 8.54 us  [shards(): lax.dynamic_update_slice_in_dim(blocks, part[:, None], (kern_pos - by) %...]
  transfers between devices with their start and end apart: 10 -> 20, of which waited for: 4 -> 7; matrix products, arithmetic and copies ran while one was open for 9% -> 8% of each run, Pallas kernels for 0% -> 10%
where the time goes in v1:
time: 193 us
  waiting for transfers between devices  109 us (56%)
  starting transfers between devices  43.7 us (23%)
  Pallas kernels  21.2 us (11%)
  local copies, waits for them, and re-layouts  14.6 us (8%)
  other arithmetic  3.41 us (2%)
    ppermute x17, waiting for transfers between devices, moved(): lax.ppermute(block, axis, [(place, (place + by) % count) for place in ran...  108 us
    ppermute x17, starting transfers between devices, moved(): lax.ppermute(block, axis, [(place, (place + by) % count) for place in ran...  26.7 us
    all_to_all x1, starting transfers between devices, shards(): got = lax.all_to_all(psi, 'atoms', split_axis=0, concat_axis=0, tiled=True)  13.3 us
    dynamic_update_slice x5, local copies, waits for them, and re-layouts, shards(): lax.dynamic_update_slice_in_dim(blocks, part[:, None], (kern_pos - by) %...  8.54 us
    pallas_call x1, Pallas kernels, split(): pl.pallas_call(split_kernel, grid=(blocks.shape[0],), in_specs=[pl.BlockS...  7.42 us
    pallas_call x1, Pallas kernels, gram(): pl.pallas_call(gram_kernel, grid=(halves,), in_specs=[pl.BlockSpec((GROUP...  6.55 us
    pallas_call x1, Pallas kernels, hamiltonian(): pl.pallas_call(ham_kernel, out_shape=jax.ShapeDtypeStruct((rows, rows), j...  4.6 us
  transfers between devices with their start and end apart: 20, of which 7 were waited for; matrix products, arithmetic and copies ran while one was open for 8% of the time, Pallas kernels for 10%

profile of v1, /device:TPU:1, one launch (start us, length us, event | category | flops | bytes accessed | tf_op | source)
XLA Modules:
  0.0 192.7 jit_solution(14389128562914291775)
XLA Ops:
  0.7 13.3 %all-to-all-start = ((bf16[64,4,32,256]{3,2,1,0:T(8,128)(2,1)}), bf16[64,4,32,256]{3,2,1,0:T(8,128)(2,1)}, u32[]{:S(2)}, u32[]{:S(2)}) async-start(bf16[64,4,32,256]{3,2,1,0:T(8,128)(2,1)} %param.8), calls=%async_computation | async-start | bytes 8388608 | tf_op jit(solution)/shard_map/all_to_all | solution.py:236
  14.0 1.7 collective-permute-start.5
  15.7 1.3 collective-permute-start.7
  17.0 3.6 %collective-permute-start.8 = (f32[1,64,256]{2,1,0:T(8,128)S(1)}, f32[1,64,256]{2,1,0:T(8,128)S(1)}, u32[]{:S(2)}, u32[]{:S(2)}) collective-permute-start(f32[1,64,256]{2,1,0:T(8,128)S(1)} %get-tuple-element.17), channel_id=1, source_target_pairs={{0,248},{4,252},{8,0},{12,4},{16,8},{20,12},{24,16},{28,20},{32,24... | collective-permute-start | bytes 196616 | tf_op jit(solution)/shard_map/ppermute | solution.py:225
  21.6 85.0 %collective-permute-done.5 = f32[3,64,256]{2,1,0:T(8,128)S(1)} collective-permute-done((f32[3,64,256]{2,1,0:T(8,128)S(1)}, f32[3,64,256]{2,1,0:T(8,128)S(1)}, u32[]{:S(2)}, u32[]{:S(2)}) %collective-permute-start.5) | collective-permute-done | bytes 196640 | tf_op jit(solution)/shard_map/ppermute | solution.py:225
  106.6 2.5 %collective-permute-done.6 = f32[3,64,256]{2,1,0:T(8,128)S(1)} collective-permute-done((f32[3,64,256]{2,1,0:T(8,128)S(1)}, f32[3,64,256]{2,1,0:T(8,128)S(1)}, u32[]{:S(2)}, u32[]{:S(2)}) %collective-permute-start.6) | collective-permute-done | bytes 196640 | tf_op jit(solution)/shard_map/ppermute | solution.py:225
  109.1 3.9 %collective-permute-done.7 = f32[1,64,256]{2,1,0:T(8,128)S(1)} collective-permute-done((f32[1,64,256]{2,1,0:T(8,128)S(1)}, f32[1,64,256]{2,1,0:T(8,128)S(1)}, u32[]{:S(2)}, u32[]{:S(2)}) %collective-permute-start.7) | collective-permute-done | bytes 65568 | tf_op jit(solution)/shard_map/ppermute | solution.py:225
  113.0 1.4 collective-permute-start.9
  114.4 2.6 %add_convert_fusion.bond_ref = f32[4]{0:T(128)S(1)} fusion(s32[1]{0:T(128)} %get-tuple-element.26, s32[1]{0:T(128)} %get-tuple-element.27, s32[1]{0:T(128)} %get-tuple-element.25, s32[1]{0:T(128)} %get-tuple-element.24), kind=kLoop, calls=%fused_computation.31 | loop fusion | flops 16 | bytes 32 | tf_op jit(solution)/shard_map/convert_element_type | solution.py:254
  117.5 2.7 %collective-permute-start.10 = (f32[11,64,256]{2,1,0:T(8,128)S(1)}, f32[11,64,256]{2,1,0:T(8,128)}, u32[]{:S(2)}, u32[]{:S(2)}) collective-permute-start(f32[11,64,256]{2,1,0:T(8,128)S(1)} %constant_dynamic-update-slice_fusion), channel_id=1, source_target_pairs={{0,2},{1,3},{2,0},{3,1},{4,6},{5,7},{6,4},{7,5},{8,10},{9,11},{10,... | collective-permute-start | bytes 2162696 | tf_op jit(solution)/shard_map/ppermute | solution.py:225
  120.2 1.1 collective-permute-start.11
  121.3 2.0 %broadcast_in_dim.33 = f32[11,4,64,256]{3,2,0,1:T(8,128)} broadcast(f32[]{:T(128)} %constant.134.clone.1), dimensions={} | broadcast | bytes 2883588 | tf_op jit(solution)/shard_map/broadcast_in_dim | solution.py:245
  123.2 0.9 bitcast_dynamic-update-slice_fusion.3
  124.2 6.5 %gram.1 = (bf16[256,8192]{1,0:T(8,128)(2,1)S(1)}, f32[256,256]{1,0:T(8,128)S(1)}, bf16[256,512]{1,0:T(8,128)(2,1)S(1)}, bf16[256,512]{1,0:T(8,128)(2,1)S(1)}) custom-call(bf16[256,256]{1,0:T(8,128)(2,1)S(1)} %copy-done.5, bf16[256,32,256]{2,1,0:T(8,128)(2,1)} %bitcast.box_ref), custom_call_target="tpu_custom_call" | custom-call | flops 2147483648 | bytes 8388608 | tf_op jit(solution)/shard_map/gram/pallas_call | solution.py:73
  130.7 2.3 %collective-permute-start = (bf16[256,512]{1,0:T(8,128)(2,1)S(1)}, bf16[256,512]{1,0:T(8,128)(2,1)S(1)}, u32[]{:S(2)}, u32[]{:S(2)}) collective-permute-start(bf16[256,512]{1,0:T(8,128)(2,1)S(1)} %get-tuple-element.9), channel_id=1, source_target_pairs={{0,1},{1,2},{2,3},{4,5},{5,6},{6,7},{8,9},{9,10},{10,11},{12,13},{... | collective-permute-start | bytes 786440 | tf_op jit(solution)/shard_map/ppermute | solution.py:262
  133.1 1.3 collective-permute-start.1
  135.3 13.7 %collective-permute-done.10 = f32[11,64,256]{2,1,0:T(8,128)} collective-permute-done((f32[11,64,256]{2,1,0:T(8,128)S(1)}, f32[11,64,256]{2,1,0:T(8,128)}, u32[]{:S(2)}, u32[]{:S(2)}) %collective-permute-start.10) | collective-permute-done | bytes 720928 | tf_op jit(solution)/shard_map/ppermute | solution.py:225
  149.0 2.0 %bitcast_dynamic-update-slice_fusion.1 = f32[11,4,64,256]{3,2,0,1:T(8,128)} fusion(f32[11,4,64,256]{3,2,0,1:T(8,128)} %bitcast_dynamic-update-slice_fusion.2, s32[]{:T(128)S(6)} %select_n.133, f32[11,64,256]{2,1,0:T(8,128)} %collective-permute-done.10), kind=kLoop, calls=%fused_computation.1 | loop fusion | bytes 1441796 | tf_op jit(solution)/shard_map/dynamic_update_slice | solution.py:247
  151.0 3.7 %copy.20 = f32[11,4,64,256]{3,2,1,0:T(8,128)} copy(f32[11,4,64,256]{3,2,0,1:T(8,128)} %bitcast_dynamic-update-slice_fusion.1) | data formatting | bytes 5767168 | tf_op jit(solution)/shard_map/dynamic_update_slice | solution.py:247
  154.8 1.5 collective-permute-start.12
  157.0 4.6 %ham.1 = f32[256,256]{1,0:T(8,128)S(1)} custom-call(bf16[256,256]{1,0:T(8,128)(2,1)S(1)} %copy-done.4, bf16[256,8192]{1,0:T(8,128)(2,1)S(1)} %get-tuple-element.8.planes_ref, bf16[256,512]{1,0:T(8,128)(2,1)S(1)} %collective-permute-done.below_ref, bf16[256,512]{1,0:T(8,128)(2,1)S(1)} %collective-permute-done.1.above_ref, f32[32,256]{1,0:T(8,128)S(1)} %bitcast.29), custom_call_target="tpu_custom_call" | custom-call | flops 2147483648 | bytes 4194304 | tf_op jit(solution)/shard_map/ham/pallas_call | solution.py:123
  161.6 1.8 collective-permute-start.4
  164.4 2.6 %collective-permute-done.13 = f32[256,256]{1,0:T(8,128)S(1)} collective-permute-done((f32[256,256]{1,0:T(8,128)S(1)}, f32[256,256]{1,0:T(8,128)S(1)}, u32[]{:S(2)}, u32[]{:S(2)}) %collective-permute-start.13) | collective-permute-done | bytes 262176 | tf_op jit(solution)/shard_map/ppermute | solution.py:225
  167.2 1.5 collective-permute-start.16
  168.7 2.7 %collective-permute-start.17 = (f32[256,256]{1,0:T(8,128)S(1)}, f32[256,256]{1,0:T(8,128)S(1)}, u32[]{:S(2)}, u32[]{:S(2)}) collective-permute-start(f32[256,256]{1,0:T(8,128)S(1)} %multiply_multiply_fusion.s_0), channel_id=1, source_target_pairs={{0,252},{4,0},{8,4},{12,8},{16,12},{20,16},{24,20},{28,24},{32,28}... | collective-permute-start | bytes 786440 | tf_op jit(solution)/shard_map/ppermute | solution.py:225
  171.4 4.9 %collective-permute-start.18 = (f32[256,256]{1,0:T(8,128)S(1)}, f32[256,256]{1,0:T(8,128)S(1)}, u32[]{:S(2)}, u32[]{:S(2)}) collective-permute-start(f32[256,256]{1,0:T(8,128)S(1)} %multiply_multiply_fusion.s_0), channel_id=1, source_target_pairs={{0,248},{4,252},{8,0},{12,4},{16,8},{20,12},{24,16},{28,20},{32,24... | collective-permute-start | bytes 786440 | tf_op jit(solution)/shard_map/ppermute | solution.py:225
  176.2 1.9 collective-permute-start.3
  178.2 0.9 bitcast_dynamic-update-slice_fusion
  179.1 7.4 %split.1 = (bf16[11,256,256]{2,1,0:T(8,128)(2,1)}, bf16[11,256,256]{2,1,0:T(8,128)(2,1)}) custom-call(f32[11,256,256]{2,1,0:T(8,128)} %bitcast.13.value_ref), custom_call_target="tpu_custom_call" | custom-call | tf_op jit(solution)/shard_map/split/pallas_call | solution.py:145
  187.3 1.4 copy-done
  188.6 1.4 copy-done.1
  190.0 2.7 %purify.1 = f32[3,64,256]{2,1,0:T(8,128)} custom-call(f32[4]{0:T(128)S(1)} %add_convert_fusion.bond_ref, f32[3,64,256]{2,1,0:T(8,128)S(1)} %bitcast.28, bf16[11,256,256]{2,1,0:T(8,128)(2,1)S(1)} %copy-done, bf16[11,256,256]{2,1,0:T(8,128)(2,1)S(1)} %copy-done.1, f32[256,256]{1,0:T(8,128)S(1)} %collective-permute-done.15.s_m2, ...), custom_call_target="tpu_custom_call" | custom-call | tf_op jit(solution)/shard_map/purify/pallas_call | solution.py:206
  (55 shorter events, 5.0 us)
Async XLA Ops:
  0.6 13.4 %copy-start.2 = (f32[1,3,64,256]{3,2,1,0:T(8,128)S(1)}, f32[1,3,64,256]{3,2,1,0:T(8,128)}, u32[]{:S(2)}) copy-start(f32[1,3,64,256]{3,2,1,0:T(8,128)} %param.10) | copy-start | bytes 589828
  0.6 20.0 %copy-start.7 = (s32[64]{0:T(128)S(1)}, s32[64]{0:T(128)}, u32[]{:S(2)}) copy-start(s32[64]{0:T(128)} %param.11) | copy-start | bytes 772
  0.7 20.0 %copy-start.8 = (s32[64]{0:T(128)S(1)}, s32[64]{0:T(128)}, u32[]{:S(2)}) copy-start(s32[64]{0:T(128)} %param.12) | copy-start | bytes 772
  0.7 20.0 %copy-start.6 = (s32[64]{0:T(128)S(1)}, s32[64]{0:T(128)}, u32[]{:S(2)}) copy-start(s32[64]{0:T(128)} %param.13) | copy-start | bytes 772
  0.7 123.5 %all-to-all-start = ((bf16[64,4,32,256]{3,2,1,0:T(8,128)(2,1)}), bf16[64,4,32,256]{3,2,1,0:T(8,128)(2,1)}, u32[]{:S(2)}, u32[]{:S(2)}) async-start(bf16[64,4,32,256]{3,2,1,0:T(8,128)(2,1)} %param.8), calls=%async_computation | async-start | bytes 8388608 | tf_op jit(solution)/shard_map/all_to_all | solution.py:236
  14.0 92.5 %collective-permute-start.5 = (f32[3,64,256]{2,1,0:T(8,128)S(1)}, f32[3,64,256]{2,1,0:T(8,128)S(1)}, u32[]{:S(2)}, u32[]{:S(2)}) collective-permute-start(f32[3,64,256]{2,1,0:T(8,128)S(1)} %bitcast.26), channel_id=1, source_target_pairs={{0,4},{4,8},{8,12},{12,16},{16,20},{20,24},{24,28},{28,32},{32,36}... | collective-permute-start | bytes 589832 | tf_op jit(solution)/shard_map/ppermute | solution.py:225
  15.7 93.4 %collective-permute-start.6 = (f32[3,64,256]{2,1,0:T(8,128)S(1)}, f32[3,64,256]{2,1,0:T(8,128)S(1)}, u32[]{:S(2)}, u32[]{:S(2)}) collective-permute-start(f32[3,64,256]{2,1,0:T(8,128)S(1)} %bitcast.27), channel_id=1, source_target_pairs={{0,252},{4,0},{8,4},{12,8},{16,12},{20,16},{24,20},{28,24},{32,28}... | collective-permute-start | bytes 589832 | tf_op jit(solution)/shard_map/ppermute | solution.py:225
  15.7 97.3 %collective-permute-start.7 = (f32[1,64,256]{2,1,0:T(8,128)S(1)}, f32[1,64,256]{2,1,0:T(8,128)S(1)}, u32[]{:S(2)}, u32[]{:S(2)}) collective-permute-start(f32[1,64,256]{2,1,0:T(8,128)S(1)} %get-tuple-element.18), channel_id=1, source_target_pairs={{0,8},{4,12},{8,16},{12,20},{16,24},{20,28},{24,32},{28,36},{32,40... | collective-permute-start | bytes 196616 | tf_op jit(solution)/shard_map/ppermute | solution.py:225
  17.0 96.0 %collective-permute-start.8 = (f32[1,64,256]{2,1,0:T(8,128)S(1)}, f32[1,64,256]{2,1,0:T(8,128)S(1)}, u32[]{:S(2)}, u32[]{:S(2)}) collective-permute-start(f32[1,64,256]{2,1,0:T(8,128)S(1)} %get-tuple-element.17), channel_id=1, source_target_pairs={{0,248},{4,252},{8,0},{12,4},{16,8},{20,12},{24,16},{28,20},{32,24... | collective-permute-start | bytes 196616 | tf_op jit(solution)/shard_map/ppermute | solution.py:225
  106.6 17.6 %copy-start.5 = (bf16[256,256]{1,0:T(8,128)(2,1)S(1)}, bf16[256,256]{1,0:T(8,128)(2,1)}, u32[]{:S(2)}) copy-start(bf16[256,256]{1,0:T(8,128)(2,1)} %constant.136.clone.order_ref) | copy-start | bytes 393220
  113.0 21.3 %collective-permute-start.9 = (f32[11,64,256]{2,1,0:T(8,128)S(1)}, f32[11,64,256]{2,1,0:T(8,128)S(1)}, u32[]{:S(2)}, u32[]{:S(2)}) collective-permute-start(f32[11,64,256]{2,1,0:T(8,128)S(1)} %constant_dynamic-update-slice_fusion), channel_id=1, source_target_pairs={{0,1},{1,2},{2,3},{3,0},{4,5},{5,6},{6,7},{7,4},{8,9},{9,10},{10,1... | collective-permute-start | bytes 2162696 | tf_op jit(solution)/shard_map/ppermute | solution.py:225
  117.5 31.5 %collective-permute-start.10 = (f32[11,64,256]{2,1,0:T(8,128)S(1)}, f32[11,64,256]{2,1,0:T(8,128)}, u32[]{:S(2)}, u32[]{:S(2)}) collective-permute-start(f32[11,64,256]{2,1,0:T(8,128)S(1)} %constant_dynamic-update-slice_fusion), channel_id=1, source_target_pairs={{0,2},{1,3},{2,0},{3,1},{4,6},{5,7},{6,4},{7,5},{8,10},{9,11},{10,... | collective-permute-start | bytes 2162696 | tf_op jit(solution)/shard_map/ppermute | solution.py:225
  120.2 48.5 %collective-permute-start.11 = (f32[11,64,256]{2,1,0:T(8,128)S(1)}, f32[11,64,256]{2,1,0:T(8,128)S(1)}, u32[]{:S(2)}, u32[]{:S(2)}) collective-permute-start(f32[11,64,256]{2,1,0:T(8,128)S(1)} %constant_dynamic-update-slice_fusion), channel_id=1, source_target_pairs={{0,3},{1,0},{2,1},{3,2},{4,7},{5,4},{6,5},{7,6},{8,11},{9,8},{10,9... | collective-permute-start | bytes 2162696 | tf_op jit(solution)/shard_map/ppermute | solution.py:225
  130.7 25.5 %collective-permute-start = (bf16[256,512]{1,0:T(8,128)(2,1)S(1)}, bf16[256,512]{1,0:T(8,128)(2,1)S(1)}, u32[]{:S(2)}, u32[]{:S(2)}) collective-permute-start(bf16[256,512]{1,0:T(8,128)(2,1)S(1)} %get-tuple-element.9), channel_id=1, source_target_pairs={{0,1},{1,2},{2,3},{4,5},{5,6},{6,7},{8,9},{9,10},{10,11},{12,13},{... | collective-permute-start | bytes 786440 | tf_op jit(solution)/shard_map/ppermute | solution.py:262
  133.1 23.9 %collective-permute-start.1 = (bf16[256,512]{1,0:T(8,128)(2,1)S(1)}, bf16[256,512]{1,0:T(8,128)(2,1)S(1)}, u32[]{:S(2)}, u32[]{:S(2)}) collective-permute-start(bf16[256,512]{1,0:T(8,128)(2,1)S(1)} %get-tuple-element.10), channel_id=1, source_target_pairs={{1,0},{2,1},{3,2},{5,4},{6,5},{7,6},{9,8},{10,9},{11,10},{13,12},{... | collective-permute-start | bytes 786440 | tf_op jit(solution)/shard_map/ppermute | solution.py:263
  151.0 5.9 %copy-start.3 = (f32[1,32,256]{2,1,0:T(8,128)S(1)}, f32[1,32,256]{2,1,0:T(8,128)}, u32[]{:S(2)}) copy-start(f32[1,32,256]{2,1,0:T(8,128)} %param.9) | copy-start | bytes 98308
  151.0 5.9 %copy-start.4 = (bf16[256,256]{1,0:T(8,128)(2,1)S(1)}, bf16[256,256]{1,0:T(8,128)(2,1)}, u32[]{:S(2)}) copy-start(bf16[256,256]{1,0:T(8,128)(2,1)} %constant.137.clone.weights_ref) | copy-start | bytes 393220
  154.8 8.6 %collective-permute-start.14 = (f32[256,256]{1,0:T(8,128)S(1)}, f32[256,256]{1,0:T(8,128)S(1)}, u32[]{:S(2)}, u32[]{:S(2)}) collective-permute-start(f32[256,256]{1,0:T(8,128)S(1)} %get-tuple-element.13), channel_id=1, source_target_pairs={{0,3},{1,0},{2,1},{3,2},{4,7},{5,4},{6,5},{7,6},{8,11},{9,8},{10,9... | collective-permute-start | bytes 786440 | tf_op jit(solution)/shard_map/ppermute | solution.py:225
  154.8 9.6 %collective-permute-start.12 = (f32[256,256]{1,0:T(8,128)S(1)}, f32[256,256]{1,0:T(8,128)S(1)}, u32[]{:S(2)}, u32[]{:S(2)}) collective-permute-start(f32[256,256]{1,0:T(8,128)S(1)} %get-tuple-element.13), channel_id=1, source_target_pairs={{0,1},{1,2},{2,3},{3,0},{4,5},{5,6},{6,7},{7,4},{8,9},{9,10},{10,1... | collective-permute-start | bytes 786440 | tf_op jit(solution)/shard_map/ppermute | solution.py:225
  156.2 10.7 %collective-permute-start.13 = (f32[256,256]{1,0:T(8,128)S(1)}, f32[256,256]{1,0:T(8,128)S(1)}, u32[]{:S(2)}, u32[]{:S(2)}) collective-permute-start(f32[256,256]{1,0:T(8,128)S(1)} %get-tuple-element.13), channel_id=1, source_target_pairs={{0,2},{1,3},{2,0},{3,1},{4,6},{5,7},{6,4},{7,5},{8,10},{9,11},{10,... | collective-permute-start | bytes 786440 | tf_op jit(solution)/shard_map/ppermute | solution.py:225
  161.6 9.8 %collective-permute-start.4 = (f32[64,256]{1,0:T(8,128)S(1)}, f32[64,256]{1,0:T(8,128)S(1)}, u32[]{:S(2)}, u32[]{:S(2)}) collective-permute-start(f32[64,256]{1,0:T(8,128)S(1)} %get-tuple-element.15), channel_id=1, source_target_pairs={{0,3},{1,0},{2,1},{3,2},{4,7},{5,4},{6,5},{7,6},{8,11},{9,8},{10,9... | collective-permute-start | bytes 196616 | tf_op jit(solution)/shard_map/ppermute | solution.py:225
  163.4 12.9 %collective-permute-start.2 = (f32[64,256]{1,0:T(8,128)S(1)}, f32[64,256]{1,0:T(8,128)S(1)}, u32[]{:S(2)}, u32[]{:S(2)}) collective-permute-start(f32[64,256]{1,0:T(8,128)S(1)} %get-tuple-element.16), channel_id=1, source_target_pairs={{0,1},{1,2},{2,3},{3,0},{4,5},{5,6},{6,7},{7,4},{8,9},{9,10},{10,1... | collective-permute-start | bytes 196616 | tf_op jit(solution)/shard_map/ppermute | solution.py:225
  167.1 20.1 %collective-permute-start.15 = (f32[256,256]{1,0:T(8,128)S(1)}, f32[256,256]{1,0:T(8,128)S(1)}, u32[]{:S(2)}, u32[]{:S(2)}) collective-permute-start(f32[256,256]{1,0:T(8,128)S(1)} %multiply_multiply_fusion.s_0), channel_id=1, source_target_pairs={{0,8},{4,12},{8,16},{12,20},{16,24},{20,28},{24,32},{28,36},{32,40... | collective-permute-start | bytes 786440 | tf_op jit(solution)/shard_map/ppermute | solution.py:225
  167.2 20.0 %collective-permute-start.16 = (f32[256,256]{1,0:T(8,128)S(1)}, f32[256,256]{1,0:T(8,128)S(1)}, u32[]{:S(2)}, u32[]{:S(2)}) collective-permute-start(f32[256,256]{1,0:T(8,128)S(1)} %multiply_multiply_fusion.s_0), channel_id=1, source_target_pairs={{0,4},{4,8},{8,12},{12,16},{16,20},{20,24},{24,28},{28,32},{32,36}... | collective-permute-start | bytes 786440 | tf_op jit(solution)/shard_map/ppermute | solution.py:225
  168.7 18.5 %collective-permute-start.17 = (f32[256,256]{1,0:T(8,128)S(1)}, f32[256,256]{1,0:T(8,128)S(1)}, u32[]{:S(2)}, u32[]{:S(2)}) collective-permute-start(f32[256,256]{1,0:T(8,128)S(1)} %multiply_multiply_fusion.s_0), channel_id=1, source_target_pairs={{0,252},{4,0},{8,4},{12,8},{16,12},{20,16},{24,20},{28,24},{32,28}... | collective-permute-start | bytes 786440 | tf_op jit(solution)/shard_map/ppermute | solution.py:225
  171.4 15.9 %collective-permute-start.18 = (f32[256,256]{1,0:T(8,128)S(1)}, f32[256,256]{1,0:T(8,128)S(1)}, u32[]{:S(2)}, u32[]{:S(2)}) collective-permute-start(f32[256,256]{1,0:T(8,128)S(1)} %multiply_multiply_fusion.s_0), channel_id=1, source_target_pairs={{0,248},{4,252},{8,0},{12,4},{16,8},{20,12},{24,16},{28,20},{32,24... | collective-permute-start | bytes 786440 | tf_op jit(solution)/shard_map/ppermute | solution.py:225
  176.2 10.3 %collective-permute-start.3 = (f32[64,256]{1,0:T(8,128)S(1)}, f32[64,256]{1,0:T(8,128)S(1)}, u32[]{:S(2)}, u32[]{:S(2)}) collective-permute-start(f32[64,256]{1,0:T(8,128)S(1)} %get-tuple-element.14), channel_id=1, source_target_pairs={{0,2},{1,3},{2,0},{3,1},{4,6},{5,7},{6,4},{7,5},{8,10},{9,11},{10,... | collective-permute-start | bytes 196616 | tf_op jit(solution)/shard_map/ppermute | solution.py:225
  187.3 1.4 copy-start
  188.6 1.4 copy-start.1

commit v2 on v1

v2 whole, which is shorter than its diff:
```python
import functools

import jax
import jax.numpy as jnp
import numpy as np
from jax import lax
from jax.experimental import pallas as pl
from jax.experimental.pallas import tpu as pltpu
from jax.sharding import PartitionSpec as P

ATOMS_REG = 64
SF_ATOM = 4
PX = 16
SFR = ATOMS_REG * SF_ATOM
GROUP = 16
EDGE = 2

REACHES_12 = ((1, 16), (2, -1))
CENTRE_12 = -90

NT = (((1,), (1,)), ((), ()))
MIB = 1024 * 1024


def plane_weights(cells):
    weights = np.zeros((cells, cells), np.float32)
    for cell in range(cells):
        weights[cell, cell] = CENTRE_12
        for reach, weight in REACHES_12:
            for step in (reach, -reach):
                if 0 <= cell % PX + step < PX:
                    weights[cell + step, cell] += weight
                if 0 <= cell + step * PX < cells:
                    weights[cell + step * PX, cell] += weight
    return weights


def packed(top, corner):
    half = corner.shape[0]
    block = half // 2
    strip = corner[:block]
    return [
        top[:block],
        jnp.concatenate([corner[block:, block:], top[block:, block:]], axis=1),
        jnp.concatenate([strip[: block // 2], strip[block // 2 :]], axis=1),
    ]


def unpacked(value):
    columns = value.shape[1]
    half, block = columns // 2, columns // 4
    first, middle, last = value[:block], value[block : 2 * block], value[2 * block :]
    strip = jnp.concatenate([last[:, :half], last[:, half:]], axis=0)
    second = jnp.concatenate([first[:, block:half].T, middle[:, block:]], axis=1)
    side = jnp.concatenate([first[:, half:], second[:, half:]], axis=0).T
    corner = jnp.concatenate([strip, jnp.concatenate([strip[:, block:].T, middle[:, :block]], axis=1)], axis=0)
    return jnp.concatenate([first, second, jnp.concatenate([side, corner], axis=1)], axis=0)


def by_planes(box_ref, planes_ref, start):
    rows, depth, cells = box_ref.shape
    for group in range(rows // GROUP):
        own = slice(group * GROUP, (group + 1) * GROUP)
        tile = jnp.swapaxes(box_ref[own], 0, 1)
        for plane in range(depth):
            planes_ref[own, start + plane * cells : start + (plane + 1) * cells] = tile[plane]


def gram_kernel(box_ref, inter_ref, planes_ref):
    rows = box_ref.shape[0]
    by_planes(box_ref, planes_ref, 0)
    upper, lower = planes_ref[: rows // 2], planes_ref[rows // 2 :]
    top = lax.dot_general(upper, planes_ref[...], NT, preferred_element_type=jnp.float32)
    corner = lax.dot_general(lower, lower, NT, preferred_element_type=jnp.float32)
    share = jnp.concatenate(packed(top, corner), axis=0)
    first = pl.program_id(0) == 0

    @pl.when(first)
    def _():
        inter_ref[...] = share

    @pl.when(jnp.logical_not(first))
    def _():
        inter_ref[...] += share


def gram(boxes):
    rows, depth, cells = boxes.shape
    kept = rows * 5 // 8
    return pl.pallas_call(
        gram_kernel,
        grid=(depth // GROUP,),
        in_specs=[pl.BlockSpec((rows, GROUP, cells), lambda step: (0, step, 0))],
        out_specs=pl.BlockSpec((kept, rows), lambda step: (0, 0)),
        out_shape=jax.ShapeDtypeStruct((kept, rows), jnp.float32),
        scratch_shapes=[pltpu.VMEM((rows, GROUP * cells), jnp.bfloat16)],
        compiler_params=pltpu.CompilerParams(vmem_limit_bytes=16 * MIB),
        cost_estimate=pl.CostEstimate(flops=2 * rows * rows * depth * cells, bytes_accessed=2 * rows * depth * cells, transcendentals=0),
        name="gram",
    )(boxes)


def image_of(plane_at, plane, weights, potential):
    field = plane_at(plane)
    lap = jnp.dot(field, weights, preferred_element_type=jnp.float32)
    for reach, weight in REACHES_12:
        both = plane_at(plane + reach).astype(jnp.float32) + plane_at(plane - reach).astype(jnp.float32)
        lap = lap + weight * both
    return (lap * (-1.0 / 24.0) + potential * field.astype(jnp.float32)).astype(jnp.bfloat16)


def inner_kernel(place_ref, weights_ref, box_ref, potential_ref, ham_ref, near_ref, far_ref, rims_ref, planes_ref, image_ref):
    depth, cells = potential_ref.shape
    block = box_ref.shape[1]
    steps = depth // block
    edge = EDGE * cells

    for step in range(steps):

        @pl.when(pl.program_id(0) == step)
        def _():
            by_planes(box_ref, planes_ref, step * block * cells)

    @pl.when(pl.program_id(0) == steps - 1)
    def _():
        weights = weights_ref[...]
        plane_at = lambda plane: planes_ref[:, plane * cells : (plane + 1) * cells]
        for plane in range(EDGE, depth - EDGE):
            at = (plane - EDGE) * cells
            image_ref[:, at : at + cells] = image_of(plane_at, plane, weights, potential_ref[plane : plane + 1, :])
        inner = planes_ref[:, edge : depth * cells - edge]
        ham_ref[...] = lax.dot_general(inner, image_ref[...], NT, preferred_element_type=jnp.float32)
        low, high = planes_ref[:, :edge], planes_ref[:, depth * cells - edge :]
        rims_ref[0] = planes_ref[:, : 2 * edge]
        rims_ref[1] = planes_ref[:, depth * cells - 2 * edge :]
        odd = place_ref[1] % 2 == 1

        @pl.when(odd)
        def _():
            near_ref[...], far_ref[...] = low, high

        @pl.when(jnp.logical_not(odd))
        def _():
            near_ref[...], far_ref[...] = high, low


def ham_inner(place, boxes, potential):
    rows, depth, cells = boxes.shape
    whole = lambda step: (0, 0)
    edge = jax.ShapeDtypeStruct((rows, EDGE * cells), jnp.bfloat16)
    return pl.pallas_call(
        inner_kernel,
        grid=(depth // GROUP,),
        out_shape=[
            jax.ShapeDtypeStruct((rows, rows), jnp.float32),
            edge,
            edge,
            jax.ShapeDtypeStruct((2, rows, 2 * EDGE * cells), jnp.bfloat16),
        ],
        in_specs=[
            pl.BlockSpec(memory_space=pltpu.SMEM),
            pl.BlockSpec((cells, cells), whole),
            pl.BlockSpec((rows, GROUP, cells), lambda step: (0, step, 0)),
            pl.BlockSpec((depth, cells), whole),
        ],
        out_specs=[
            pl.BlockSpec((rows, rows), whole),
            pl.BlockSpec(edge.shape, whole),
            pl.BlockSpec(edge.shape, whole),
            pl.BlockSpec((2, rows, 2 * EDGE * cells), lambda step: (0, 0, 0)),
        ],
        scratch_shapes=[pltpu.VMEM((rows, depth * cells), jnp.bfloat16), pltpu.VMEM((rows, (depth - 2 * EDGE) * cells), jnp.bfloat16)],
        compiler_params=pltpu.CompilerParams(vmem_limit_bytes=24 * MIB),
        cost_estimate=pl.CostEstimate(flops=4 * rows * rows * depth * cells, bytes_accessed=2 * rows * depth * cells, transcendentals=0),
        name="ham_inner",
    )(place, jnp.asarray(plane_weights(cells), jnp.bfloat16), boxes, potential)


def outer_kernel(count, place_ref, weights_ref, inner_ref, near_ref, far_ref, rims_ref, potential_ref, *refs):
    slab_refs, ham_ref = refs[:-1], refs[-1]
    depth, cells = potential_ref.shape
    position = place_ref[1]
    odd = position % 2 == 1
    none = jnp.zeros_like(near_ref[...])
    below = jnp.where(position > 0, jnp.where(odd, near_ref[...], far_ref[...]), none)
    above = jnp.where(position < count - 1, jnp.where(odd, far_ref[...], near_ref[...]), none)
    weights = weights_ref[...]
    total = inner_ref[...]
    for side, (halo, start) in enumerate(((below, -EDGE), (above, depth))):
        rim_start = 0 if side == 0 else depth - 2 * EDGE

        def plane_at(plane):
            if 0 <= plane < depth:
                at = (plane - rim_start) * cells
                return rims_ref[side, :, at : at + cells]
            at = (plane - start) * cells
            return halo[:, at : at + cells]

        for plane in range(EDGE) if side == 0 else range(depth - EDGE, depth):
            image = image_of(plane_at, plane, weights, potential_ref[plane : plane + 1, :])
            total = total + lax.dot_general(plane_at(plane), image, NT, preferred_element_type=jnp.float32)
    ham_ref[...] = total
    rows = slab_refs[0].shape[0]
    for by, slab_ref in enumerate(slab_refs):
        at = pl.multiple_of(lax.bitwise_xor(position, by) * rows, rows)
        slab_ref[...] = ham_ref[pl.ds(at, rows), :]


def ham_outer(place, inner, near, far, rims, potential, count):
    rows = inner.shape[0]
    cells = potential.shape[1]
    vmem = pl.BlockSpec(memory_space=pltpu.VMEM)
    return pl.pallas_call(
        functools.partial(outer_kernel, count),
        out_shape=[jax.ShapeDtypeStruct((rows // count, rows), jnp.float32)] * count,
        in_specs=[pl.BlockSpec(memory_space=pltpu.SMEM)] + [vmem] * 6,
        out_specs=[vmem] * count,
        scratch_shapes=[pltpu.VMEM((rows, rows), jnp.float32)],
        compiler_params=pltpu.CompilerParams(vmem_limit_bytes=16 * MIB),
        name="ham_outer",
    )(place, jnp.asarray(plane_weights(cells), jnp.bfloat16), inner, near, far, rims, potential)


def halves_of(value):
    high = value.astype(jnp.bfloat16)
    return high, (value - high.astype(jnp.float32)).astype(jnp.bfloat16)


def assemble_kernel(place_ref, *refs):
    part_refs, out_ref = refs[:-1], refs[-1]
    rows = part_refs[0].shape[1]
    for by, part_ref in enumerate(part_refs):
        at = pl.multiple_of(lax.bitwise_xor(place_ref[1], by) * rows, rows)
        for block in range(part_ref.shape[0]):
            high, low = halves_of(part_ref[block])
            out_ref[2 * block, pl.ds(at, rows), :] = high
            out_ref[2 * block + 1, pl.ds(at, rows), :] = low


def assemble(place, parts):
    blocks, rows, columns = parts[0].shape
    vmem = pl.BlockSpec(memory_space=pltpu.VMEM)
    return pl.pallas_call(
        assemble_kernel,
        out_shape=jax.ShapeDtypeStruct((2 * blocks, rows * len(parts), columns), jnp.bfloat16),
        in_specs=[pl.BlockSpec(memory_space=pltpu.SMEM)] + [vmem] * len(parts),
        out_specs=vmem,
        compiler_params=pltpu.CompilerParams(vmem_limit_bytes=16 * MIB),
        name="assemble",
    )(place, *parts)


def times(left, high, low):
    count = left.shape[0]
    left_high, left_low = halves_of(left)
    both = jnp.dot(jnp.concatenate([left_high, left_low], axis=0), high, preferred_element_type=jnp.float32)
    return both[:count] + both[count:] + jnp.dot(left_high, low, preferred_element_type=jnp.float32)


NEAR = (-1, 0, 1)
REACH = range(-2, 3)


def live_atoms(position, count, rotation):
    shifted = lax.rem(position // SF_ATOM - rotation + ATOMS_REG, ATOMS_REG)
    return (shifted < count).astype(jnp.float32)


def finish_kernel(place_ref, count_ref, rotation_ref, *refs):
    part_refs, out_ref = refs[:-1], refs[-1]
    rows, columns = out_ref.shape
    count, rotation = count_ref[place_ref[0]], rotation_ref[place_ref[0]]
    own_rows = lax.broadcasted_iota(jnp.int32, (rows, 1), 0) + place_ref[1] * rows
    lanes = lax.broadcasted_iota(jnp.int32, (1, columns), 1)
    kept = live_atoms(own_rows, count, rotation) * live_atoms(lanes, count, rotation)
    out_ref[...] = sum(ref[...] for ref in part_refs) * kept


def finish(place, live_count, rotation, parts):
    smem, vmem = pl.BlockSpec(memory_space=pltpu.SMEM), pl.BlockSpec(memory_space=pltpu.VMEM)
    return pl.pallas_call(
        finish_kernel,
        out_shape=jax.ShapeDtypeStruct(parts[0].shape, jnp.float32),
        in_specs=[smem] * 3 + [vmem] * len(parts),
        out_specs=vmem,
        name="finish",
    )(place, live_count, rotation, *parts)


def purify_kernel(place_ref, count_ref, rotation_ref, bond_ref, slab_ref, *refs):
    blocks_ref, out_ref = refs[0], refs[6]
    own, core, cross, even_pair, odd_pair = (ref[...] for ref in refs[1:6])
    odd_region, odd_chip = place_ref[0] % 2 == 1, place_ref[0] // 2 % 2 == 1
    shares = {
        -2: jnp.where(odd_chip, even_pair, odd_pair),
        -1: jnp.where(odd_region, core, cross),
        0: own,
        1: jnp.where(odd_region, cross, core),
        2: jnp.where(odd_chip, odd_pair, even_pair),
    }
    regions = count_ref.shape[0]
    rows, columns = slab_ref.shape[1:]

    def at(e):
        return lax.rem(place_ref[0] + e + regions, regions)

    bonds = {e: bond_ref[at(e)].astype(jnp.float32) for e in range(-2, 2)}
    lanes = lax.broadcasted_iota(jnp.int32, (1, columns), 1)
    live = {e: live_atoms(lanes, count_ref[at(e)], rotation_ref[at(e)]) for e in REACH}
    own_rows = lax.broadcasted_iota(jnp.int32, (rows, 1), 0) + place_ref[1] * rows
    row_live = live_atoms(own_rows, count_ref[at(0)], rotation_ref[at(0)])

    def pattern(region, offset):
        return 1.0 if offset == 0 else bonds[region + min(offset, 0)]

    overlap = {e: halves_of(unpacked(shares[e])) for e in REACH}

    def by_block(left, region, offset):
        block = {-2: 0, 2: 10}.get(region, 5 + 3 * region + offset)
        return times(left, blocks_ref[2 * block], blocks_ref[2 * block + 1])

    first = {e: times(slab_ref[e + 1] * (live[e] * pattern(0, e)), *overlap[e]) * live[e] for e in NEAR}
    chain = {(e, f): by_block(first[e], e, f) * (live[e + f] * pattern(e, f)) for e in NEAR for f in NEAR}
    longer = {}
    for h in REACH:
        members = [(e, h - e) for e in NEAR if h - e in NEAR]
        product = times(jnp.concatenate([chain[m] for m in members], axis=0), *overlap[h]) * live[h]
        for place, member in enumerate(members):
            longer[member] = product[place * rows : (place + 1) * rows]
    for d in NEAR:
        second = sum(chain[e, d - e] for e in NEAR if d - e in NEAR)
        triple = jnp.zeros_like(second)
        for h in REACH:
            if d - h not in NEAR:
                continue
            left = sum(longer[e, h - e] * pattern(e, d - e) for e in NEAR if h - e in NEAR and d - e in NEAR)
            triple = triple + by_block(left * pattern(h, d - h), h, d - h)
        out_ref[d + 1] = (3.0 * second - 2.0 * triple) * (row_live * (live[d] * pattern(0, d)))


def purify(place, live_count, rotation, bond, slab, blocks, overlaps):
    smem, vmem = pl.BlockSpec(memory_space=pltpu.SMEM), pl.BlockSpec(memory_space=pltpu.VMEM)
    return pl.pallas_call(
        purify_kernel,
        out_shape=jax.ShapeDtypeStruct(slab.shape, jnp.float32),
        in_specs=[smem] * 4 + [vmem] * 7,
        out_specs=vmem,
        compiler_params=pltpu.CompilerParams(vmem_limit_bytes=24 * MIB),
        name="purify",
    )(place, live_count, rotation, bond, slab, blocks, *overlaps)


def swapped(block, axis, partner):
    count = lax.axis_size(axis)
    return lax.ppermute(block, axis, [(at, partner(at) % count) for at in range(count)])


def same_chip(at):
    return at ^ 1


def next_region_across(at):
    return at + 1 if at % 2 else at - 1


def even_chip_with_next(at):
    return at - 2 if at // 2 % 2 else at + 2


def odd_chip_with_next(at):
    return at + 2 if at // 2 % 2 else at - 2


def shards(psi, potential, kernel, live_count, rotation, bond):
    kern_count = lax.axis_size("kern")
    depth, cells = psi.shape[2:]
    place = jnp.stack([lax.axis_index("atoms"), lax.axis_index("kern")]).astype(jnp.int32)
    odd_region, odd_chip = place[0] % 2 == 1, place[0] // 2 % 2 == 1
    along_kern = [lambda at, by=by: at ^ by for by in range(kern_count)]

    slab = kernel[0]
    with_even, with_odd = swapped(slab, "atoms", even_chip_with_next), swapped(slab, "atoms", odd_chip_with_next)
    psi, with_even, with_odd = lax.optimization_barrier((psi, with_even, with_odd))

    got = lax.all_to_all(psi, "atoms", split_axis=0, concat_axis=0, tiled=True)

    before_two, after_two = jnp.where(odd_chip, with_even, with_odd), jnp.where(odd_chip, with_odd, with_even)
    other, beyond = swapped(jnp.stack([slab, jnp.where(odd_region, before_two, after_two)]), "atoms", same_chip)
    before, after = jnp.where(odd_region, other, beyond), jnp.where(odd_region, beyond, other)
    stack = jnp.concatenate([before_two[2:], before, slab, after, after_two[:1]], axis=0)
    blocks = assemble(place, [stack] + [swapped(stack, "kern", partner) for partner in along_kern[1:]])
    got, blocks = lax.optimization_barrier((got, blocks))

    boxes = got.reshape(-1, depth, cells)
    share = gram(boxes)
    half_sum = share + swapped(share, "kern", along_kern[1])
    inner, near, far, rims = ham_inner(place, boxes, potential[0])
    half_sum, near, far = lax.optimization_barrier((half_sum, near, far))
    inter = half_sum + swapped(half_sum, "kern", along_kern[3])
    near, far = swapped(near, "kern", along_kern[1]), swapped(far, "kern", along_kern[3])

    partners = (same_chip, next_region_across, even_chip_with_next, odd_chip_with_next)
    overlaps = [inter] + [swapped(inter, "atoms", partner) for partner in partners]
    slabs = ham_outer(place, inner, near, far, rims, potential[0], kern_count)
    parts = [slabs[0]] + [swapped(part, "kern", partner) for part, partner in zip(slabs[1:], along_kern[1:])]
    ham_mine = finish(place, live_count, rotation, parts)

    kernel_new = purify(place, live_count, rotation, bond, slab, blocks, overlaps)
    return (ham_mine[None], kernel_new[None])


def solution(mesh):
    in_specs = (
        P("atoms", None, "kern", None),
        P("atoms", "kern", None),
        P("atoms", None, "kern", None),
        P(),
        P(),
        P(),
    )
    out_specs = (P("atoms", "kern", None), P("atoms", None, "kern", None))
    return jax.shard_map(shards, mesh=mesh, in_specs=in_specs, out_specs=out_specs, check_vma=False)
```

time: 193 us -> 158 us (0.82)
  waiting for transfers between devices: 109 us -> 90.2 us
  starting transfers between devices: 43.7 us -> 38.6 us
  local copies, waits for them, and re-layouts: 14.6 us -> 9.8 us
  Pallas kernels: 21.2 us -> 18 us
  other arithmetic: 3.41 us -> 0.24 us
    ppermute x19 -> x17, waiting for transfers between devices: 109 us -> 40.1 us  [swapped(): lax.ppermute(block, axis, [(at, partner(at) % count) for at in range(coun...]
    all_to_all x1, waiting for transfers between devices: 0.01 us -> 50.1 us  [shards(): got = lax.all_to_all(psi, 'atoms', split_axis=0, concat_axis=0, tiled=True)]
    dynamic_update_slice x5 -> x0, local copies, waits for them, and re-layouts: 8.54 us -> none  [shards(): lax.dynamic_update_slice_in_dim(blocks, part[:, None], (kern_pos - by) %...]
    unnamed x25 -> x40, local copies, waits for them, and re-layouts: 3.04 us -> 9.79 us
    all_to_all x1, starting transfers between devices: 13.3 us -> 8.6 us  [shards(): got = lax.all_to_all(psi, 'atoms', split_axis=0, concat_axis=0, tiled=True)]
    pallas_call x3 -> x5, Pallas kernels: 18.6 us -> 15.2 us  [the longest x1 7.04 us: ham_inner(): pl.pallas_call(inner_kernel, grid=(depth // GROUP,), out_shape=[jax.Shape...]
    convert_element_type x2 -> x0, other arithmetic: 2.58 us -> none  [the longest x1 2.56 us: shards(): jnp.stack([lax.dynamic_index_in_dim(bond, (region + e) % atom_count, 0, k...]
    broadcast_in_dim x3 -> x0, local copies, waits for them, and re-layouts: 2.17 us -> none  [the longest x1 1.96 us: shards(): jnp.zeros((stack.shape[0], kern_count) + stack.shape[1:], stack.dtype)]
  transfers between devices with their start and end apart: 20 -> 18, of which waited for: 7 -> 9; matrix products, arithmetic and copies ran while one was open for 8% -> 0% of each run, Pallas kernels for 10% -> 8%
where the time goes in v2:
time: 158 us
  waiting for transfers between devices  90.2 us (57%)
  starting transfers between devices  38.6 us (24%)
  Pallas kernels  18 us (11%)
  local copies, waits for them, and re-layouts  9.8 us (6%)
    all_to_all x1, waiting for transfers between devices, shards(): got = lax.all_to_all(psi, 'atoms', split_axis=0, concat_axis=0, tiled=True)  50.1 us
    ppermute x17, waiting for transfers between devices, swapped(): lax.ppermute(block, axis, [(at, partner(at) % count) for at in range(coun...  40.1 us
    ppermute x17, starting transfers between devices, swapped(): lax.ppermute(block, axis, [(at, partner(at) % count) for at in range(coun...  30 us
    unnamed x40, local copies, waits for them, and re-layouts  9.79 us
    all_to_all x1, starting transfers between devices, shards(): got = lax.all_to_all(psi, 'atoms', split_axis=0, concat_axis=0, tiled=True)  8.6 us
    pallas_call x1, Pallas kernels, ham_inner(): pl.pallas_call(inner_kernel, grid=(depth // GROUP,), out_shape=[jax.Shape...  7.04 us
    pallas_call x1, Pallas kernels, gram(): pl.pallas_call(gram_kernel, grid=(depth // GROUP,), in_specs=[pl.BlockSpe...  4.26 us
  transfers between devices with their start and end apart: 18, of which 9 were waited for; matrix products, arithmetic and copies ran while one was open for 0% of the time, Pallas kernels for 8%

profile of v2, /device:TPU:1, one launch (start us, length us, event | category | flops | bytes accessed | tf_op | source)
XLA Modules:
  0.0 157.7 jit_solution(17415784015100542531)
XLA Ops:
  0.6 2.6 %collective-permute-start = (f32[3,64,256]{2,1,0:T(8,128)}, f32[3,64,256]{2,1,0:T(8,128)S(1)}, u32[]{:S(2)}, u32[]{:S(2)}) collective-permute-start(f32[3,64,256]{2,1,0:T(8,128)} %bitcast.14), channel_id=1, source_target_pairs={{0,8},{4,12},{8,0},{12,4},{16,24},{20,28},{24,16},{28,20},{32,40},... | collective-permute-start | bytes 589832 | tf_op jit(solution)/shard_map/ppermute | solution.py:355
  3.2 6.9 %collective-permute-start.1 = (f32[3,64,256]{2,1,0:T(8,128)}, f32[3,64,256]{2,1,0:T(8,128)S(1)}, u32[]{:S(2)}, u32[]{:S(2)}) collective-permute-start(f32[3,64,256]{2,1,0:T(8,128)} %bitcast.15), channel_id=1, source_target_pairs={{0,248},{4,252},{8,16},{12,20},{16,8},{20,12},{24,32},{28,36},{32,... | collective-permute-start | bytes 589832 | tf_op jit(solution)/shard_map/ppermute | solution.py:355
  10.1 4.5 %collective-permute-done.1 = f32[3,64,256]{2,1,0:T(8,128)S(1)} collective-permute-done((f32[3,64,256]{2,1,0:T(8,128)}, f32[3,64,256]{2,1,0:T(8,128)S(1)}, u32[]{:S(2)}, u32[]{:S(2)}) %collective-permute-start.1) | collective-permute-done | bytes 196640 | tf_op jit(solution)/shard_map/ppermute | solution.py:355
  14.6 8.6 %all-to-all-start = ((bf16[64,4,32,256]{3,2,1,0:T(8,128)(2,1)}), bf16[64,4,32,256]{3,2,1,0:T(8,128)(2,1)}, u32[]{:S(2)}, u32[]{:S(2)}) async-start(bf16[64,4,32,256]{3,2,1,0:T(8,128)(2,1)} %param.8), calls=%async_computation | async-start | bytes 8388608 | tf_op jit(solution)/shard_map/all_to_all | solution.py:385
  24.0 1.3 collective-permute-done.2
  25.4 1.4 collective-permute-start.3
  26.8 2.6 %collective-permute-start.4 = (f32[11,64,256]{2,1,0:T(8,128)S(1)}, f32[11,64,256]{2,1,0:T(8,128)S(1)}, u32[]{:S(2)}, u32[]{:S(2)}) collective-permute-start(f32[11,64,256]{2,1,0:T(8,128)S(1)} %slice_dynamic-update-slice_fusion.refs_0_), channel_id=1, source_target_pairs={{0,2},{1,3},{2,0},{3,1},{4,6},{5,7},{6,4},{7,5},{8,10},{9,11},{10,... | collective-permute-start | bytes 2162696 | tf_op jit(solution)/shard_map/ppermute | solution.py:355
  29.4 0.9 copy-done.1
  30.4 12.6 %collective-permute-done.3.refs_1_ = f32[11,64,256]{2,1,0:T(8,128)S(1)} collective-permute-done((f32[11,64,256]{2,1,0:T(8,128)S(1)}, f32[11,64,256]{2,1,0:T(8,128)S(1)}, u32[]{:S(2)}, u32[]{:S(2)}) %collective-permute-start.3) | collective-permute-done | bytes 720928 | tf_op jit(solution)/shard_map/ppermute | solution.py:355
  43.0 0.9 copy-done.3
  43.9 17.1 %collective-permute-done.4.refs_2_ = f32[11,64,256]{2,1,0:T(8,128)S(1)} collective-permute-done((f32[11,64,256]{2,1,0:T(8,128)S(1)}, f32[11,64,256]{2,1,0:T(8,128)S(1)}, u32[]{:S(2)}, u32[]{:S(2)}) %collective-permute-start.4) | collective-permute-done | bytes 720928 | tf_op jit(solution)/shard_map/ppermute | solution.py:355
  60.9 0.9 copy-done.5
  61.8 1.0 collective-permute-done.5.refs_3_
  63.6 1.1 copy-done.2
  64.8 1.1 copy-done.4
  65.9 1.1 copy-done.6
  67.0 1.1 copy-done.8
  68.1 0.9 assemble.1.refs_0_
  69.0 50.1 %all-to-all-done = bf16[64,4,32,256]{3,2,1,0:T(8,128)(2,1)} async-done(((bf16[64,4,32,256]{3,2,1,0:T(8,128)(2,1)}), bf16[64,4,32,256]{3,2,1,0:T(8,128)(2,1)}, u32[]{:S(2)}, u32[]{:S(2)}) %all-to-all-start) | async-done | bytes 4194336 | tf_op jit(solution)/shard_map/all_to_all | solution.py:385
  119.1 4.3 %gram.1 = f32[160,256]{1,0:T(8,128)S(1)} custom-call(bf16[256,32,256]{2,1,0:T(8,128)(2,1)} %bitcast.6.box_ref), custom_call_target="tpu_custom_call" | custom-call | flops 1073741824 | bytes 4194304 | tf_op jit(solution)/shard_map/gram/pallas_call | solution.py:90
  123.4 1.4 collective-permute-start.6
  124.8 7.0 %ham_inner.1 = (f32[256,256]{1,0:T(8,128)S(1)}, bf16[256,512]{1,0:T(8,128)(2,1)S(1)}, bf16[256,512]{1,0:T(8,128)(2,1)S(1)}, bf16[2,256,1024]{2,1,0:T(8,128)(2,1)S(1)}) custom-call(s32[2]{0:T(128)S(1)} %pad_add_fusion.place_ref, bf16[256,256]{1,0:T(8,128)(2,1)S(1)} %copy-done.9, bf16[256,32,256]{2,1,0:T(8,128)(2,1)} %bitcast.6.box_ref, f32[32,256]{1,0:T(8,128)S(1)} %bitcast.17), custom_call_target="tpu_custom_call" | custom-call | flops 2147483648 | bytes 4194304 | tf_op jit(solution)/shard_map/ham_inner/pallas_call | solution.py:151
  132.3 2.7 %collective-permute-start.12 = (f32[160,256]{1,0:T(8,128)S(1)}, f32[160,256]{1,0:T(8,128)S(1)}, u32[]{:S(2)}, u32[]{:S(2)}) collective-permute-start(f32[160,256]{1,0:T(8,128)S(1)} %add.16), channel_id=1, source_target_pairs={{0,3},{1,2},{2,1},{3,0},{4,7},{5,6},{6,5},{7,4},{8,11},{9,10},{10,... | collective-permute-start | bytes 491528 | tf_op jit(solution)/shard_map/ppermute | solution.py:355
  135.1 3.4 %collective-permute-done.12 = f32[160,256]{1,0:T(8,128)S(1)} collective-permute-done((f32[160,256]{1,0:T(8,128)S(1)}, f32[160,256]{1,0:T(8,128)S(1)}, u32[]{:S(2)}, u32[]{:S(2)}) %collective-permute-start.12) | collective-permute-done | bytes 163872 | tf_op jit(solution)/shard_map/ppermute | solution.py:355
  138.5 2.6 %collective-permute-start.13 = (f32[160,256]{1,0:T(8,128)S(1)}, f32[160,256]{1,0:T(8,128)S(1)}, u32[]{:S(2)}, u32[]{:S(2)}) collective-permute-start(f32[160,256]{1,0:T(8,128)S(1)} %add.17.refs_1_), channel_id=1, source_target_pairs={{0,4},{4,0},{8,12},{12,8},{16,20},{20,16},{24,28},{28,24},{32,36},... | collective-permute-start | bytes 491528 | tf_op jit(solution)/shard_map/ppermute | solution.py:355
  141.1 1.1 collective-permute-start.15
  142.2 3.6 %collective-permute-start.16 = (f32[160,256]{1,0:T(8,128)S(1)}, f32[160,256]{1,0:T(8,128)S(1)}, u32[]{:S(2)}, u32[]{:S(2)}) collective-permute-start(f32[160,256]{1,0:T(8,128)S(1)} %add.17.refs_1_), channel_id=1, source_target_pairs={{0,248},{4,252},{8,16},{12,20},{16,8},{20,12},{24,32},{28,36},{32,... | collective-permute-start | bytes 491528 | tf_op jit(solution)/shard_map/ppermute | solution.py:355
  145.9 1.4 ham_outer.1
  147.9 2.3 %collective-permute-start.10 = (f32[64,256]{1,0:T(8,128)S(1)}, f32[64,256]{1,0:T(8,128)S(1)}, u32[]{:S(2)}, u32[]{:S(2)}) collective-permute-start(f32[64,256]{1,0:T(8,128)S(1)} %get-tuple-element.30), channel_id=1, source_target_pairs={{0,2},{1,3},{2,0},{3,1},{4,6},{5,7},{6,4},{7,5},{8,10},{9,11},{10,... | collective-permute-start | bytes 196616 | tf_op jit(solution)/shard_map/ppermute | solution.py:355
  150.1 1.1 collective-permute-start.11
  151.9 2.8 %purify.1 = f32[3,64,256]{2,1,0:T(8,128)} custom-call(s32[2]{0:T(128)S(1)} %pad_add_fusion.place_ref, s32[64]{0:T(128)S(1)} %copy-done.13, s32[64]{0:T(128)S(1)} %copy-done.14, s32[64]{0:T(128)S(1)} %copy-done.15, f32[3,64,256]{2,1,0:T(8,128)S(1)} %bitcast.16, bf16[22,256,256]{2,1,0:T(8,128)(2,1)S(1)} %assemble.1.refs_0_, f32[160,256]{1,0:T(8,128)S(1)} %add.17.refs_1_, ...), custom_call_target="tpu_custom_call" | custom-call | tf_op jit(solution)/shard_map/purify/pallas_call | solution.py:343
  156.1 1.6 %finish.1 = f32[64,256]{1,0:T(8,128)} custom-call(s32[2]{0:T(128)} %copy-done.12, s32[64]{0:T(128)} %count_ref.3, s32[64]{0:T(128)} %rotation_ref.3, f32[64,256]{1,0:T(8,128)} %copy-done.10, f32[64,256]{1,0:T(8,128)} %copy-done.18, f32[64,256]{1,0:T(8,128)} %copy-done.16, f32[64,256]{1,0:T(8,128)} %copy-done.17), custom_call_target="tpu_custom_call" | custom-call | tf_op jit(solution)/shard_map/finish/pallas_call | solution.py:281
  (58 shorter events, 4.9 us)
Async XLA Ops:
  0.6 22.7 %copy-start = (f32[1,3,64,256]{3,2,1,0:T(8,128)S(1)}, f32[1,3,64,256]{3,2,1,0:T(8,128)}, u32[]{:S(2)}) copy-start(f32[1,3,64,256]{3,2,1,0:T(8,128)} %param.10) | copy-start | bytes 589828
  0.6 9.4 %collective-permute-start = (f32[3,64,256]{2,1,0:T(8,128)}, f32[3,64,256]{2,1,0:T(8,128)S(1)}, u32[]{:S(2)}, u32[]{:S(2)}) collective-permute-start(f32[3,64,256]{2,1,0:T(8,128)} %bitcast.14), channel_id=1, source_target_pairs={{0,8},{4,12},{8,0},{12,4},{16,24},{20,28},{24,16},{28,20},{32,40},... | collective-permute-start | bytes 589832 | tf_op jit(solution)/shard_map/ppermute | solution.py:355
  3.2 11.4 %collective-permute-start.1 = (f32[3,64,256]{2,1,0:T(8,128)}, f32[3,64,256]{2,1,0:T(8,128)S(1)}, u32[]{:S(2)}, u32[]{:S(2)}) collective-permute-start(f32[3,64,256]{2,1,0:T(8,128)} %bitcast.15), channel_id=1, source_target_pairs={{0,248},{4,252},{8,16},{12,20},{16,8},{20,12},{24,32},{28,36},{32,... | collective-permute-start | bytes 589832 | tf_op jit(solution)/shard_map/ppermute | solution.py:355
  14.6 104.5 %all-to-all-start = ((bf16[64,4,32,256]{3,2,1,0:T(8,128)(2,1)}), bf16[64,4,32,256]{3,2,1,0:T(8,128)(2,1)}, u32[]{:S(2)}, u32[]{:S(2)}) async-start(bf16[64,4,32,256]{3,2,1,0:T(8,128)(2,1)} %param.8), calls=%async_computation | async-start | bytes 8388608 | tf_op jit(solution)/shard_map/all_to_all | solution.py:385
  23.4 2.0 %collective-permute-start.2 = (f32[2,3,64,256]{3,2,1,0:T(8,128)S(1)}, f32[2,3,64,256]{3,2,1,0:T(8,128)S(1)}, u32[]{:S(2)}, u32[]{:S(2)}) collective-permute-start(f32[2,3,64,256]{3,2,1,0:T(8,128)S(1)} %pad_maximum_fusion), channel_id=1, source_target_pairs={{0,4},{4,0},{8,12},{12,8},{16,20},{20,16},{24,28},{28,24},{32,36},... | collective-permute-start | bytes 1179656 | tf_op jit(solution)/shard_map/ppermute | solution.py:355
  25.4 17.5 %collective-permute-start.3 = (f32[11,64,256]{2,1,0:T(8,128)S(1)}, f32[11,64,256]{2,1,0:T(8,128)S(1)}, u32[]{:S(2)}, u32[]{:S(2)}) collective-permute-start(f32[11,64,256]{2,1,0:T(8,128)S(1)} %slice_dynamic-update-slice_fusion.refs_0_), channel_id=1, source_target_pairs={{0,1},{1,0},{2,3},{3,2},{4,5},{5,4},{6,7},{7,6},{8,9},{9,8},{10,11... | collective-permute-start | bytes 2162696 | tf_op jit(solution)/shard_map/ppermute | solution.py:355
  26.8 34.1 %collective-permute-start.4 = (f32[11,64,256]{2,1,0:T(8,128)S(1)}, f32[11,64,256]{2,1,0:T(8,128)S(1)}, u32[]{:S(2)}, u32[]{:S(2)}) collective-permute-start(f32[11,64,256]{2,1,0:T(8,128)S(1)} %slice_dynamic-update-slice_fusion.refs_0_), channel_id=1, source_target_pairs={{0,2},{1,3},{2,0},{3,1},{4,6},{5,7},{6,4},{7,5},{8,10},{9,11},{10,... | collective-permute-start | bytes 2162696 | tf_op jit(solution)/shard_map/ppermute | solution.py:355
  29.4 33.4 %collective-permute-start.5 = (f32[11,64,256]{2,1,0:T(8,128)S(1)}, f32[11,64,256]{2,1,0:T(8,128)S(1)}, u32[]{:S(2)}, u32[]{:S(2)}) collective-permute-start(f32[11,64,256]{2,1,0:T(8,128)S(1)} %slice_dynamic-update-slice_fusion.refs_0_), channel_id=1, source_target_pairs={{0,3},{1,2},{2,1},{3,0},{4,7},{5,6},{6,5},{7,4},{8,11},{9,10},{10,... | collective-permute-start | bytes 2162696 | tf_op jit(solution)/shard_map/ppermute | solution.py:355
  29.4 0.9 copy-start.1
  43.0 0.9 copy-start.3
  60.9 0.9 copy-start.5
  62.8 0.9 copy-start.7
  63.6 1.1 copy-start.2
  64.8 1.1 copy-start.4
  65.9 1.1 copy-start.6
  67.0 1.1 copy-start.8
  68.1 56.7 %copy-start.9 = (bf16[256,256]{1,0:T(8,128)(2,1)S(1)}, bf16[256,256]{1,0:T(8,128)(2,1)}, u32[]{:S(2)}) copy-start(bf16[256,256]{1,0:T(8,128)(2,1)} %constant.40.clone.weights_ref) | copy-start | bytes 393220
  68.1 56.7 %copy-start.11 = (f32[1,32,256]{2,1,0:T(8,128)S(1)}, f32[1,32,256]{2,1,0:T(8,128)}, u32[]{:S(2)}) copy-start(f32[1,32,256]{2,1,0:T(8,128)} %param.9) | copy-start | bytes 98308
  123.4 8.5 %collective-permute-start.6 = (f32[160,256]{1,0:T(8,128)S(1)}, f32[160,256]{1,0:T(8,128)S(1)}, u32[]{:S(2)}, u32[]{:S(2)}) collective-permute-start(f32[160,256]{1,0:T(8,128)S(1)} %gram.1), channel_id=1, source_target_pairs={{0,1},{1,0},{2,3},{3,2},{4,5},{5,4},{6,7},{7,6},{8,9},{9,8},{10,11... | collective-permute-start | bytes 491528 | tf_op jit(solution)/shard_map/ppermute | solution.py:355
  124.8 27.1 %copy-start.13 = (s32[64]{0:T(128)S(1)}, s32[64]{0:T(128)}, u32[]{:S(2)}) copy-start(s32[64]{0:T(128)} %count_ref.3) | copy-start | bytes 772
  124.8 27.1 %copy-start.14 = (s32[64]{0:T(128)S(1)}, s32[64]{0:T(128)}, u32[]{:S(2)}) copy-start(s32[64]{0:T(128)} %rotation_ref.3) | copy-start | bytes 772
  124.8 27.1 %copy-start.15 = (s32[64]{0:T(128)S(1)}, s32[64]{0:T(128)}, u32[]{:S(2)}) copy-start(s32[64]{0:T(128)} %bond_ref.1) | copy-start | bytes 772
  131.9 10.4 %collective-permute-start.7 = (bf16[256,512]{1,0:T(8,128)(2,1)S(1)}, bf16[256,512]{1,0:T(8,128)(2,1)S(1)}, u32[]{:S(2)}, u32[]{:S(2)}) collective-permute-start(bf16[256,512]{1,0:T(8,128)(2,1)S(1)} %get-tuple-element.25), channel_id=1, source_target_pairs={{0,1},{1,0},{2,3},{3,2},{4,5},{5,4},{6,7},{7,6},{8,9},{9,8},{10,11... | collective-permute-start | bytes 786440 | tf_op jit(solution)/shard_map/ppermute | solution.py:355
  132.3 6.2 %collective-permute-start.12 = (f32[160,256]{1,0:T(8,128)S(1)}, f32[160,256]{1,0:T(8,128)S(1)}, u32[]{:S(2)}, u32[]{:S(2)}) collective-permute-start(f32[160,256]{1,0:T(8,128)S(1)} %add.16), channel_id=1, source_target_pairs={{0,3},{1,2},{2,1},{3,0},{4,7},{5,6},{6,5},{7,4},{8,11},{9,10},{10,... | collective-permute-start | bytes 491528 | tf_op jit(solution)/shard_map/ppermute | solution.py:355
  135.0 10.8 %collective-permute-start.8 = (bf16[256,512]{1,0:T(8,128)(2,1)S(1)}, bf16[256,512]{1,0:T(8,128)(2,1)S(1)}, u32[]{:S(2)}, u32[]{:S(2)}) collective-permute-start(bf16[256,512]{1,0:T(8,128)(2,1)S(1)} %get-tuple-element.26), channel_id=1, source_target_pairs={{0,3},{1,2},{2,1},{3,0},{4,7},{5,6},{6,5},{7,4},{8,11},{9,10},{10,... | collective-permute-start | bytes 786440 | tf_op jit(solution)/shard_map/ppermute | solution.py:355
  138.5 11.7 %collective-permute-start.13 = (f32[160,256]{1,0:T(8,128)S(1)}, f32[160,256]{1,0:T(8,128)S(1)}, u32[]{:S(2)}, u32[]{:S(2)}) collective-permute-start(f32[160,256]{1,0:T(8,128)S(1)} %add.17.refs_1_), channel_id=1, source_target_pairs={{0,4},{4,0},{8,12},{12,8},{16,20},{20,16},{24,28},{28,24},{32,36},... | collective-permute-start | bytes 491528 | tf_op jit(solution)/shard_map/ppermute | solution.py:355
  141.1 10.1 %collective-permute-start.14 = (f32[160,256]{1,0:T(8,128)S(1)}, f32[160,256]{1,0:T(8,128)S(1)}, u32[]{:S(2)}, u32[]{:S(2)}) collective-permute-start(f32[160,256]{1,0:T(8,128)S(1)} %add.17.refs_1_), channel_id=1, source_target_pairs={{0,252},{4,8},{8,4},{12,16},{16,12},{20,24},{24,20},{28,32},{32,28... | collective-permute-start | bytes 491528 | tf_op jit(solution)/shard_map/ppermute | solution.py:355
  141.1 10.8 %collective-permute-start.15 = (f32[160,256]{1,0:T(8,128)S(1)}, f32[160,256]{1,0:T(8,128)S(1)}, u32[]{:S(2)}, u32[]{:S(2)}) collective-permute-start(f32[160,256]{1,0:T(8,128)S(1)} %add.17.refs_1_), channel_id=1, source_target_pairs={{0,8},{4,12},{8,0},{12,4},{16,24},{20,28},{24,16},{28,20},{32,40},... | collective-permute-start | bytes 491528 | tf_op jit(solution)/shard_map/ppermute | solution.py:355
  142.2 9.6 %collective-permute-start.16 = (f32[160,256]{1,0:T(8,128)S(1)}, f32[160,256]{1,0:T(8,128)S(1)}, u32[]{:S(2)}, u32[]{:S(2)}) collective-permute-start(f32[160,256]{1,0:T(8,128)S(1)} %add.17.refs_1_), channel_id=1, source_target_pairs={{0,248},{4,252},{8,16},{12,20},{16,8},{20,12},{24,32},{28,36},{32,... | collective-permute-start | bytes 491528 | tf_op jit(solution)/shard_map/ppermute | solution.py:355
  147.9 7.4 %collective-permute-start.10 = (f32[64,256]{1,0:T(8,128)S(1)}, f32[64,256]{1,0:T(8,128)S(1)}, u32[]{:S(2)}, u32[]{:S(2)}) collective-permute-start(f32[64,256]{1,0:T(8,128)S(1)} %get-tuple-element.30), channel_id=1, source_target_pairs={{0,2},{1,3},{2,0},{3,1},{4,6},{5,7},{6,4},{7,5},{8,10},{9,11},{10,... | collective-permute-start | bytes 196616 | tf_op jit(solution)/shard_map/ppermute | solution.py:355
  150.1 5.3 %collective-permute-start.11 = (f32[64,256]{1,0:T(8,128)S(1)}, f32[64,256]{1,0:T(8,128)S(1)}, u32[]{:S(2)}, u32[]{:S(2)}) collective-permute-start(f32[64,256]{1,0:T(8,128)S(1)} %get-tuple-element.31), channel_id=1, source_target_pairs={{0,3},{1,2},{2,1},{3,0},{4,7},{5,6},{6,5},{7,4},{8,11},{9,10},{10,... | collective-permute-start | bytes 196616 | tf_op jit(solution)/shard_map/ppermute | solution.py:355
  151.2 4.3 %collective-permute-start.9 = (f32[64,256]{1,0:T(8,128)S(1)}, f32[64,256]{1,0:T(8,128)S(1)}, u32[]{:S(2)}, u32[]{:S(2)}) collective-permute-start(f32[64,256]{1,0:T(8,128)S(1)} %get-tuple-element.29), channel_id=1, source_target_pairs={{0,1},{1,0},{2,3},{3,2},{4,5},{5,4},{6,7},{7,6},{8,9},{9,8},{10,11... | collective-permute-start | bytes 196616 | tf_op jit(solution)/shard_map/ppermute | solution.py:355
  (5 other events, 3.1 us)

commit v3 on v2

--- a/solution.py
+++ b/solution.py
@@ -20,6 +20,7 @@
 
 NT = (((1,), (1,)), ((), ()))
 MIB = 1024 * 1024
+ANY = pl.BlockSpec(memory_space=pl.ANY)
 
 
 def plane_weights(cells):
@@ -66,7 +67,8 @@
             planes_ref[own, start + plane * cells : start + (plane + 1) * cells] = tile[plane]
 
 
-def gram_kernel(box_ref, inter_ref, planes_ref):
+def gram_kernel(box_ref, *refs):
+    inter_ref, planes_ref = refs[-2:]
     rows = box_ref.shape[0]
     by_planes(box_ref, planes_ref, 0)
     upper, lower = planes_ref[: rows // 2], planes_ref[rows // 2 :]
@@ -84,20 +86,20 @@
         inter_ref[...] += share
 
 
-def gram(boxes):
+def gram(boxes, ahead):
     rows, depth, cells = boxes.shape
     kept = rows * 5 // 8
     return pl.pallas_call(
         gram_kernel,
         grid=(depth // GROUP,),
-        in_specs=[pl.BlockSpec((rows, GROUP, cells), lambda step: (0, step, 0))],
+        in_specs=[pl.BlockSpec((rows, GROUP, cells), lambda step: (0, step, 0))] + [ANY] * len(ahead),
         out_specs=pl.BlockSpec((kept, rows), lambda step: (0, 0)),
         out_shape=jax.ShapeDtypeStruct((kept, rows), jnp.float32),
         scratch_shapes=[pltpu.VMEM((rows, GROUP * cells), jnp.bfloat16)],
         compiler_params=pltpu.CompilerParams(vmem_limit_bytes=16 * MIB),
         cost_estimate=pl.CostEstimate(flops=2 * rows * rows * depth * cells, bytes_accessed=2 * rows * depth * cells, transcendentals=0),
         name="gram",
-    )(boxes)
+    )(boxes, *ahead)
 
 
 def image_of(plane_at, plane, weights, potential):
@@ -216,9 +218,60 @@
         in_specs=[pl.BlockSpec(memory_space=pltpu.SMEM)] + [vmem] * 6,
         out_specs=[vmem] * count,
         scratch_shapes=[pltpu.VMEM((rows, rows), jnp.float32)],
-        compiler_params=pltpu.CompilerParams(vmem_limit_bytes=16 * MIB),
+        compiler_params=pltpu.CompilerParams(vmem_limit_bytes=10 * MIB),
         name="ham_outer",
     )(place, jnp.asarray(plane_weights(cells), jnp.bfloat16), inner, near, far, rims, potential)
+
+
+def outward_kernel(place_ref, blocks_ref, *refs):
+    odd = place_ref[0] % 2 == 1
+    count = refs[-1].shape[0]
+    refs[-1][...] = jnp.where(odd, blocks_ref[:count], blocks_ref[-count:])
+
+
+def outward(place, blocks, ahead):
+    vmem = pl.BlockSpec(memory_space=pltpu.VMEM)
+    return pl.pallas_call(
+        outward_kernel,
+        out_shape=jax.ShapeDtypeStruct((2,) + blocks.shape[1:], blocks.dtype),
+        in_specs=[pl.BlockSpec(memory_space=pltpu.SMEM), vmem] + [ANY] * len(ahead),
+        out_specs=vmem,
+        compiler_params=pltpu.CompilerParams(vmem_limit_bytes=4 * MIB),
+        name="outward",
+    )(place, blocks, *ahead)
+
+
+def pick_kernel(place_ref, even_ref, odd_ref, *refs):
+    even = place_ref[0] % 2 == place_ref[0] // 2 % 2
+    refs[-1][...] = jnp.where(even, even_ref[...], odd_ref[...])
+
+
+def pick(place, even, odd, ahead):
+    vmem = pl.BlockSpec(memory_space=pltpu.VMEM)
+    return pl.pallas_call(
+        pick_kernel,
+        out_shape=jax.ShapeDtypeStruct(even.shape, even.dtype),
+        in_specs=[pl.BlockSpec(memory_space=pltpu.SMEM), vmem, vmem] + [ANY] * len(ahead),
+        out_specs=vmem,
+        compiler_params=pltpu.CompilerParams(vmem_limit_bytes=4 * MIB),
+        name="pick",
+    )(place, even, odd, *ahead)
+
+
+def total_kernel(count, *refs):
+    refs[-1][...] = sum(ref[...] for ref in refs[:count])
+
+
+def total(parts, ahead):
+    vmem = pl.BlockSpec(memory_space=pltpu.VMEM)
+    return pl.pallas_call(
+        functools.partial(total_kernel, len(parts)),
+        out_shape=jax.ShapeDtypeStruct(parts[0].shape, parts[0].dtype),
+        in_specs=[vmem] * len(parts) + [ANY] * len(ahead),
+        out_specs=vmem,
+        compiler_params=pltpu.CompilerParams(vmem_limit_bytes=4 * MIB),
+        name="total",
+    )(*parts, *ahead)
 
 
 def halves_of(value):
@@ -283,13 +336,14 @@
         out_shape=jax.ShapeDtypeStruct(parts[0].shape, jnp.float32),
         in_specs=[smem] * 3 + [vmem] * len(parts),
         out_specs=vmem,
+        compiler_params=pltpu.CompilerParams(vmem_limit_bytes=4 * MIB),
         name="finish",
     )(place, live_count, rotation, *parts)
 
 
 def purify_kernel(place_ref, count_ref, rotation_ref, bond_ref, slab_ref, *refs):
-    blocks_ref, out_ref = refs[0], refs[6]
-    own, core, cross, even_pair, odd_pair = (ref[...] for ref in refs[1:6])
+    block_refs, out_ref = refs[5:10], refs[10]
+    own, core, cross, even_pair, odd_pair = (ref[...] for ref in refs[:5])
     odd_region, odd_chip = place_ref[0] % 2 == 1, place_ref[0] // 2 % 2 == 1
     shares = {
         -2: jnp.where(odd_chip, even_pair, odd_pair),
@@ -316,8 +370,16 @@
     overlap = {e: halves_of(unpacked(shares[e])) for e in REACH}
 
     def by_block(left, region, offset):
-        block = {-2: 0, 2: 10}.get(region, 5 + 3 * region + offset)
-        return times(left, blocks_ref[2 * block], blocks_ref[2 * block + 1])
+        part = lambda ref, block: (ref[2 * block], ref[2 * block + 1])
+        choose = lambda odd, yes, no: [jnp.where(odd, a, b) for a, b in zip(yes, no)]
+        own_ref, core_ref, cross_ref, beyond_ref, behind_ref = block_refs
+        if region == 0:
+            return times(left, *part(own_ref, offset + 1))
+        if abs(region) == 1:
+            core_part, cross_part = part(core_ref, offset + 1), part(cross_ref, offset + 1)
+            return times(left, *(choose(odd_region, core_part, cross_part) if region < 0 else choose(odd_region, cross_part, core_part)))
+        beyond_part, behind_part = part(beyond_ref, 0), part(behind_ref, 0)
+        return times(left, *(choose(odd_region, behind_part, beyond_part) if region < 0 else choose(odd_region, beyond_part, behind_part)))
 
     first = {e: times(slab_ref[e + 1] * (live[e] * pattern(0, e)), *overlap[e]) * live[e] for e in NEAR}
     chain = {(e, f): by_block(first[e], e, f) * (live[e + f] * pattern(e, f)) for e in NEAR for f in NEAR}
@@ -338,16 +400,16 @@
         out_ref[d + 1] = (3.0 * second - 2.0 * triple) * (row_live * (live[d] * pattern(0, d)))
 
 
-def purify(place, live_count, rotation, bond, slab, blocks, overlaps):
+def purify(place, live_count, rotation, bond, slab, overlaps, blocks):
     smem, vmem = pl.BlockSpec(memory_space=pltpu.SMEM), pl.BlockSpec(memory_space=pltpu.VMEM)
     return pl.pallas_call(
         purify_kernel,
         out_shape=jax.ShapeDtypeStruct(slab.shape, jnp.float32),
-        in_specs=[smem] * 4 + [vmem] * 7,
+        in_specs=[smem] * 4 + [vmem] * 11,
         out_specs=vmem,
         compiler_params=pltpu.CompilerParams(vmem_limit_bytes=24 * MIB),
         name="purify",
-    )(place, live_count, rotation, bond, slab, blocks, *overlaps)
+    )(place, live_count, rotation, bond, slab, *overlaps, *blocks)
 
 
 def swapped(block, axis, partner):
@@ -372,40 +434,37 @@
 
 
 def shards(psi, potential, kernel, live_count, rotation, bond):
-    kern_count = lax.axis_size("kern")
+    atom_count, kern_count = lax.axis_size("atoms"), lax.axis_size("kern")
     depth, cells = psi.shape[2:]
     place = jnp.stack([lax.axis_index("atoms"), lax.axis_index("kern")]).astype(jnp.int32)
-    odd_region, odd_chip = place[0] % 2 == 1, place[0] // 2 % 2 == 1
     along_kern = [lambda at, by=by: at ^ by for by in range(kern_count)]
 
+    got = lax.all_to_all(psi, "atoms", split_axis=0, concat_axis=0, tiled=True)
+
     slab = kernel[0]
-    with_even, with_odd = swapped(slab, "atoms", even_chip_with_next), swapped(slab, "atoms", odd_chip_with_next)
-    psi, with_even, with_odd = lax.optimization_barrier((psi, with_even, with_odd))
-
-    got = lax.all_to_all(psi, "atoms", split_axis=0, concat_axis=0, tiled=True)
-
-    before_two, after_two = jnp.where(odd_chip, with_even, with_odd), jnp.where(odd_chip, with_odd, with_even)
-    other, beyond = swapped(jnp.stack([slab, jnp.where(odd_region, before_two, after_two)]), "atoms", same_chip)
-    before, after = jnp.where(odd_region, other, beyond), jnp.where(odd_region, beyond, other)
-    stack = jnp.concatenate([before_two[2:], before, slab, after, after_two[:1]], axis=0)
-    blocks = assemble(place, [stack] + [swapped(stack, "kern", partner) for partner in along_kern[1:]])
-    got, blocks = lax.optimization_barrier((got, blocks))
-
+    own = assemble(place, [slab] + [swapped(slab, "kern", partner) for partner in along_kern[1:]])
+    core = swapped(own, "atoms", same_chip)
+    cross = swapped(own, "atoms", next_region_across)
+    away = [(at, (at - 2 if at % 2 else at + 2) % atom_count) for at in range(atom_count)]
+    beyond = lax.ppermute(outward(place, own, ()), "atoms", away)
     boxes = got.reshape(-1, depth, cells)
-    share = gram(boxes)
-    half_sum = share + swapped(share, "kern", along_kern[1])
+    share = gram(boxes, (own, core))
+    shares = [share] + [swapped(share, "kern", partner) for partner in along_kern[1:]]
     inner, near, far, rims = ham_inner(place, boxes, potential[0])
-    half_sum, near, far = lax.optimization_barrier((half_sum, near, far))
-    inter = half_sum + swapped(half_sum, "kern", along_kern[3])
     near, far = swapped(near, "kern", along_kern[1]), swapped(far, "kern", along_kern[3])
-
-    partners = (same_chip, next_region_across, even_chip_with_next, odd_chip_with_next)
-    overlaps = [inter] + [swapped(inter, "atoms", partner) for partner in partners]
+    behind = swapped(outward(place, cross, (beyond, inner)), "atoms", same_chip)
+    inter = total(shares, (inner,))
+
+    near_core = swapped(inter, "atoms", same_chip)
+    two_even, two_odd = swapped(inter, "atoms", even_chip_with_next), swapped(inter, "atoms", odd_chip_with_next)
     slabs = ham_outer(place, inner, near, far, rims, potential[0], kern_count)
     parts = [slabs[0]] + [swapped(part, "kern", partner) for part, partner in zip(slabs[1:], along_kern[1:])]
     ham_mine = finish(place, live_count, rotation, parts)
-
-    kernel_new = purify(place, live_count, rotation, bond, slab, blocks, overlaps)
+    across = swapped(pick(place, two_even, two_odd, (slabs[0],)), "atoms", same_chip)
+    overlaps = [inter, near_core, across, two_even, two_odd]
+
+    blocks = [own, core, cross, beyond, behind]
+    kernel_new = purify(place, live_count, rotation, bond, slab, overlaps, blocks)
     return (ham_mine[None], kernel_new[None])
 
 

time: 158 us -> 152 us (0.962)
  local copies, waits for them, and re-layouts: 9.8 us -> 0.03 us
  starting transfers between devices: 38.6 us -> 40.5 us
    all_to_all x1, waiting for transfers between devices: 50.1 us -> 73.1 us  [shards(): got = lax.all_to_all(psi, 'atoms', split_axis=0, concat_axis=0, tiled=True)]
    ppermute x17 -> x18, waiting for transfers between devices: 40.1 us -> 18.1 us  [swapped(): lax.ppermute(block, axis, [(at, partner(at) % count) for at in range(coun...]
    unnamed x40 -> x12, local copies, waits for them, and re-layouts: 9.79 us -> 0.03 us
    ppermute x17 -> x18, starting transfers between devices: 30 us -> 23.5 us  [swapped(): lax.ppermute(block, axis, [(at, partner(at) % count) for at in range(coun...]
    all_to_all x1, starting transfers between devices: 8.6 us -> 13.3 us  [shards(): got = lax.all_to_all(psi, 'atoms', split_axis=0, concat_axis=0, tiled=True)]
    ppermute x0 -> x1, starting transfers between devices: none -> 3.72 us  [shards(): beyond = lax.ppermute(outward(place, own, ()), 'atoms', away)]
    pallas_call x0 -> x4, Pallas kernels: none -> 1.74 us  [the longest x2 1.14 us: outward(): pl.pallas_call(outward_kernel, out_shape=jax.ShapeDtypeStruct((2,) + bloc...]
  transfers between devices with their start and end apart: 18 -> 20, of which waited for: 9 -> 11; matrix products, arithmetic and copies ran while one was open for 0% -> 0% of each run, Pallas kernels for 8% -> 11%
where the time goes in v3:
time: 152 us
  waiting for transfers between devices  91.1 us (60%)
  starting transfers between devices  40.5 us (27%)
  Pallas kernels  19.2 us (13%)
    all_to_all x1, waiting for transfers between devices, shards(): got = lax.all_to_all(psi, 'atoms', split_axis=0, concat_axis=0, tiled=True)  73.1 us
    ppermute x18, starting transfers between devices, swapped(): lax.ppermute(block, axis, [(at, partner(at) % count) for at in range(coun...  23.5 us
    ppermute x18, waiting for transfers between devices, swapped(): lax.ppermute(block, axis, [(at, partner(at) % count) for at in range(coun...  18.1 us
    all_to_all x1, starting transfers between devices, shards(): got = lax.all_to_all(psi, 'atoms', split_axis=0, concat_axis=0, tiled=True)  13.3 us
    pallas_call x1, Pallas kernels, ham_inner(): pl.pallas_call(inner_kernel, grid=(depth // GROUP,), out_shape=[jax.Shape...  7.02 us
    pallas_call x1, Pallas kernels, gram(): pl.pallas_call(gram_kernel, grid=(depth // GROUP,), in_specs=[pl.BlockSpe...  4.26 us
    ppermute x1, starting transfers between devices, shards(): beyond = lax.ppermute(outward(place, own, ()), 'atoms', away)  3.72 us
  transfers between devices with their start and end apart: 20, of which 11 were waited for; matrix products, arithmetic and copies ran while one was open for 0% of the time, Pallas kernels for 11%

profile of v3, /device:TPU:1, one launch (start us, length us, event | category | flops | bytes accessed | tf_op | source)
XLA Modules:
  0.0 151.7 jit_solution(6117199046587762142)
XLA Ops:
  0.6 13.3 %all-to-all-start = ((bf16[64,4,32,256]{3,2,1,0:T(8,128)(2,1)}), bf16[64,4,32,256]{3,2,1,0:T(8,128)(2,1)}, u32[]{:S(2)}, u32[]{:S(2)}) async-start(bf16[64,4,32,256]{3,2,1,0:T(8,128)(2,1)} %param.8), calls=%async_computation | async-start | bytes 8388608 | tf_op jit(solution)/shard_map/all_to_all | solution.py:442
  14.0 1.4 collective-permute-start.5
  15.4 2.6 %collective-permute-start.6 = (f32[3,64,256]{2,1,0:T(8,128)S(1)}, f32[3,64,256]{2,1,0:T(8,128)S(1)}, u32[]{:S(2)}, u32[]{:S(2)}) collective-permute-start(f32[3,64,256]{2,1,0:T(8,128)S(1)} %bitcast.8), channel_id=1, source_target_pairs={{0,2},{1,3},{2,0},{3,1},{4,6},{5,7},{6,4},{7,5},{8,10},{9,11},{10,... | collective-permute-start | bytes 589832 | tf_op jit(solution)/shard_map/ppermute | solution.py:417
  18.1 2.0 %collective-permute-done.5.refs_1_ = f32[3,64,256]{2,1,0:T(8,128)S(1)} collective-permute-done((f32[3,64,256]{2,1,0:T(8,128)S(1)}, f32[3,64,256]{2,1,0:T(8,128)S(1)}, u32[]{:S(2)}, u32[]{:S(2)}) %collective-permute-start.5) | collective-permute-done | bytes 196640 | tf_op jit(solution)/shard_map/ppermute | solution.py:417
  20.1 6.7 %collective-permute-done.6.refs_2_ = f32[3,64,256]{2,1,0:T(8,128)S(1)} collective-permute-done((f32[3,64,256]{2,1,0:T(8,128)S(1)}, f32[3,64,256]{2,1,0:T(8,128)S(1)}, u32[]{:S(2)}, u32[]{:S(2)}) %collective-permute-start.6) | collective-permute-done | bytes 196640 | tf_op jit(solution)/shard_map/ppermute | solution.py:417
  26.8 2.5 %collective-permute-done.7.refs_3_ = f32[3,64,256]{2,1,0:T(8,128)S(1)} collective-permute-done((f32[3,64,256]{2,1,0:T(8,128)S(1)}, f32[3,64,256]{2,1,0:T(8,128)S(1)}, u32[]{:S(2)}, u32[]{:S(2)}) %collective-permute-start.7) | collective-permute-done | bytes 196640 | tf_op jit(solution)/shard_map/ppermute | solution.py:417
  29.3 0.6 assemble.1.refs_0_.blocks_ref.refs_5_
  30.0 1.5 collective-permute-start.8
  31.4 1.4 collective-permute-start.16
  32.8 0.6 outward.2
  33.4 3.7 %collective-permute-start.17 = (bf16[2,256,256]{2,1,0:T(8,128)(2,1)S(1)}, bf16[2,256,256]{2,1,0:T(8,128)(2,1)S(1)}, u32[]{:S(2)}, u32[]{:S(2)}) collective-permute-start(bf16[2,256,256]{2,1,0:T(8,128)(2,1)S(1)} %outward.2), channel_id=1, source_target_pairs={{0,8},{4,252},{8,16},{12,4},{16,24},{20,12},{24,32},{28,20},{32,40... | collective-permute-start | bytes 786440 | tf_op jit(solution)/shard_map/ppermute | solution.py:449
  37.1 73.1 %all-to-all-done = bf16[64,4,32,256]{3,2,1,0:T(8,128)(2,1)} async-done(((bf16[64,4,32,256]{3,2,1,0:T(8,128)(2,1)}), bf16[64,4,32,256]{3,2,1,0:T(8,128)(2,1)}, u32[]{:S(2)}, u32[]{:S(2)}) %all-to-all-start) | async-done | bytes 4194336 | tf_op jit(solution)/shard_map/all_to_all | solution.py:442
  110.2 4.3 %gram.1.refs_0_ = f32[160,256]{1,0:T(8,128)S(1)} custom-call(bf16[256,32,256]{2,1,0:T(8,128)(2,1)} %bitcast.2.box_ref, bf16[6,256,256]{2,1,0:T(8,128)(2,1)S(1)} %assemble.1.refs_0_.blocks_ref.refs_5_, bf16[6,256,256]{2,1,0:T(8,128)(2,1)S(1)} %collective-permute-done.8.refs_1_.refs_6_), custom_call_target="tpu_custom_call" | custom-call | flops 1073741824 | bytes 4194304 | tf_op jit(solution)/shard_map/gram/pallas_call | solution.py:92
  114.5 1.4 collective-permute-start.9
  115.8 2.6 %collective-permute-start.10 = (f32[160,256]{1,0:T(8,128)S(1)}, f32[160,256]{1,0:T(8,128)S(1)}, u32[]{:S(2)}, u32[]{:S(2)}) collective-permute-start(f32[160,256]{1,0:T(8,128)S(1)} %gram.1.refs_0_), channel_id=1, source_target_pairs={{0,2},{1,3},{2,0},{3,1},{4,6},{5,7},{6,4},{7,5},{8,10},{9,11},{10,... | collective-permute-start | bytes 491528 | tf_op jit(solution)/shard_map/ppermute | solution.py:417
  118.5 7.0 %ham_inner.1 = (f32[256,256]{1,0:T(8,128)S(1)}, bf16[256,512]{1,0:T(8,128)(2,1)S(1)}, bf16[256,512]{1,0:T(8,128)(2,1)S(1)}, bf16[2,256,1024]{2,1,0:T(8,128)(2,1)S(1)}) custom-call(s32[2]{0:T(128)S(1)} %pad_add_fusion.place_ref, bf16[256,256]{1,0:T(8,128)(2,1)S(1)} %copy-done.1, bf16[256,32,256]{2,1,0:T(8,128)(2,1)} %bitcast.2.box_ref, f32[32,256]{1,0:T(8,128)S(1)} %bitcast.12), custom_call_target="tpu_custom_call" | custom-call | flops 2147483648 | bytes 4194304 | tf_op jit(solution)/shard_map/ham_inner/pallas_call | solution.py:153
  125.6 0.7 collective-permute-done.10.refs_2_
  126.4 2.0 %collective-permute-start.1 = (bf16[256,512]{1,0:T(8,128)(2,1)S(1)}, bf16[256,512]{1,0:T(8,128)(2,1)S(1)}, u32[]{:S(2)}, u32[]{:S(2)}) collective-permute-start(bf16[256,512]{1,0:T(8,128)(2,1)S(1)} %get-tuple-element.12), channel_id=1, source_target_pairs={{0,3},{1,2},{2,1},{3,0},{4,7},{5,6},{6,5},{7,4},{8,11},{9,10},{10,... | collective-permute-start | bytes 786440 | tf_op jit(solution)/shard_map/ppermute | solution.py:417
  129.0 1.7 %collective-permute-start.14 = (f32[160,256]{1,0:T(8,128)S(1)}, f32[160,256]{1,0:T(8,128)S(1)}, u32[]{:S(2)}, u32[]{:S(2)}) collective-permute-start(f32[160,256]{1,0:T(8,128)S(1)} %total.1.refs_0_), channel_id=1, source_target_pairs={{0,248},{4,252},{8,16},{12,20},{16,8},{20,12},{24,32},{28,36},{32,... | collective-permute-start | bytes 491528 | tf_op jit(solution)/shard_map/ppermute | solution.py:417
  130.7 0.6 outward.3
  131.3 2.5 %collective-permute-start.18 = (bf16[2,256,256]{2,1,0:T(8,128)(2,1)S(1)}, bf16[2,256,256]{2,1,0:T(8,128)(2,1)S(1)}, u32[]{:S(2)}, u32[]{:S(2)}) collective-permute-start(bf16[2,256,256]{2,1,0:T(8,128)(2,1)S(1)} %outward.3), channel_id=1, source_target_pairs={{0,4},{4,0},{8,12},{12,8},{16,20},{20,16},{24,28},{28,24},{32,36},... | collective-permute-start | bytes 786440 | tf_op jit(solution)/shard_map/ppermute | solution.py:417
  133.8 0.6 collective-permute-start.12
  134.6 1.4 ham_outer.1
  136.5 0.6 pick.1
  137.0 2.5 %collective-permute-start.15 = (f32[160,256]{1,0:T(8,128)S(1)}, f32[160,256]{1,0:T(8,128)S(1)}, u32[]{:S(2)}, u32[]{:S(2)}) collective-permute-start(f32[160,256]{1,0:T(8,128)S(1)} %pick.1), channel_id=1, source_target_pairs={{0,4},{4,0},{8,12},{12,8},{16,20},{20,16},{24,28},{28,24},{32,36},... | collective-permute-start | bytes 491528 | tf_op jit(solution)/shard_map/ppermute | solution.py:417
  140.1 1.5 %collective-permute-start.3 = (f32[64,256]{1,0:T(8,128)S(1)}, f32[64,256]{1,0:T(8,128)S(1)}, u32[]{:S(2)}, u32[]{:S(2)}) collective-permute-start(f32[64,256]{1,0:T(8,128)S(1)} %get-tuple-element.16), channel_id=1, source_target_pairs={{0,2},{1,3},{2,0},{3,1},{4,6},{5,7},{6,4},{7,5},{8,10},{9,11},{10,... | collective-permute-start | bytes 196616 | tf_op jit(solution)/shard_map/ppermute | solution.py:417
  141.6 1.6 %collective-permute-done.2.refs_1_ = f32[64,256]{1,0:T(8,128)S(1)} collective-permute-done((f32[64,256]{1,0:T(8,128)S(1)}, f32[64,256]{1,0:T(8,128)S(1)}, u32[]{:S(2)}, u32[]{:S(2)}) %collective-permute-start.2) | collective-permute-done | bytes 65568 | tf_op jit(solution)/shard_map/ppermute | solution.py:417
  143.2 0.8 collective-permute-start.4
  144.1 0.6 collective-permute-done.3.refs_2_
  144.7 2.8 %collective-permute-done.4.refs_3_ = f32[64,256]{1,0:T(8,128)S(1)} collective-permute-done((f32[64,256]{1,0:T(8,128)S(1)}, f32[64,256]{1,0:T(8,128)S(1)}, u32[]{:S(2)}, u32[]{:S(2)}) %collective-permute-start.4) | collective-permute-done | bytes 65568 | tf_op jit(solution)/shard_map/ppermute | solution.py:417
  147.6 1.2 finish.1
  148.8 2.9 %purify.1 = f32[3,64,256]{2,1,0:T(8,128)} custom-call(s32[2]{0:T(128)S(1)} %pad_add_fusion.place_ref, s32[64]{0:T(128)S(1)} %copy-done.3, s32[64]{0:T(128)S(1)} %copy-done.4, s32[64]{0:T(128)S(1)} %copy-done.5, f32[3,64,256]{2,1,0:T(8,128)S(1)} %bitcast.11, f32[160,256]{1,0:T(8,128)S(1)} %total.1.refs_0_, f32[160,256]{1,0:T(8,128)S(1)} %collective-permute-done.12.refs_1_, ...), custom_call_target="tpu_custom_call" | custom-call | tf_op jit(solution)/shard_map/purify/pallas_call | solution.py:405
  (31 shorter events, 2.0 us)
Async XLA Ops:
  0.6 13.3 %copy-start = (f32[1,3,64,256]{3,2,1,0:T(8,128)S(1)}, f32[1,3,64,256]{3,2,1,0:T(8,128)}, u32[]{:S(2)}) copy-start(f32[1,3,64,256]{3,2,1,0:T(8,128)} %param.10) | copy-start | bytes 589828
  0.6 109.6 %all-to-all-start = ((bf16[64,4,32,256]{3,2,1,0:T(8,128)(2,1)}), bf16[64,4,32,256]{3,2,1,0:T(8,128)(2,1)}, u32[]{:S(2)}, u32[]{:S(2)}) async-start(bf16[64,4,32,256]{3,2,1,0:T(8,128)(2,1)} %param.8), calls=%async_computation | async-start | bytes 8388608 | tf_op jit(solution)/shard_map/all_to_all | solution.py:442
  14.0 6.1 %collective-permute-start.5 = (f32[3,64,256]{2,1,0:T(8,128)S(1)}, f32[3,64,256]{2,1,0:T(8,128)S(1)}, u32[]{:S(2)}, u32[]{:S(2)}) collective-permute-start(f32[3,64,256]{2,1,0:T(8,128)S(1)} %bitcast.7), channel_id=1, source_target_pairs={{0,1},{1,0},{2,3},{3,2},{4,5},{5,4},{6,7},{7,6},{8,9},{9,8},{10,11... | collective-permute-start | bytes 589832 | tf_op jit(solution)/shard_map/ppermute | solution.py:417
  15.4 11.5 %collective-permute-start.6 = (f32[3,64,256]{2,1,0:T(8,128)S(1)}, f32[3,64,256]{2,1,0:T(8,128)S(1)}, u32[]{:S(2)}, u32[]{:S(2)}) collective-permute-start(f32[3,64,256]{2,1,0:T(8,128)S(1)} %bitcast.8), channel_id=1, source_target_pairs={{0,2},{1,3},{2,0},{3,1},{4,6},{5,7},{6,4},{7,5},{8,10},{9,11},{10,... | collective-permute-start | bytes 589832 | tf_op jit(solution)/shard_map/ppermute | solution.py:417
  18.0 11.3 %collective-permute-start.7 = (f32[3,64,256]{2,1,0:T(8,128)S(1)}, f32[3,64,256]{2,1,0:T(8,128)S(1)}, u32[]{:S(2)}, u32[]{:S(2)}) collective-permute-start(f32[3,64,256]{2,1,0:T(8,128)S(1)} %bitcast.9), channel_id=1, source_target_pairs={{0,3},{1,2},{2,1},{3,0},{4,7},{5,6},{6,5},{7,4},{8,11},{9,10},{10,... | collective-permute-start | bytes 589832 | tf_op jit(solution)/shard_map/ppermute | solution.py:417
  18.1 100.4 %copy-start.1 = (bf16[256,256]{1,0:T(8,128)(2,1)S(1)}, bf16[256,256]{1,0:T(8,128)(2,1)}, u32[]{:S(2)}) copy-start(bf16[256,256]{1,0:T(8,128)(2,1)} %constant.11.clone.weights_ref) | copy-start | bytes 393220
  18.1 100.4 %copy-start.2 = (f32[1,32,256]{2,1,0:T(8,128)S(1)}, f32[1,32,256]{2,1,0:T(8,128)}, u32[]{:S(2)}) copy-start(f32[1,32,256]{2,1,0:T(8,128)} %param.9) | copy-start | bytes 98308
  30.0 7.2 %collective-permute-start.8 = (bf16[6,256,256]{2,1,0:T(8,128)(2,1)S(1)}, bf16[6,256,256]{2,1,0:T(8,128)(2,1)S(1)}, u32[]{:S(2)}, u32[]{:S(2)}) collective-permute-start(bf16[6,256,256]{2,1,0:T(8,128)(2,1)S(1)} %assemble.1.refs_0_.blocks_ref.refs_5_), channel_id=1, source_target_pairs={{0,4},{4,0},{8,12},{12,8},{16,20},{20,16},{24,28},{28,24},{32,36},... | collective-permute-start | bytes 2359304 | tf_op jit(solution)/shard_map/ppermute | solution.py:417
  31.4 99.2 %collective-permute-start.16 = (bf16[6,256,256]{2,1,0:T(8,128)(2,1)S(1)}, bf16[6,256,256]{2,1,0:T(8,128)(2,1)S(1)}, u32[]{:S(2)}, u32[]{:S(2)}) collective-permute-start(bf16[6,256,256]{2,1,0:T(8,128)(2,1)S(1)} %assemble.1.refs_0_.blocks_ref.refs_5_), channel_id=1, source_target_pairs={{0,252},{4,8},{8,4},{12,16},{16,12},{20,24},{24,20},{28,32},{32,28... | collective-permute-start | bytes 2359304 | tf_op jit(solution)/shard_map/ppermute | solution.py:417
  33.4 95.6 %collective-permute-start.17 = (bf16[2,256,256]{2,1,0:T(8,128)(2,1)S(1)}, bf16[2,256,256]{2,1,0:T(8,128)(2,1)S(1)}, u32[]{:S(2)}, u32[]{:S(2)}) collective-permute-start(bf16[2,256,256]{2,1,0:T(8,128)(2,1)S(1)} %outward.2), channel_id=1, source_target_pairs={{0,8},{4,252},{8,16},{12,4},{16,24},{20,12},{24,32},{28,20},{32,40... | collective-permute-start | bytes 786440 | tf_op jit(solution)/shard_map/ppermute | solution.py:449
  114.5 11.1 %collective-permute-start.9 = (f32[160,256]{1,0:T(8,128)S(1)}, f32[160,256]{1,0:T(8,128)S(1)}, u32[]{:S(2)}, u32[]{:S(2)}) collective-permute-start(f32[160,256]{1,0:T(8,128)S(1)} %gram.1.refs_0_), channel_id=1, source_target_pairs={{0,1},{1,0},{2,3},{3,2},{4,5},{5,4},{6,7},{7,6},{8,9},{9,8},{10,11... | collective-permute-start | bytes 491528 | tf_op jit(solution)/shard_map/ppermute | solution.py:417
  115.8 10.5 %collective-permute-start.10 = (f32[160,256]{1,0:T(8,128)S(1)}, f32[160,256]{1,0:T(8,128)S(1)}, u32[]{:S(2)}, u32[]{:S(2)}) collective-permute-start(f32[160,256]{1,0:T(8,128)S(1)} %gram.1.refs_0_), channel_id=1, source_target_pairs={{0,2},{1,3},{2,0},{3,1},{4,6},{5,7},{6,4},{7,5},{8,10},{9,11},{10,... | collective-permute-start | bytes 491528 | tf_op jit(solution)/shard_map/ppermute | solution.py:417
  118.5 10.2 %collective-permute-start.11 = (f32[160,256]{1,0:T(8,128)S(1)}, f32[160,256]{1,0:T(8,128)S(1)}, u32[]{:S(2)}, u32[]{:S(2)}) collective-permute-start(f32[160,256]{1,0:T(8,128)S(1)} %gram.1.refs_0_), channel_id=1, source_target_pairs={{0,3},{1,2},{2,1},{3,0},{4,7},{5,6},{6,5},{7,4},{8,11},{9,10},{10,... | collective-permute-start | bytes 491528 | tf_op jit(solution)/shard_map/ppermute | solution.py:417
  125.5 22.1 %copy-start.3 = (s32[64]{0:T(128)S(1)}, s32[64]{0:T(128)}, u32[]{:S(2)}) copy-start(s32[64]{0:T(128)} %count_ref.3) | copy-start | bytes 772
  125.5 22.1 %copy-start.4 = (s32[64]{0:T(128)S(1)}, s32[64]{0:T(128)}, u32[]{:S(2)}) copy-start(s32[64]{0:T(128)} %rotation_ref.3) | copy-start | bytes 772
  125.5 23.3 %copy-start.5 = (s32[64]{0:T(128)S(1)}, s32[64]{0:T(128)}, u32[]{:S(2)}) copy-start(s32[64]{0:T(128)} %bond_ref.1) | copy-start | bytes 772
  125.5 8.2 %collective-permute-start = (bf16[256,512]{1,0:T(8,128)(2,1)S(1)}, bf16[256,512]{1,0:T(8,128)(2,1)S(1)}, u32[]{:S(2)}, u32[]{:S(2)}) collective-permute-start(bf16[256,512]{1,0:T(8,128)(2,1)S(1)} %get-tuple-element.11), channel_id=1, source_target_pairs={{0,1},{1,0},{2,3},{3,2},{4,5},{5,4},{6,7},{7,6},{8,9},{9,8},{10,11... | collective-permute-start | bytes 786440 | tf_op jit(solution)/shard_map/ppermute | solution.py:417
  126.4 8.2 %collective-permute-start.1 = (bf16[256,512]{1,0:T(8,128)(2,1)S(1)}, bf16[256,512]{1,0:T(8,128)(2,1)S(1)}, u32[]{:S(2)}, u32[]{:S(2)}) collective-permute-start(bf16[256,512]{1,0:T(8,128)(2,1)S(1)} %get-tuple-element.12), channel_id=1, source_target_pairs={{0,3},{1,2},{2,1},{3,0},{4,7},{5,6},{6,5},{7,4},{8,11},{9,10},{10,... | collective-permute-start | bytes 786440 | tf_op jit(solution)/shard_map/ppermute | solution.py:417
  128.7 7.3 %collective-permute-start.13 = (f32[160,256]{1,0:T(8,128)S(1)}, f32[160,256]{1,0:T(8,128)S(1)}, u32[]{:S(2)}, u32[]{:S(2)}) collective-permute-start(f32[160,256]{1,0:T(8,128)S(1)} %total.1.refs_0_), channel_id=1, source_target_pairs={{0,8},{4,12},{8,0},{12,4},{16,24},{20,28},{24,16},{28,20},{32,40},... | collective-permute-start | bytes 491528 | tf_op jit(solution)/shard_map/ppermute | solution.py:417
  129.0 7.5 %collective-permute-start.14 = (f32[160,256]{1,0:T(8,128)S(1)}, f32[160,256]{1,0:T(8,128)S(1)}, u32[]{:S(2)}, u32[]{:S(2)}) collective-permute-start(f32[160,256]{1,0:T(8,128)S(1)} %total.1.refs_0_), channel_id=1, source_target_pairs={{0,248},{4,252},{8,16},{12,20},{16,8},{20,12},{24,32},{28,36},{32,... | collective-permute-start | bytes 491528 | tf_op jit(solution)/shard_map/ppermute | solution.py:417
  131.3 17.5 %collective-permute-start.18 = (bf16[2,256,256]{2,1,0:T(8,128)(2,1)S(1)}, bf16[2,256,256]{2,1,0:T(8,128)(2,1)S(1)}, u32[]{:S(2)}, u32[]{:S(2)}) collective-permute-start(bf16[2,256,256]{2,1,0:T(8,128)(2,1)S(1)} %outward.3), channel_id=1, source_target_pairs={{0,4},{4,0},{8,12},{12,8},{16,20},{20,16},{24,28},{28,24},{32,36},... | collective-permute-start | bytes 786440 | tf_op jit(solution)/shard_map/ppermute | solution.py:417
  133.8 15.0 %collective-permute-start.12 = (f32[160,256]{1,0:T(8,128)S(1)}, f32[160,256]{1,0:T(8,128)S(1)}, u32[]{:S(2)}, u32[]{:S(2)}) collective-permute-start(f32[160,256]{1,0:T(8,128)S(1)} %total.1.refs_0_), channel_id=1, source_target_pairs={{0,4},{4,0},{8,12},{12,8},{16,20},{20,16},{24,28},{28,24},{32,36},... | collective-permute-start | bytes 491528 | tf_op jit(solution)/shard_map/ppermute | solution.py:417
  137.0 11.8 %collective-permute-start.15 = (f32[160,256]{1,0:T(8,128)S(1)}, f32[160,256]{1,0:T(8,128)S(1)}, u32[]{:S(2)}, u32[]{:S(2)}) collective-permute-start(f32[160,256]{1,0:T(8,128)S(1)} %pick.1), channel_id=1, source_target_pairs={{0,4},{4,0},{8,12},{12,8},{16,20},{20,16},{24,28},{28,24},{32,36},... | collective-permute-start | bytes 491528 | tf_op jit(solution)/shard_map/ppermute | solution.py:417
  139.6 3.7 %collective-permute-start.2 = (f32[64,256]{1,0:T(8,128)S(1)}, f32[64,256]{1,0:T(8,128)S(1)}, u32[]{:S(2)}, u32[]{:S(2)}) collective-permute-start(f32[64,256]{1,0:T(8,128)S(1)} %get-tuple-element.15), channel_id=1, source_target_pairs={{0,1},{1,0},{2,3},{3,2},{4,5},{5,4},{6,7},{7,6},{8,9},{9,8},{10,11... | collective-permute-start | bytes 196616 | tf_op jit(solution)/shard_map/ppermute | solution.py:417
  140.1 4.6 %collective-permute-start.3 = (f32[64,256]{1,0:T(8,128)S(1)}, f32[64,256]{1,0:T(8,128)S(1)}, u32[]{:S(2)}, u32[]{:S(2)}) collective-permute-start(f32[64,256]{1,0:T(8,128)S(1)} %get-tuple-element.16), channel_id=1, source_target_pairs={{0,2},{1,3},{2,0},{3,1},{4,6},{5,7},{6,4},{7,5},{8,10},{9,11},{10,... | collective-permute-start | bytes 196616 | tf_op jit(solution)/shard_map/ppermute | solution.py:417
  143.2 4.3 %collective-permute-start.4 = (f32[64,256]{1,0:T(8,128)S(1)}, f32[64,256]{1,0:T(8,128)S(1)}, u32[]{:S(2)}, u32[]{:S(2)}) collective-permute-start(f32[64,256]{1,0:T(8,128)S(1)} %get-tuple-element.17), channel_id=1, source_target_pairs={{0,3},{1,2},{2,1},{3,0},{4,7},{5,6},{6,5},{7,4},{8,11},{9,10},{10,... | collective-permute-start | bytes 196616 | tf_op jit(solution)/shard_map/ppermute | solution.py:417

commit v4 on v3

--- a/solution.py
+++ b/solution.py
@@ -67,15 +67,22 @@
             planes_ref[own, start + plane * cells : start + (plane + 1) * cells] = tile[plane]
 
 
-def gram_kernel(box_ref, *refs):
-    inter_ref, planes_ref = refs[-2:]
-    rows = box_ref.shape[0]
+def gram_kernel(place_ref, box_ref, *refs):
+    inter_ref, near_ref, far_ref, planes_ref = refs[-4:]
+    rows, depth, cells = box_ref.shape
     by_planes(box_ref, planes_ref, 0)
     upper, lower = planes_ref[: rows // 2], planes_ref[rows // 2 :]
     top = lax.dot_general(upper, planes_ref[...], NT, preferred_element_type=jnp.float32)
     corner = lax.dot_general(lower, lower, NT, preferred_element_type=jnp.float32)
     share = jnp.concatenate(packed(top, corner), axis=0)
+    kept = share.shape[0]
     first = pl.program_id(0) == 0
+    odd = place_ref[1] % 2 == 1
+
+    def put(edge_ref, start):
+        for edge in range(EDGE):
+            at = 2 * kept + edge * rows
+            edge_ref[at : at + rows] = planes_ref[:, (start + edge) * cells : (start + edge + 1) * cells]
 
     @pl.when(first)
     def _():
@@ -83,23 +90,46 @@
 
     @pl.when(jnp.logical_not(first))
     def _():
-        inter_ref[...] += share
-
-
-def gram(boxes, ahead):
+        whole = inter_ref[...] + share
+        inter_ref[...] = whole
+        high, low = halves_of(whole)
+        for message_ref in (near_ref, far_ref):
+            message_ref[:kept] = high
+            message_ref[kept : 2 * kept] = low
+
+    @pl.when(jnp.logical_and(first, odd))
+    def _():
+        put(near_ref, 0)
+
+    @pl.when(jnp.logical_and(first, jnp.logical_not(odd)))
+    def _():
+        put(far_ref, 0)
+
+    @pl.when(jnp.logical_and(jnp.logical_not(first), odd))
+    def _():
+        put(far_ref, depth - EDGE)
+
+    @pl.when(jnp.logical_and(jnp.logical_not(first), jnp.logical_not(odd)))
+    def _():
+        put(near_ref, depth - EDGE)
+
+
+def gram(place, boxes, ahead):
     rows, depth, cells = boxes.shape
     kept = rows * 5 // 8
+    whole = lambda step: (0, 0)
+    message = jax.ShapeDtypeStruct((2 * kept + EDGE * rows, cells), jnp.bfloat16)
     return pl.pallas_call(
         gram_kernel,
         grid=(depth // GROUP,),
-        in_specs=[pl.BlockSpec((rows, GROUP, cells), lambda step: (0, step, 0))] + [ANY] * len(ahead),
-        out_specs=pl.BlockSpec((kept, rows), lambda step: (0, 0)),
-        out_shape=jax.ShapeDtypeStruct((kept, rows), jnp.float32),
+        in_specs=[pl.BlockSpec(memory_space=pltpu.SMEM), pl.BlockSpec((rows, GROUP, cells), lambda step: (0, step, 0))] + [ANY] * len(ahead),
+        out_specs=[pl.BlockSpec((kept, rows), whole), pl.BlockSpec(message.shape, whole), pl.BlockSpec(message.shape, whole)],
+        out_shape=[jax.ShapeDtypeStruct((kept, rows), jnp.float32), message, message],
         scratch_shapes=[pltpu.VMEM((rows, GROUP * cells), jnp.bfloat16)],
         compiler_params=pltpu.CompilerParams(vmem_limit_bytes=16 * MIB),
         cost_estimate=pl.CostEstimate(flops=2 * rows * rows * depth * cells, bytes_accessed=2 * rows * depth * cells, transcendentals=0),
         name="gram",
-    )(boxes, *ahead)
+    )(place, boxes, *ahead)
 
 
 def image_of(plane_at, plane, weights, potential):
@@ -111,7 +141,7 @@
     return (lap * (-1.0 / 24.0) + potential * field.astype(jnp.float32)).astype(jnp.bfloat16)
 
 
-def inner_kernel(place_ref, weights_ref, box_ref, potential_ref, ham_ref, near_ref, far_ref, rims_ref, planes_ref, image_ref):
+def inner_kernel(weights_ref, box_ref, potential_ref, ham_ref, rims_ref, planes_ref, image_ref):
     depth, cells = potential_ref.shape
     block = box_ref.shape[1]
     steps = depth // block
@@ -132,50 +162,34 @@
             image_ref[:, at : at + cells] = image_of(plane_at, plane, weights, potential_ref[plane : plane + 1, :])
         inner = planes_ref[:, edge : depth * cells - edge]
         ham_ref[...] = lax.dot_general(inner, image_ref[...], NT, preferred_element_type=jnp.float32)
-        low, high = planes_ref[:, :edge], planes_ref[:, depth * cells - edge :]
         rims_ref[0] = planes_ref[:, : 2 * edge]
         rims_ref[1] = planes_ref[:, depth * cells - 2 * edge :]
-        odd = place_ref[1] % 2 == 1
-
-        @pl.when(odd)
-        def _():
-            near_ref[...], far_ref[...] = low, high
-
-        @pl.when(jnp.logical_not(odd))
-        def _():
-            near_ref[...], far_ref[...] = high, low
-
-
-def ham_inner(place, boxes, potential):
+
+
+def ham_inner(boxes, potential):
     rows, depth, cells = boxes.shape
     whole = lambda step: (0, 0)
-    edge = jax.ShapeDtypeStruct((rows, EDGE * cells), jnp.bfloat16)
     return pl.pallas_call(
         inner_kernel,
         grid=(depth // GROUP,),
         out_shape=[
             jax.ShapeDtypeStruct((rows, rows), jnp.float32),
-            edge,
-            edge,
             jax.ShapeDtypeStruct((2, rows, 2 * EDGE * cells), jnp.bfloat16),
         ],
         in_specs=[
-            pl.BlockSpec(memory_space=pltpu.SMEM),
             pl.BlockSpec((cells, cells), whole),
             pl.BlockSpec((rows, GROUP, cells), lambda step: (0, step, 0)),
             pl.BlockSpec((depth, cells), whole),
         ],
         out_specs=[
             pl.BlockSpec((rows, rows), whole),
-            pl.BlockSpec(edge.shape, whole),
-            pl.BlockSpec(edge.shape, whole),
             pl.BlockSpec((2, rows, 2 * EDGE * cells), lambda step: (0, 0, 0)),
         ],
         scratch_shapes=[pltpu.VMEM((rows, depth * cells), jnp.bfloat16), pltpu.VMEM((rows, (depth - 2 * EDGE) * cells), jnp.bfloat16)],
         compiler_params=pltpu.CompilerParams(vmem_limit_bytes=24 * MIB),
         cost_estimate=pl.CostEstimate(flops=4 * rows * rows * depth * cells, bytes_accessed=2 * rows * depth * cells, transcendentals=0),
         name="ham_inner",
-    )(place, jnp.asarray(plane_weights(cells), jnp.bfloat16), boxes, potential)
+    )(jnp.asarray(plane_weights(cells), jnp.bfloat16), boxes, potential)
 
 
 def outer_kernel(count, place_ref, weights_ref, inner_ref, near_ref, far_ref, rims_ref, potential_ref, *refs):
@@ -183,9 +197,11 @@
     depth, cells = potential_ref.shape
     position = place_ref[1]
     odd = position % 2 == 1
-    none = jnp.zeros_like(near_ref[...])
-    below = jnp.where(position > 0, jnp.where(odd, near_ref[...], far_ref[...]), none)
-    above = jnp.where(position < count - 1, jnp.where(odd, far_ref[...], near_ref[...]), none)
+    edges = near_ref.shape[0] - EDGE * inner_ref.shape[0]
+    near, far = near_ref[edges:], far_ref[edges:]
+    none = jnp.zeros_like(near)
+    below = jnp.where(position > 0, jnp.where(odd, near, far), none)
+    above = jnp.where(position < count - 1, jnp.where(odd, far, near), none)
     weights = weights_ref[...]
     total = inner_ref[...]
     for side, (halo, start) in enumerate(((below, -EDGE), (above, depth))):
@@ -195,8 +211,8 @@
             if 0 <= plane < depth:
                 at = (plane - rim_start) * cells
                 return rims_ref[side, :, at : at + cells]
-            at = (plane - start) * cells
-            return halo[:, at : at + cells]
+            at = (plane - start) * halo.shape[0] // EDGE
+            return halo[at : at + halo.shape[0] // EDGE]
 
         for plane in range(EDGE) if side == 0 else range(depth - EDGE, depth):
             image = image_of(plane_at, plane, weights, potential_ref[plane : plane + 1, :])
@@ -241,37 +257,42 @@
     )(place, blocks, *ahead)
 
 
-def pick_kernel(place_ref, even_ref, odd_ref, *refs):
+def pick_kernel(place_ref, own_ref, even_ref, odd_ref, *refs):
     even = place_ref[0] % 2 == place_ref[0] // 2 % 2
-    refs[-1][...] = jnp.where(even, even_ref[...], odd_ref[...])
-
-
-def pick(place, even, odd, ahead):
+    refs[-1][0] = own_ref[...]
+    refs[-1][1] = jnp.where(even, even_ref[...], odd_ref[...])
+
+
+def pick(place, own, even, odd, ahead):
     vmem = pl.BlockSpec(memory_space=pltpu.VMEM)
     return pl.pallas_call(
         pick_kernel,
-        out_shape=jax.ShapeDtypeStruct(even.shape, even.dtype),
-        in_specs=[pl.BlockSpec(memory_space=pltpu.SMEM), vmem, vmem] + [ANY] * len(ahead),
+        out_shape=jax.ShapeDtypeStruct((2,) + own.shape, own.dtype),
+        in_specs=[pl.BlockSpec(memory_space=pltpu.SMEM), vmem, vmem, vmem] + [ANY] * len(ahead),
         out_specs=vmem,
         compiler_params=pltpu.CompilerParams(vmem_limit_bytes=4 * MIB),
         name="pick",
-    )(place, even, odd, *ahead)
-
-
-def total_kernel(count, *refs):
-    refs[-1][...] = sum(ref[...] for ref in refs[:count])
-
-
-def total(parts, ahead):
+    )(place, own, even, odd, *ahead)
+
+
+def total_kernel(own_ref, across_ref, near_ref, far_ref, *refs):
+    kept = own_ref.shape[0]
+    whole = own_ref[...] + across_ref[...]
+    for message_ref in (near_ref, far_ref):
+        whole = whole + (message_ref[:kept].astype(jnp.float32) + message_ref[kept : 2 * kept].astype(jnp.float32))
+    refs[-1][...] = whole
+
+
+def total(own, across, near, far, ahead):
     vmem = pl.BlockSpec(memory_space=pltpu.VMEM)
     return pl.pallas_call(
-        functools.partial(total_kernel, len(parts)),
-        out_shape=jax.ShapeDtypeStruct(parts[0].shape, parts[0].dtype),
-        in_specs=[vmem] * len(parts) + [ANY] * len(ahead),
+        total_kernel,
+        out_shape=jax.ShapeDtypeStruct(own.shape, own.dtype),
+        in_specs=[vmem] * 4 + [ANY] * len(ahead),
         out_specs=vmem,
         compiler_params=pltpu.CompilerParams(vmem_limit_bytes=4 * MIB),
         name="total",
-    )(*parts, *ahead)
+    )(own, across, near, far, *ahead)
 
 
 def halves_of(value):
@@ -319,8 +340,8 @@
     return (shifted < count).astype(jnp.float32)
 
 
-def finish_kernel(place_ref, count_ref, rotation_ref, *refs):
-    part_refs, out_ref = refs[:-1], refs[-1]
+def finish_kernel(parts, place_ref, count_ref, rotation_ref, *refs):
+    part_refs, out_ref = refs[:parts], refs[-1]
     rows, columns = out_ref.shape
     count, rotation = count_ref[place_ref[0]], rotation_ref[place_ref[0]]
     own_rows = lax.broadcasted_iota(jnp.int32, (rows, 1), 0) + place_ref[1] * rows
@@ -329,21 +350,21 @@
     out_ref[...] = sum(ref[...] for ref in part_refs) * kept
 
 
-def finish(place, live_count, rotation, parts):
+def finish(place, live_count, rotation, parts, ahead):
     smem, vmem = pl.BlockSpec(memory_space=pltpu.SMEM), pl.BlockSpec(memory_space=pltpu.VMEM)
     return pl.pallas_call(
-        finish_kernel,
+        functools.partial(finish_kernel, len(parts)),
         out_shape=jax.ShapeDtypeStruct(parts[0].shape, jnp.float32),
-        in_specs=[smem] * 3 + [vmem] * len(parts),
+        in_specs=[smem] * 3 + [vmem] * len(parts) + [ANY] * len(ahead),
         out_specs=vmem,
         compiler_params=pltpu.CompilerParams(vmem_limit_bytes=4 * MIB),
         name="finish",
-    )(place, live_count, rotation, *parts)
+    )(place, live_count, rotation, *parts, *ahead)
 
 
 def purify_kernel(place_ref, count_ref, rotation_ref, bond_ref, slab_ref, *refs):
-    block_refs, out_ref = refs[5:10], refs[10]
-    own, core, cross, even_pair, odd_pair = (ref[...] for ref in refs[:5])
+    block_refs, out_ref = refs[4:9], refs[9]
+    own, (core, cross), even_pair, odd_pair = (ref[...] for ref in refs[:4])
     odd_region, odd_chip = place_ref[0] % 2 == 1, place_ref[0] // 2 % 2 == 1
     shares = {
         -2: jnp.where(odd_chip, even_pair, odd_pair),
@@ -405,7 +426,7 @@
     return pl.pallas_call(
         purify_kernel,
         out_shape=jax.ShapeDtypeStruct(slab.shape, jnp.float32),
-        in_specs=[smem] * 4 + [vmem] * 11,
+        in_specs=[smem] * 4 + [vmem] * 10,
         out_specs=vmem,
         compiler_params=pltpu.CompilerParams(vmem_limit_bytes=24 * MIB),
         name="purify",
@@ -448,20 +469,20 @@
     away = [(at, (at - 2 if at % 2 else at + 2) % atom_count) for at in range(atom_count)]
     beyond = lax.ppermute(outward(place, own, ()), "atoms", away)
     boxes = got.reshape(-1, depth, cells)
-    share = gram(boxes, (own, core))
-    shares = [share] + [swapped(share, "kern", partner) for partner in along_kern[1:]]
-    inner, near, far, rims = ham_inner(place, boxes, potential[0])
+    share, near, far = gram(place, boxes, (own, core))
+    opposite = swapped(share, "kern", along_kern[2])
     near, far = swapped(near, "kern", along_kern[1]), swapped(far, "kern", along_kern[3])
-    behind = swapped(outward(place, cross, (beyond, inner)), "atoms", same_chip)
-    inter = total(shares, (inner,))
-
-    near_core = swapped(inter, "atoms", same_chip)
+    inner, rims = ham_inner(boxes, potential[0])
+    inter = total(share, opposite, near, far, (inner, cross, beyond))
+    behind = swapped(outward(place, cross, (inter,)), "atoms", same_chip)
+
     two_even, two_odd = swapped(inter, "atoms", even_chip_with_next), swapped(inter, "atoms", odd_chip_with_next)
     slabs = ham_outer(place, inner, near, far, rims, potential[0], kern_count)
     parts = [slabs[0]] + [swapped(part, "kern", partner) for part, partner in zip(slabs[1:], along_kern[1:])]
-    ham_mine = finish(place, live_count, rotation, parts)
-    across = swapped(pick(place, two_even, two_odd, (slabs[0],)), "atoms", same_chip)
-    overlaps = [inter, near_core, across, two_even, two_odd]
+    picked = pick(place, inter, two_even, two_odd, parts)
+    from_core = swapped(picked, "atoms", same_chip)
+    ham_mine = finish(place, live_count, rotation, parts, (picked,))
+    overlaps = [inter, from_core, two_even, two_odd]
 
     blocks = [own, core, cross, beyond, behind]
     kernel_new = purify(place, live_count, rotation, bond, slab, overlaps, blocks)

time: 152 us -> 152 us (level)
  waiting for transfers between devices: 91.1 us -> 97.7 us
  starting transfers between devices: 40.5 us -> 34.3 us
    all_to_all x1, waiting for transfers between devices: 73.1 us -> 76.8 us  [shards(): got = lax.all_to_all(psi, 'atoms', split_axis=0, concat_axis=0, tiled=True)]
    ppermute x1, starting transfers between devices: 3.72 us -> 0.08 us  [shards(): beyond = lax.ppermute(outward(place, own, ()), 'atoms', away)]
    ppermute x18 -> x15, waiting for transfers between devices: 18.1 us -> 20.9 us  [swapped(): lax.ppermute(block, axis, [(at, partner(at) % count) for at in range(coun...]
    ppermute x18 -> x15, starting transfers between devices: 23.5 us -> 20.9 us  [swapped(): lax.ppermute(block, axis, [(at, partner(at) % count) for at in range(coun...]
  transfers between devices with their start and end apart: 20 -> 17, of which waited for: 11 -> 9; matrix products, arithmetic and copies ran while one was open for 0% -> 0% of each run, Pallas kernels for 11% -> 10%
where the time goes in v4:
time: 152 us
  waiting for transfers between devices  97.7 us (64%)
  starting transfers between devices  34.3 us (23%)
  Pallas kernels  19.3 us (13%)
    all_to_all x1, waiting for transfers between devices, shards(): got = lax.all_to_all(psi, 'atoms', split_axis=0, concat_axis=0, tiled=True)  76.8 us
    ppermute x15, starting transfers between devices, swapped(): lax.ppermute(block, axis, [(at, partner(at) % count) for at in range(coun...  20.9 us
    ppermute x15, waiting for transfers between devices, swapped(): lax.ppermute(block, axis, [(at, partner(at) % count) for at in range(coun...  20.9 us
    all_to_all x1, starting transfers between devices, shards(): got = lax.all_to_all(psi, 'atoms', split_axis=0, concat_axis=0, tiled=True)  13.3 us
    pallas_call x1, Pallas kernels, ham_inner(): pl.pallas_call(inner_kernel, grid=(depth // GROUP,), out_shape=[jax.Shape...  6.96 us
    pallas_call x1, Pallas kernels, gram(): pl.pallas_call(gram_kernel, grid=(depth // GROUP,), in_specs=[pl.BlockSpe...  4.41 us
  transfers between devices with their start and end apart: 17, of which 9 were waited for; matrix products, arithmetic and copies ran while one was open for 0% of the time, Pallas kernels for 10%

profile of v4, /device:TPU:1, one launch (start us, length us, event | category | flops | bytes accessed | tf_op | source)
XLA Modules:
  0.0 152.2 jit_solution(15523283838764203792)
XLA Ops:
  0.6 13.3 %all-to-all-start = ((bf16[64,4,32,256]{3,2,1,0:T(8,128)(2,1)}), bf16[64,4,32,256]{3,2,1,0:T(8,128)(2,1)}, u32[]{:S(2)}, u32[]{:S(2)}) async-start(bf16[64,4,32,256]{3,2,1,0:T(8,128)(2,1)} %param.8), calls=%async_computation | async-start | bytes 8388608 | tf_op jit(solution)/shard_map/all_to_all | solution.py:463
  14.0 1.4 collective-permute-start
  15.4 2.6 %collective-permute-start.1 = (f32[3,64,256]{2,1,0:T(8,128)S(1)}, f32[3,64,256]{2,1,0:T(8,128)S(1)}, u32[]{:S(2)}, u32[]{:S(2)}) collective-permute-start(f32[3,64,256]{2,1,0:T(8,128)S(1)} %bitcast.8), channel_id=1, source_target_pairs={{0,2},{1,3},{2,0},{3,1},{4,6},{5,7},{6,4},{7,5},{8,10},{9,11},{10,... | collective-permute-start | bytes 589832 | tf_op jit(solution)/shard_map/ppermute | solution.py:438
  18.1 2.0 %collective-permute-done.refs_1_ = f32[3,64,256]{2,1,0:T(8,128)S(1)} collective-permute-done((f32[3,64,256]{2,1,0:T(8,128)S(1)}, f32[3,64,256]{2,1,0:T(8,128)S(1)}, u32[]{:S(2)}, u32[]{:S(2)}) %collective-permute-start) | collective-permute-done | bytes 196640 | tf_op jit(solution)/shard_map/ppermute | solution.py:438
  20.1 6.7 %collective-permute-done.1.refs_2_ = f32[3,64,256]{2,1,0:T(8,128)S(1)} collective-permute-done((f32[3,64,256]{2,1,0:T(8,128)S(1)}, f32[3,64,256]{2,1,0:T(8,128)S(1)}, u32[]{:S(2)}, u32[]{:S(2)}) %collective-permute-start.1) | collective-permute-done | bytes 196640 | tf_op jit(solution)/shard_map/ppermute | solution.py:438
  26.8 2.5 %collective-permute-done.2.refs_3_ = f32[3,64,256]{2,1,0:T(8,128)S(1)} collective-permute-done((f32[3,64,256]{2,1,0:T(8,128)S(1)}, f32[3,64,256]{2,1,0:T(8,128)S(1)}, u32[]{:S(2)}, u32[]{:S(2)}) %collective-permute-start.2) | collective-permute-done | bytes 196640 | tf_op jit(solution)/shard_map/ppermute | solution.py:438
  29.3 0.6 assemble.1.refs_0_.blocks_ref.refs_4_
  30.0 1.5 collective-permute-start.3
  31.4 1.4 collective-permute-start.10
  32.8 0.5 collective-permute-done.3.refs_1_.refs_5_
  33.4 76.8 %all-to-all-done = bf16[64,4,32,256]{3,2,1,0:T(8,128)(2,1)} async-done(((bf16[64,4,32,256]{3,2,1,0:T(8,128)(2,1)}), bf16[64,4,32,256]{3,2,1,0:T(8,128)(2,1)}, u32[]{:S(2)}, u32[]{:S(2)}) %all-to-all-start) | async-done | bytes 4194336 | tf_op jit(solution)/shard_map/all_to_all | solution.py:463
  110.2 4.4 %gram.1 = (f32[160,256]{1,0:T(8,128)S(1)}, bf16[832,256]{1,0:T(8,128)(2,1)S(1)}, bf16[832,256]{1,0:T(8,128)(2,1)S(1)}) custom-call(s32[2]{0:T(128)S(1)} %pad_add_fusion.place_ref, bf16[256,32,256]{2,1,0:T(8,128)(2,1)} %bitcast.2.box_ref, bf16[6,256,256]{2,1,0:T(8,128)(2,1)S(1)} %assemble.1.refs_0_.blocks_ref.refs_4_, ...), custom_call_target="tpu_custom_call" | custom-call | flops 1073741824 | bytes 4194304 | tf_op jit(solution)/shard_map/gram/pallas_call | solution.py:122
  114.6 1.4 collective-permute-start.4
  116.0 1.9 %collective-permute-start.5 = (bf16[832,256]{1,0:T(8,128)(2,1)S(1)}, bf16[832,256]{1,0:T(8,128)(2,1)S(1)}, u32[]{:S(2)}, u32[]{:S(2)}) collective-permute-start(bf16[832,256]{1,0:T(8,128)(2,1)S(1)} %get-tuple-element.13), channel_id=1, source_target_pairs={{0,3},{1,2},{2,1},{3,0},{4,7},{5,6},{6,5},{7,4},{8,11},{9,10},{10,... | collective-permute-start | bytes 1277960 | tf_op jit(solution)/shard_map/ppermute | solution.py:438
  117.9 0.6 outward.2
  118.6 1.0 collective-permute-start.9
  119.6 7.0 %ham_inner.1 = (f32[256,256]{1,0:T(8,128)S(1)}, bf16[2,256,1024]{2,1,0:T(8,128)(2,1)S(1)}) custom-call(bf16[256,256]{1,0:T(8,128)(2,1)S(1)} %copy-done.1, bf16[256,32,256]{2,1,0:T(8,128)(2,1)} %bitcast.2.box_ref, f32[32,256]{1,0:T(8,128)S(1)} %bitcast.12), custom_call_target="tpu_custom_call" | custom-call | flops 2147483648 | bytes 4194304 | tf_op jit(solution)/shard_map/ham_inner/pallas_call | solution.py:172
  126.6 5.5 %collective-permute-done.9.across_ref = f32[160,256]{1,0:T(8,128)S(1)} collective-permute-done((f32[160,256]{1,0:T(8,128)S(1)}, f32[160,256]{1,0:T(8,128)S(1)}, u32[]{:S(2)}, u32[]{:S(2)}) %collective-permute-start.9) | collective-permute-done | bytes 163872 | tf_op jit(solution)/shard_map/ppermute | solution.py:438
  132.2 0.5 collective-permute-start.12
  132.7 1.0 collective-permute-start.13
  133.6 1.4 ham_outer.1
  135.1 2.8 %collective-permute-start.7 = (f32[64,256]{1,0:T(8,128)S(1)}, f32[64,256]{1,0:T(8,128)S(1)}, u32[]{:S(2)}, u32[]{:S(2)}) collective-permute-start(f32[64,256]{1,0:T(8,128)S(1)} %get-tuple-element.17), channel_id=1, source_target_pairs={{0,2},{1,3},{2,0},{3,1},{4,6},{5,7},{6,4},{7,5},{8,10},{9,11},{10,... | collective-permute-start | bytes 196616 | tf_op jit(solution)/shard_map/ppermute | solution.py:438
  137.9 1.1 collective-permute-start.8
  139.0 1.6 %collective-permute-done.7.refs_2_ = f32[64,256]{1,0:T(8,128)S(1)} collective-permute-done((f32[64,256]{1,0:T(8,128)S(1)}, f32[64,256]{1,0:T(8,128)S(1)}, u32[]{:S(2)}, u32[]{:S(2)}) %collective-permute-start.7) | collective-permute-done | bytes 65568 | tf_op jit(solution)/shard_map/ppermute | solution.py:438
  140.6 1.7 %collective-permute-done.8.refs_3_ = f32[64,256]{1,0:T(8,128)S(1)} collective-permute-done((f32[64,256]{1,0:T(8,128)S(1)}, f32[64,256]{1,0:T(8,128)S(1)}, u32[]{:S(2)}, u32[]{:S(2)}) %collective-permute-start.8) | collective-permute-done | bytes 65568 | tf_op jit(solution)/shard_map/ppermute | solution.py:438
  142.2 0.6 pick.1.refs_4_
  142.8 4.3 %collective-permute-start.14 = (f32[2,160,256]{2,1,0:T(8,128)S(1)}, f32[2,160,256]{2,1,0:T(8,128)S(1)}, u32[]{:S(2)}, u32[]{:S(2)}) collective-permute-start(f32[2,160,256]{2,1,0:T(8,128)S(1)} %pick.1.refs_4_), channel_id=1, source_target_pairs={{0,4},{4,0},{8,12},{12,8},{16,20},{20,16},{24,28},{28,24},{32,36},... | collective-permute-start | bytes 983048 | tf_op jit(solution)/shard_map/ppermute | solution.py:438
  147.1 0.6 outward.3
  147.7 0.1 collective-permute-start.15
  147.8 1.2 finish.1
  149.0 0.3 collective-permute-done.15.refs_8_
  149.3 2.9 %purify.1 = f32[3,64,256]{2,1,0:T(8,128)} custom-call(s32[2]{0:T(128)S(1)} %pad_add_fusion.place_ref, s32[64]{0:T(128)S(1)} %copy-done.3, s32[64]{0:T(128)S(1)} %copy-done.4, s32[64]{0:T(128)S(1)} %copy-done.5, f32[3,64,256]{2,1,0:T(8,128)S(1)} %bitcast.11, f32[160,256]{1,0:T(8,128)S(1)} %total.1.own_ref.refs_0_, ...), custom_call_target="tpu_custom_call" | custom-call | tf_op jit(solution)/shard_map/purify/pallas_call | solution.py:426
  (25 shorter events, 0.4 us)
Async XLA Ops:
  0.6 13.3 %copy-start = (f32[1,3,64,256]{3,2,1,0:T(8,128)S(1)}, f32[1,3,64,256]{3,2,1,0:T(8,128)}, u32[]{:S(2)}) copy-start(f32[1,3,64,256]{3,2,1,0:T(8,128)} %param.10) | copy-start | bytes 589828
  0.6 109.6 %all-to-all-start = ((bf16[64,4,32,256]{3,2,1,0:T(8,128)(2,1)}), bf16[64,4,32,256]{3,2,1,0:T(8,128)(2,1)}, u32[]{:S(2)}, u32[]{:S(2)}) async-start(bf16[64,4,32,256]{3,2,1,0:T(8,128)(2,1)} %param.8), calls=%async_computation | async-start | bytes 8388608 | tf_op jit(solution)/shard_map/all_to_all | solution.py:463
  14.0 6.1 %collective-permute-start = (f32[3,64,256]{2,1,0:T(8,128)S(1)}, f32[3,64,256]{2,1,0:T(8,128)S(1)}, u32[]{:S(2)}, u32[]{:S(2)}) collective-permute-start(f32[3,64,256]{2,1,0:T(8,128)S(1)} %bitcast.7), channel_id=1, source_target_pairs={{0,1},{1,0},{2,3},{3,2},{4,5},{5,4},{6,7},{7,6},{8,9},{9,8},{10,11... | collective-permute-start | bytes 589832 | tf_op jit(solution)/shard_map/ppermute | solution.py:438
  15.4 11.5 %collective-permute-start.1 = (f32[3,64,256]{2,1,0:T(8,128)S(1)}, f32[3,64,256]{2,1,0:T(8,128)S(1)}, u32[]{:S(2)}, u32[]{:S(2)}) collective-permute-start(f32[3,64,256]{2,1,0:T(8,128)S(1)} %bitcast.8), channel_id=1, source_target_pairs={{0,2},{1,3},{2,0},{3,1},{4,6},{5,7},{6,4},{7,5},{8,10},{9,11},{10,... | collective-permute-start | bytes 589832 | tf_op jit(solution)/shard_map/ppermute | solution.py:438
  18.0 11.3 %collective-permute-start.2 = (f32[3,64,256]{2,1,0:T(8,128)S(1)}, f32[3,64,256]{2,1,0:T(8,128)S(1)}, u32[]{:S(2)}, u32[]{:S(2)}) collective-permute-start(f32[3,64,256]{2,1,0:T(8,128)S(1)} %bitcast.9), channel_id=1, source_target_pairs={{0,3},{1,2},{2,1},{3,0},{4,7},{5,6},{6,5},{7,4},{8,11},{9,10},{10,... | collective-permute-start | bytes 589832 | tf_op jit(solution)/shard_map/ppermute | solution.py:438
  18.1 101.5 %copy-start.1 = (bf16[256,256]{1,0:T(8,128)(2,1)S(1)}, bf16[256,256]{1,0:T(8,128)(2,1)}, u32[]{:S(2)}) copy-start(bf16[256,256]{1,0:T(8,128)(2,1)} %constant.11.clone.weights_ref) | copy-start | bytes 393220
  18.1 101.5 %copy-start.2 = (f32[1,32,256]{2,1,0:T(8,128)S(1)}, f32[1,32,256]{2,1,0:T(8,128)}, u32[]{:S(2)}) copy-start(f32[1,32,256]{2,1,0:T(8,128)} %param.9) | copy-start | bytes 98308
  30.0 3.4 %collective-permute-start.3 = (bf16[6,256,256]{2,1,0:T(8,128)(2,1)S(1)}, bf16[6,256,256]{2,1,0:T(8,128)(2,1)S(1)}, u32[]{:S(2)}, u32[]{:S(2)}) collective-permute-start(bf16[6,256,256]{2,1,0:T(8,128)(2,1)S(1)} %assemble.1.refs_0_.blocks_ref.refs_4_), channel_id=1, source_target_pairs={{0,4},{4,0},{8,12},{12,8},{16,20},{20,16},{24,28},{28,24},{32,36},... | collective-permute-start | bytes 2359304 | tf_op jit(solution)/shard_map/ppermute | solution.py:438
  31.4 95.1 %collective-permute-start.10 = (bf16[6,256,256]{2,1,0:T(8,128)(2,1)S(1)}, bf16[6,256,256]{2,1,0:T(8,128)(2,1)S(1)}, u32[]{:S(2)}, u32[]{:S(2)}) collective-permute-start(bf16[6,256,256]{2,1,0:T(8,128)(2,1)S(1)} %assemble.1.refs_0_.blocks_ref.refs_4_), channel_id=1, source_target_pairs={{0,252},{4,8},{8,4},{12,16},{16,12},{20,24},{24,20},{28,32},{32,28... | collective-permute-start | bytes 2359304 | tf_op jit(solution)/shard_map/ppermute | solution.py:438
  114.6 17.5 %collective-permute-start.4 = (bf16[832,256]{1,0:T(8,128)(2,1)S(1)}, bf16[832,256]{1,0:T(8,128)(2,1)S(1)}, u32[]{:S(2)}, u32[]{:S(2)}) collective-permute-start(bf16[832,256]{1,0:T(8,128)(2,1)S(1)} %get-tuple-element.12), channel_id=1, source_target_pairs={{0,1},{1,0},{2,3},{3,2},{4,5},{5,4},{6,7},{7,6},{8,9},{9,8},{10,11... | collective-permute-start | bytes 1277960 | tf_op jit(solution)/shard_map/ppermute | solution.py:438
  116.0 16.1 %collective-permute-start.5 = (bf16[832,256]{1,0:T(8,128)(2,1)S(1)}, bf16[832,256]{1,0:T(8,128)(2,1)S(1)}, u32[]{:S(2)}, u32[]{:S(2)}) collective-permute-start(bf16[832,256]{1,0:T(8,128)(2,1)S(1)} %get-tuple-element.13), channel_id=1, source_target_pairs={{0,3},{1,2},{2,1},{3,0},{4,7},{5,6},{6,5},{7,4},{8,11},{9,10},{10,... | collective-permute-start | bytes 1277960 | tf_op jit(solution)/shard_map/ppermute | solution.py:438
  118.5 8.1 %collective-permute-start.11 = (bf16[2,256,256]{2,1,0:T(8,128)(2,1)S(1)}, bf16[2,256,256]{2,1,0:T(8,128)(2,1)S(1)}, u32[]{:S(2)}, u32[]{:S(2)}) collective-permute-start(bf16[2,256,256]{2,1,0:T(8,128)(2,1)S(1)} %outward.2), channel_id=1, source_target_pairs={{0,8},{4,252},{8,16},{12,4},{16,24},{20,12},{24,32},{28,20},{32,40... | collective-permute-start | bytes 786440 | tf_op jit(solution)/shard_map/ppermute | solution.py:470
  118.6 13.6 %collective-permute-start.9 = (f32[160,256]{1,0:T(8,128)S(1)}, f32[160,256]{1,0:T(8,128)S(1)}, u32[]{:S(2)}, u32[]{:S(2)}) collective-permute-start(f32[160,256]{1,0:T(8,128)S(1)} %get-tuple-element.19.own_ref), channel_id=1, source_target_pairs={{0,2},{1,3},{2,0},{3,1},{4,6},{5,7},{6,4},{7,5},{8,10},{9,11},{10,... | collective-permute-start | bytes 491528 | tf_op jit(solution)/shard_map/ppermute | solution.py:438
  126.5 21.3 %copy-start.3 = (s32[64]{0:T(128)S(1)}, s32[64]{0:T(128)}, u32[]{:S(2)}) copy-start(s32[64]{0:T(128)} %count_ref.3) | copy-start | bytes 772
  126.5 21.3 %copy-start.4 = (s32[64]{0:T(128)S(1)}, s32[64]{0:T(128)}, u32[]{:S(2)}) copy-start(s32[64]{0:T(128)} %rotation_ref.3) | copy-start | bytes 772
  126.5 22.8 %copy-start.5 = (s32[64]{0:T(128)S(1)}, s32[64]{0:T(128)}, u32[]{:S(2)}) copy-start(s32[64]{0:T(128)} %bond_ref.1) | copy-start | bytes 772
  132.2 10.1 %collective-permute-start.12 = (f32[160,256]{1,0:T(8,128)S(1)}, f32[160,256]{1,0:T(8,128)S(1)}, u32[]{:S(2)}, u32[]{:S(2)}) collective-permute-start(f32[160,256]{1,0:T(8,128)S(1)} %total.1.own_ref.refs_0_), channel_id=1, source_target_pairs={{0,8},{4,12},{8,0},{12,4},{16,24},{20,28},{24,16},{28,20},{32,40},... | collective-permute-start | bytes 491528 | tf_op jit(solution)/shard_map/ppermute | solution.py:438
  132.7 9.6 %collective-permute-start.13 = (f32[160,256]{1,0:T(8,128)S(1)}, f32[160,256]{1,0:T(8,128)S(1)}, u32[]{:S(2)}, u32[]{:S(2)}) collective-permute-start(f32[160,256]{1,0:T(8,128)S(1)} %total.1.own_ref.refs_0_), channel_id=1, source_target_pairs={{0,248},{4,252},{8,16},{12,20},{16,8},{20,12},{24,32},{28,36},{32,... | collective-permute-start | bytes 491528 | tf_op jit(solution)/shard_map/ppermute | solution.py:438
  135.0 3.9 %collective-permute-start.6 = (f32[64,256]{1,0:T(8,128)S(1)}, f32[64,256]{1,0:T(8,128)S(1)}, u32[]{:S(2)}, u32[]{:S(2)}) collective-permute-start(f32[64,256]{1,0:T(8,128)S(1)} %get-tuple-element.16), channel_id=1, source_target_pairs={{0,1},{1,0},{2,3},{3,2},{4,5},{5,4},{6,7},{7,6},{8,9},{9,8},{10,11... | collective-permute-start | bytes 196616 | tf_op jit(solution)/shard_map/ppermute | solution.py:438
  135.1 5.4 %collective-permute-start.7 = (f32[64,256]{1,0:T(8,128)S(1)}, f32[64,256]{1,0:T(8,128)S(1)}, u32[]{:S(2)}, u32[]{:S(2)}) collective-permute-start(f32[64,256]{1,0:T(8,128)S(1)} %get-tuple-element.17), channel_id=1, source_target_pairs={{0,2},{1,3},{2,0},{3,1},{4,6},{5,7},{6,4},{7,5},{8,10},{9,11},{10,... | collective-permute-start | bytes 196616 | tf_op jit(solution)/shard_map/ppermute | solution.py:438
  137.9 4.3 %collective-permute-start.8 = (f32[64,256]{1,0:T(8,128)S(1)}, f32[64,256]{1,0:T(8,128)S(1)}, u32[]{:S(2)}, u32[]{:S(2)}) collective-permute-start(f32[64,256]{1,0:T(8,128)S(1)} %get-tuple-element.18), channel_id=1, source_target_pairs={{0,3},{1,2},{2,1},{3,0},{4,7},{5,6},{6,5},{7,4},{8,11},{9,10},{10,... | collective-permute-start | bytes 196616 | tf_op jit(solution)/shard_map/ppermute | solution.py:438
  142.8 6.5 %collective-permute-start.14 = (f32[2,160,256]{2,1,0:T(8,128)S(1)}, f32[2,160,256]{2,1,0:T(8,128)S(1)}, u32[]{:S(2)}, u32[]{:S(2)}) collective-permute-start(f32[2,160,256]{2,1,0:T(8,128)S(1)} %pick.1.refs_4_), channel_id=1, source_target_pairs={{0,4},{4,0},{8,12},{12,8},{16,20},{20,16},{24,28},{28,24},{32,36},... | collective-permute-start | bytes 983048 | tf_op jit(solution)/shard_map/ppermute | solution.py:438
  147.7 1.6 %collective-permute-start.15 = (bf16[2,256,256]{2,1,0:T(8,128)(2,1)S(1)}, bf16[2,256,256]{2,1,0:T(8,128)(2,1)S(1)}, u32[]{:S(2)}, u32[]{:S(2)}) collective-permute-start(bf16[2,256,256]{2,1,0:T(8,128)(2,1)S(1)} %outward.3), channel_id=1, source_target_pairs={{0,4},{4,0},{8,12},{12,8},{16,20},{20,16},{24,28},{28,24},{32,36},... | collective-permute-start | bytes 786440 | tf_op jit(solution)/shard_map/ppermute | solution.py:438

commit v5 on v4

--- a/solution.py
+++ b/solution.py
@@ -473,13 +473,14 @@
     opposite = swapped(share, "kern", along_kern[2])
     near, far = swapped(near, "kern", along_kern[1]), swapped(far, "kern", along_kern[3])
     inner, rims = ham_inner(boxes, potential[0])
-    inter = total(share, opposite, near, far, (inner, cross, beyond))
-    behind = swapped(outward(place, cross, (inter,)), "atoms", same_chip)
+    slabs = ham_outer(place, inner, near, far, rims, potential[0], kern_count)
+    inter = total(share, opposite, near, far, (slabs[0], cross, beyond))
+    sent = outward(place, cross, (inter,))
+    behind = swapped(sent, "atoms", same_chip)
 
     two_even, two_odd = swapped(inter, "atoms", even_chip_with_next), swapped(inter, "atoms", odd_chip_with_next)
-    slabs = ham_outer(place, inner, near, far, rims, potential[0], kern_count)
     parts = [slabs[0]] + [swapped(part, "kern", partner) for part, partner in zip(slabs[1:], along_kern[1:])]
-    picked = pick(place, inter, two_even, two_odd, parts)
+    picked = pick(place, inter, two_even, two_odd, (sent, *parts[:-1]))
     from_core = swapped(picked, "atoms", same_chip)
     ham_mine = finish(place, live_count, rotation, parts, (picked,))
     overlaps = [inter, from_core, two_even, two_odd]

time: 152 us -> 153 us (level)
  transfers between devices with their start and end apart: 17 -> 17, of which waited for: 9 -> 10; matrix products, arithmetic and copies ran while one was open for 0% -> 0% of each run, Pallas kernels for 10% -> 10%
where the time goes in v5:
time: 153 us
  waiting for transfers between devices  97.8 us (64%)
  starting transfers between devices  35.2 us (23%)
  Pallas kernels  19.3 us (13%)
    all_to_all x1, waiting for transfers between devices, shards(): got = lax.all_to_all(psi, 'atoms', split_axis=0, concat_axis=0, tiled=True)  76.8 us
    ppermute x15, starting transfers between devices, swapped(): lax.ppermute(block, axis, [(at, partner(at) % count) for at in range(coun...  21.8 us
    ppermute x15, waiting for transfers between devices, swapped(): lax.ppermute(block, axis, [(at, partner(at) % count) for at in range(coun...  20.9 us
    all_to_all x1, starting transfers between devices, shards(): got = lax.all_to_all(psi, 'atoms', split_axis=0, concat_axis=0, tiled=True)  13.3 us
    pallas_call x1, Pallas kernels, ham_inner(): pl.pallas_call(inner_kernel, grid=(depth // GROUP,), out_shape=[jax.Shape...  6.96 us
    pallas_call x1, Pallas kernels, gram(): pl.pallas_call(gram_kernel, grid=(depth // GROUP,), in_specs=[pl.BlockSpe...  4.41 us
  transfers between devices with their start and end apart: 17, of which 10 were waited for; matrix products, arithmetic and copies ran while one was open for 0% of the time, Pallas kernels for 10%

profile of v5, /device:TPU:1, one launch (start us, length us, event | category | flops | bytes accessed | tf_op | source)
XLA Modules:
  0.0 153.1 jit_solution(9812802153895796833)
XLA Ops:
  0.6 13.3 %all-to-all-start = ((bf16[64,4,32,256]{3,2,1,0:T(8,128)(2,1)}), bf16[64,4,32,256]{3,2,1,0:T(8,128)(2,1)}, u32[]{:S(2)}, u32[]{:S(2)}) async-start(bf16[64,4,32,256]{3,2,1,0:T(8,128)(2,1)} %param.8), calls=%async_computation | async-start | bytes 8388608 | tf_op jit(solution)/shard_map/all_to_all | solution.py:463
  14.0 1.4 collective-permute-start
  15.4 2.6 %collective-permute-start.1 = (f32[3,64,256]{2,1,0:T(8,128)S(1)}, f32[3,64,256]{2,1,0:T(8,128)S(1)}, u32[]{:S(2)}, u32[]{:S(2)}) collective-permute-start(f32[3,64,256]{2,1,0:T(8,128)S(1)} %bitcast.8), channel_id=1, source_target_pairs={{0,2},{1,3},{2,0},{3,1},{4,6},{5,7},{6,4},{7,5},{8,10},{9,11},{10,... | collective-permute-start | bytes 589832 | tf_op jit(solution)/shard_map/ppermute | solution.py:438
  18.1 2.0 %collective-permute-done.refs_1_ = f32[3,64,256]{2,1,0:T(8,128)S(1)} collective-permute-done((f32[3,64,256]{2,1,0:T(8,128)S(1)}, f32[3,64,256]{2,1,0:T(8,128)S(1)}, u32[]{:S(2)}, u32[]{:S(2)}) %collective-permute-start) | collective-permute-done | bytes 196640 | tf_op jit(solution)/shard_map/ppermute | solution.py:438
  20.1 6.7 %collective-permute-done.1.refs_2_ = f32[3,64,256]{2,1,0:T(8,128)S(1)} collective-permute-done((f32[3,64,256]{2,1,0:T(8,128)S(1)}, f32[3,64,256]{2,1,0:T(8,128)S(1)}, u32[]{:S(2)}, u32[]{:S(2)}) %collective-permute-start.1) | collective-permute-done | bytes 196640 | tf_op jit(solution)/shard_map/ppermute | solution.py:438
  26.8 2.5 %collective-permute-done.2.refs_3_ = f32[3,64,256]{2,1,0:T(8,128)S(1)} collective-permute-done((f32[3,64,256]{2,1,0:T(8,128)S(1)}, f32[3,64,256]{2,1,0:T(8,128)S(1)}, u32[]{:S(2)}, u32[]{:S(2)}) %collective-permute-start.2) | collective-permute-done | bytes 196640 | tf_op jit(solution)/shard_map/ppermute | solution.py:438
  29.3 0.6 assemble.1.refs_0_.blocks_ref.refs_4_
  30.0 1.5 collective-permute-start.3
  31.4 1.4 collective-permute-start.10
  32.8 0.5 collective-permute-done.3.refs_1_.refs_5_
  33.4 76.8 %all-to-all-done = bf16[64,4,32,256]{3,2,1,0:T(8,128)(2,1)} async-done(((bf16[64,4,32,256]{3,2,1,0:T(8,128)(2,1)}), bf16[64,4,32,256]{3,2,1,0:T(8,128)(2,1)}, u32[]{:S(2)}, u32[]{:S(2)}) %all-to-all-start) | async-done | bytes 4194336 | tf_op jit(solution)/shard_map/all_to_all | solution.py:463
  110.2 4.4 %gram.1 = (f32[160,256]{1,0:T(8,128)S(1)}, bf16[832,256]{1,0:T(8,128)(2,1)S(1)}, bf16[832,256]{1,0:T(8,128)(2,1)S(1)}) custom-call(s32[2]{0:T(128)S(1)} %pad_add_fusion.place_ref, bf16[256,32,256]{2,1,0:T(8,128)(2,1)} %bitcast.2.box_ref, bf16[6,256,256]{2,1,0:T(8,128)(2,1)S(1)} %assemble.1.refs_0_.blocks_ref.refs_4_, ...), custom_call_target="tpu_custom_call" | custom-call | flops 1073741824 | bytes 4194304 | tf_op jit(solution)/shard_map/gram/pallas_call | solution.py:122
  114.6 1.4 collective-permute-start.4
  116.0 1.9 %collective-permute-start.5 = (bf16[832,256]{1,0:T(8,128)(2,1)S(1)}, bf16[832,256]{1,0:T(8,128)(2,1)S(1)}, u32[]{:S(2)}, u32[]{:S(2)}) collective-permute-start(bf16[832,256]{1,0:T(8,128)(2,1)S(1)} %get-tuple-element.13), channel_id=1, source_target_pairs={{0,3},{1,2},{2,1},{3,0},{4,7},{5,6},{6,5},{7,4},{8,11},{9,10},{10,... | collective-permute-start | bytes 1277960 | tf_op jit(solution)/shard_map/ppermute | solution.py:438
  117.9 0.6 outward.2
  118.6 1.0 collective-permute-start.9
  119.6 7.0 %ham_inner.1 = (f32[256,256]{1,0:T(8,128)S(1)}, bf16[2,256,1024]{2,1,0:T(8,128)(2,1)S(1)}) custom-call(bf16[256,256]{1,0:T(8,128)(2,1)S(1)} %copy-done.1, bf16[256,32,256]{2,1,0:T(8,128)(2,1)} %bitcast.2.box_ref, f32[32,256]{1,0:T(8,128)S(1)} %bitcast.12), custom_call_target="tpu_custom_call" | custom-call | flops 2147483648 | bytes 4194304 | tf_op jit(solution)/shard_map/ham_inner/pallas_call | solution.py:172
  126.6 3.6 %collective-permute-done.5.far_ref = bf16[832,256]{1,0:T(8,128)(2,1)S(1)} collective-permute-done((bf16[832,256]{1,0:T(8,128)(2,1)S(1)}, bf16[832,256]{1,0:T(8,128)(2,1)S(1)}, u32[]{:S(2)}, u32[]{:S(2)}) %collective-permute-start.5) | collective-permute-done | bytes 426016 | tf_op jit(solution)/shard_map/ppermute | solution.py:438
  130.2 1.4 ham_outer.1
  131.6 0.5 collective-permute-done.9.across_ref
  132.2 0.5 collective-permute-start.12
  132.6 1.0 collective-permute-start.13
  133.6 4.2 %collective-permute-start.7 = (f32[64,256]{1,0:T(8,128)S(1)}, f32[64,256]{1,0:T(8,128)S(1)}, u32[]{:S(2)}, u32[]{:S(2)}) collective-permute-start(f32[64,256]{1,0:T(8,128)S(1)} %get-tuple-element.17), channel_id=1, source_target_pairs={{0,2},{1,3},{2,0},{3,1},{4,6},{5,7},{6,4},{7,5},{8,10},{9,11},{10,... | collective-permute-start | bytes 196616 | tf_op jit(solution)/shard_map/ppermute | solution.py:438
  137.9 0.6 outward.3.refs_0_
  138.4 2.1 %collective-permute-done.7.refs_3_.refs_2_ = f32[64,256]{1,0:T(8,128)S(1)} collective-permute-done((f32[64,256]{1,0:T(8,128)S(1)}, f32[64,256]{1,0:T(8,128)S(1)}, u32[]{:S(2)}, u32[]{:S(2)}) %collective-permute-start.7) | collective-permute-done | bytes 65568 | tf_op jit(solution)/shard_map/ppermute | solution.py:438
  140.5 0.4 collective-permute-done.13.odd_ref.refs_3_
  140.9 0.6 pick.1.refs_4_
  141.5 3.0 %collective-permute-start.14 = (f32[2,160,256]{2,1,0:T(8,128)S(1)}, f32[2,160,256]{2,1,0:T(8,128)S(1)}, u32[]{:S(2)}, u32[]{:S(2)}) collective-permute-start(f32[2,160,256]{2,1,0:T(8,128)S(1)} %pick.1.refs_4_), channel_id=1, source_target_pairs={{0,4},{4,0},{8,12},{12,8},{16,20},{20,16},{24,28},{28,24},{32,36},... | collective-permute-start | bytes 983048 | tf_op jit(solution)/shard_map/ppermute | solution.py:438
  144.6 1.8 %collective-permute-start.8 = (f32[64,256]{1,0:T(8,128)S(1)}, f32[64,256]{1,0:T(8,128)S(1)}, u32[]{:S(2)}, u32[]{:S(2)}) collective-permute-start(f32[64,256]{1,0:T(8,128)S(1)} %get-tuple-element.18), channel_id=1, source_target_pairs={{0,3},{1,2},{2,1},{3,0},{4,7},{5,6},{6,5},{7,4},{8,11},{9,10},{10,... | collective-permute-start | bytes 196616 | tf_op jit(solution)/shard_map/ppermute | solution.py:438
  146.5 2.5 %collective-permute-done.8.refs_3_ = f32[64,256]{1,0:T(8,128)S(1)} collective-permute-done((f32[64,256]{1,0:T(8,128)S(1)}, f32[64,256]{1,0:T(8,128)S(1)}, u32[]{:S(2)}, u32[]{:S(2)}) %collective-permute-start.8) | collective-permute-done | bytes 65568 | tf_op jit(solution)/shard_map/ppermute | solution.py:438
  149.0 1.2 finish.1
  150.2 2.9 %purify.1 = f32[3,64,256]{2,1,0:T(8,128)} custom-call(s32[2]{0:T(128)S(1)} %pad_add_fusion.place_ref, s32[64]{0:T(128)S(1)} %copy-done.3, s32[64]{0:T(128)S(1)} %copy-done.4, s32[64]{0:T(128)S(1)} %copy-done.5, f32[3,64,256]{2,1,0:T(8,128)S(1)} %bitcast.11, f32[160,256]{1,0:T(8,128)S(1)} %total.1.refs_0_.own_ref, ...), custom_call_target="tpu_custom_call" | custom-call | tf_op jit(solution)/shard_map/purify/pallas_call | solution.py:426
  (25 shorter events, 0.4 us)
Async XLA Ops:
  0.6 13.3 %copy-start = (f32[1,3,64,256]{3,2,1,0:T(8,128)S(1)}, f32[1,3,64,256]{3,2,1,0:T(8,128)}, u32[]{:S(2)}) copy-start(f32[1,3,64,256]{3,2,1,0:T(8,128)} %param.10) | copy-start | bytes 589828
  0.6 109.6 %all-to-all-start = ((bf16[64,4,32,256]{3,2,1,0:T(8,128)(2,1)}), bf16[64,4,32,256]{3,2,1,0:T(8,128)(2,1)}, u32[]{:S(2)}, u32[]{:S(2)}) async-start(bf16[64,4,32,256]{3,2,1,0:T(8,128)(2,1)} %param.8), calls=%async_computation | async-start | bytes 8388608 | tf_op jit(solution)/shard_map/all_to_all | solution.py:463
  14.0 6.1 %collective-permute-start = (f32[3,64,256]{2,1,0:T(8,128)S(1)}, f32[3,64,256]{2,1,0:T(8,128)S(1)}, u32[]{:S(2)}, u32[]{:S(2)}) collective-permute-start(f32[3,64,256]{2,1,0:T(8,128)S(1)} %bitcast.7), channel_id=1, source_target_pairs={{0,1},{1,0},{2,3},{3,2},{4,5},{5,4},{6,7},{7,6},{8,9},{9,8},{10,11... | collective-permute-start | bytes 589832 | tf_op jit(solution)/shard_map/ppermute | solution.py:438
  15.4 11.5 %collective-permute-start.1 = (f32[3,64,256]{2,1,0:T(8,128)S(1)}, f32[3,64,256]{2,1,0:T(8,128)S(1)}, u32[]{:S(2)}, u32[]{:S(2)}) collective-permute-start(f32[3,64,256]{2,1,0:T(8,128)S(1)} %bitcast.8), channel_id=1, source_target_pairs={{0,2},{1,3},{2,0},{3,1},{4,6},{5,7},{6,4},{7,5},{8,10},{9,11},{10,... | collective-permute-start | bytes 589832 | tf_op jit(solution)/shard_map/ppermute | solution.py:438
  18.0 11.3 %collective-permute-start.2 = (f32[3,64,256]{2,1,0:T(8,128)S(1)}, f32[3,64,256]{2,1,0:T(8,128)S(1)}, u32[]{:S(2)}, u32[]{:S(2)}) collective-permute-start(f32[3,64,256]{2,1,0:T(8,128)S(1)} %bitcast.9), channel_id=1, source_target_pairs={{0,3},{1,2},{2,1},{3,0},{4,7},{5,6},{6,5},{7,4},{8,11},{9,10},{10,... | collective-permute-start | bytes 589832 | tf_op jit(solution)/shard_map/ppermute | solution.py:438
  18.1 101.5 %copy-start.1 = (bf16[256,256]{1,0:T(8,128)(2,1)S(1)}, bf16[256,256]{1,0:T(8,128)(2,1)}, u32[]{:S(2)}) copy-start(bf16[256,256]{1,0:T(8,128)(2,1)} %constant.11.clone.weights_ref) | copy-start | bytes 393220
  18.1 101.5 %copy-start.2 = (f32[1,32,256]{2,1,0:T(8,128)S(1)}, f32[1,32,256]{2,1,0:T(8,128)}, u32[]{:S(2)}) copy-start(f32[1,32,256]{2,1,0:T(8,128)} %param.9) | copy-start | bytes 98308
  30.0 3.4 %collective-permute-start.3 = (bf16[6,256,256]{2,1,0:T(8,128)(2,1)S(1)}, bf16[6,256,256]{2,1,0:T(8,128)(2,1)S(1)}, u32[]{:S(2)}, u32[]{:S(2)}) collective-permute-start(bf16[6,256,256]{2,1,0:T(8,128)(2,1)S(1)} %assemble.1.refs_0_.blocks_ref.refs_4_), channel_id=1, source_target_pairs={{0,4},{4,0},{8,12},{12,8},{16,20},{20,16},{24,28},{28,24},{32,36},... | collective-permute-start | bytes 2359304 | tf_op jit(solution)/shard_map/ppermute | solution.py:438
  31.4 100.2 %collective-permute-start.10 = (bf16[6,256,256]{2,1,0:T(8,128)(2,1)S(1)}, bf16[6,256,256]{2,1,0:T(8,128)(2,1)S(1)}, u32[]{:S(2)}, u32[]{:S(2)}) collective-permute-start(bf16[6,256,256]{2,1,0:T(8,128)(2,1)S(1)} %assemble.1.refs_0_.blocks_ref.refs_4_), channel_id=1, source_target_pairs={{0,252},{4,8},{8,4},{12,16},{16,12},{20,24},{24,20},{28,32},{32,28... | collective-permute-start | bytes 2359304 | tf_op jit(solution)/shard_map/ppermute | solution.py:438
  114.6 11.9 %collective-permute-start.4 = (bf16[832,256]{1,0:T(8,128)(2,1)S(1)}, bf16[832,256]{1,0:T(8,128)(2,1)S(1)}, u32[]{:S(2)}, u32[]{:S(2)}) collective-permute-start(bf16[832,256]{1,0:T(8,128)(2,1)S(1)} %get-tuple-element.12), channel_id=1, source_target_pairs={{0,1},{1,0},{2,3},{3,2},{4,5},{5,4},{6,7},{7,6},{8,9},{9,8},{10,11... | collective-permute-start | bytes 1277960 | tf_op jit(solution)/shard_map/ppermute | solution.py:438
  116.0 14.2 %collective-permute-start.5 = (bf16[832,256]{1,0:T(8,128)(2,1)S(1)}, bf16[832,256]{1,0:T(8,128)(2,1)S(1)}, u32[]{:S(2)}, u32[]{:S(2)}) collective-permute-start(bf16[832,256]{1,0:T(8,128)(2,1)S(1)} %get-tuple-element.13), channel_id=1, source_target_pairs={{0,3},{1,2},{2,1},{3,0},{4,7},{5,6},{6,5},{7,4},{8,11},{9,10},{10,... | collective-permute-start | bytes 1277960 | tf_op jit(solution)/shard_map/ppermute | solution.py:438
  118.5 13.1 %collective-permute-start.11 = (bf16[2,256,256]{2,1,0:T(8,128)(2,1)S(1)}, bf16[2,256,256]{2,1,0:T(8,128)(2,1)S(1)}, u32[]{:S(2)}, u32[]{:S(2)}) collective-permute-start(bf16[2,256,256]{2,1,0:T(8,128)(2,1)S(1)} %outward.2), channel_id=1, source_target_pairs={{0,8},{4,252},{8,16},{12,4},{16,24},{20,12},{24,32},{28,20},{32,40... | collective-permute-start | bytes 786440 | tf_op jit(solution)/shard_map/ppermute | solution.py:470
  118.6 13.6 %collective-permute-start.9 = (f32[160,256]{1,0:T(8,128)S(1)}, f32[160,256]{1,0:T(8,128)S(1)}, u32[]{:S(2)}, u32[]{:S(2)}) collective-permute-start(f32[160,256]{1,0:T(8,128)S(1)} %get-tuple-element.19.own_ref), channel_id=1, source_target_pairs={{0,2},{1,3},{2,0},{3,1},{4,6},{5,7},{6,4},{7,5},{8,10},{9,11},{10,... | collective-permute-start | bytes 491528 | tf_op jit(solution)/shard_map/ppermute | solution.py:438
  126.5 22.4 %copy-start.3 = (s32[64]{0:T(128)S(1)}, s32[64]{0:T(128)}, u32[]{:S(2)}) copy-start(s32[64]{0:T(128)} %count_ref.3) | copy-start | bytes 772
  126.5 22.4 %copy-start.4 = (s32[64]{0:T(128)S(1)}, s32[64]{0:T(128)}, u32[]{:S(2)}) copy-start(s32[64]{0:T(128)} %rotation_ref.3) | copy-start | bytes 772
  126.5 23.7 %copy-start.5 = (s32[64]{0:T(128)S(1)}, s32[64]{0:T(128)}, u32[]{:S(2)}) copy-start(s32[64]{0:T(128)} %bond_ref.1) | copy-start | bytes 772
  132.2 8.3 %collective-permute-start.12 = (f32[160,256]{1,0:T(8,128)S(1)}, f32[160,256]{1,0:T(8,128)S(1)}, u32[]{:S(2)}, u32[]{:S(2)}) collective-permute-start(f32[160,256]{1,0:T(8,128)S(1)} %total.1.refs_0_.own_ref), channel_id=1, source_target_pairs={{0,8},{4,12},{8,0},{12,4},{16,24},{20,28},{24,16},{28,20},{32,40},... | collective-permute-start | bytes 491528 | tf_op jit(solution)/shard_map/ppermute | solution.py:438
  132.6 8.3 %collective-permute-start.13 = (f32[160,256]{1,0:T(8,128)S(1)}, f32[160,256]{1,0:T(8,128)S(1)}, u32[]{:S(2)}, u32[]{:S(2)}) collective-permute-start(f32[160,256]{1,0:T(8,128)S(1)} %total.1.refs_0_.own_ref), channel_id=1, source_target_pairs={{0,248},{4,252},{8,16},{12,20},{16,8},{20,12},{24,32},{28,36},{32,... | collective-permute-start | bytes 491528 | tf_op jit(solution)/shard_map/ppermute | solution.py:438
  133.6 4.8 %collective-permute-start.6 = (f32[64,256]{1,0:T(8,128)S(1)}, f32[64,256]{1,0:T(8,128)S(1)}, u32[]{:S(2)}, u32[]{:S(2)}) collective-permute-start(f32[64,256]{1,0:T(8,128)S(1)} %get-tuple-element.16), channel_id=1, source_target_pairs={{0,1},{1,0},{2,3},{3,2},{4,5},{5,4},{6,7},{7,6},{8,9},{9,8},{10,11... | collective-permute-start | bytes 196616 | tf_op jit(solution)/shard_map/ppermute | solution.py:438
  133.6 6.9 %collective-permute-start.7 = (f32[64,256]{1,0:T(8,128)S(1)}, f32[64,256]{1,0:T(8,128)S(1)}, u32[]{:S(2)}, u32[]{:S(2)}) collective-permute-start(f32[64,256]{1,0:T(8,128)S(1)} %get-tuple-element.17), channel_id=1, source_target_pairs={{0,2},{1,3},{2,0},{3,1},{4,6},{5,7},{6,4},{7,5},{8,10},{9,11},{10,... | collective-permute-start | bytes 196616 | tf_op jit(solution)/shard_map/ppermute | solution.py:438
  141.5 8.7 %collective-permute-start.14 = (f32[2,160,256]{2,1,0:T(8,128)S(1)}, f32[2,160,256]{2,1,0:T(8,128)S(1)}, u32[]{:S(2)}, u32[]{:S(2)}) collective-permute-start(f32[2,160,256]{2,1,0:T(8,128)S(1)} %pick.1.refs_4_), channel_id=1, source_target_pairs={{0,4},{4,0},{8,12},{12,8},{16,20},{20,16},{24,28},{28,24},{32,36},... | collective-permute-start | bytes 983048 | tf_op jit(solution)/shard_map/ppermute | solution.py:438
  144.5 5.7 %collective-permute-start.15 = (bf16[2,256,256]{2,1,0:T(8,128)(2,1)S(1)}, bf16[2,256,256]{2,1,0:T(8,128)(2,1)S(1)}, u32[]{:S(2)}, u32[]{:S(2)}) collective-permute-start(bf16[2,256,256]{2,1,0:T(8,128)(2,1)S(1)} %outward.3.refs_0_), channel_id=1, source_target_pairs={{0,4},{4,0},{8,12},{12,8},{16,20},{20,16},{24,28},{28,24},{32,36},... | collective-permute-start | bytes 786440 | tf_op jit(solution)/shard_map/ppermute | solution.py:438
  144.6 4.3 %collective-permute-start.8 = (f32[64,256]{1,0:T(8,128)S(1)}, f32[64,256]{1,0:T(8,128)S(1)}, u32[]{:S(2)}, u32[]{:S(2)}) collective-permute-start(f32[64,256]{1,0:T(8,128)S(1)} %get-tuple-element.18), channel_id=1, source_target_pairs={{0,3},{1,2},{2,1},{3,0},{4,7},{5,6},{6,5},{7,4},{8,11},{9,10},{10,... | collective-permute-start | bytes 196616 | tf_op jit(solution)/shard_map/ppermute | solution.py:438
